TPU v7x, 32 devices: a whole 2x2x4 slice. The times are simulated.
32 devices in a mesh: seq: 8 (over z, y), tp: 4 (over x, core).
Axes of the slice: x: 2, y: 2, z: 4, core: 2. Of those that a mesh axis runs over, the one named last changes fastest.
Arguments:
- stream_in: bfloat16 [2, 1536, 2048], P(None, 'seq'), may hold values from -6 to 6
- cache_keys: bfloat16 [2, 1536, 2048], P(None, 'seq', 'tp'), may hold values from -6 to 6
- cache_values: bfloat16 [2, 1536, 2048], P(None, 'seq', 'tp'), may hold values from -6 to 6
- memory: bfloat16 [2, 1536, 4096], P(None, 'seq', 'tp'), may hold values from -6 to 6
- cotangent: bfloat16 [2, 1536, 2048], P(None, 'seq'), may hold values from -6 to 6
- query_proj: bfloat16 [2048, 2048], P('seq', 'tp'), may hold values from -0.125 to 0.125
- output_proj: bfloat16 [2048, 2048], P('seq', 'tp'), may hold values from -3 to 3
- gate_first: bfloat16 [2048, 8192], P('seq', 'tp'), may hold values from -0.125 to 0.125
- up_first: bfloat16 [2048, 8192], P('seq', 'tp'), may hold values from -0.125 to 0.125
- down_first: bfloat16 [2048, 8192], P('seq', 'tp'), may hold values from -0.0625 to 0.0625
- memory_in: bfloat16 [2048, 4096], P('seq', 'tp'), may hold values from -0.125 to 0.125
- memory_out: bfloat16 [2048, 4096], P('seq', 'tp'), may hold values from -0.09375 to 0.09375
- gate_second: bfloat16 [2048, 8192], P('seq', 'tp'), may hold values from -0.125 to 0.125
- up_second: bfloat16 [2048, 8192], P('seq', 'tp'), may hold values from -0.125 to 0.125
- down_second: bfloat16 [2048, 8192], P('seq', 'tp'), may hold values from -0.0625 to 0.0625
- norm_gains: float32 [4, 2048], replicated, may hold values from 0.5 to 1.5
- group_order: int32 [16], replicated, may hold values from 0 to 15, each once
- seq_lengths: int32 [2], replicated, may hold values from 384 to 1536, as said below
Outputs:
- stream_out: bfloat16 [2, 1536, 2048], P(None, 'seq')
- stream_grad: float32 [2, 1536, 2048], P(None, 'seq')
- keys_grad: float32 [2, 1536, 2048], P(None, 'seq', 'tp')
- values_grad: float32 [2, 1536, 2048], P(None, 'seq', 'tp')
- memory_grad: float32 [2, 1536, 4096], P(None, 'seq', 'tp')
- query_grad: float32 [2048, 2048], P('seq', 'tp')
- output_grad: float32 [2048, 2048], P('seq', 'tp')
- gate_first_grad: float32 [2048, 8192], P('seq', 'tp')
- up_first_grad: float32 [2048, 8192], P('seq', 'tp')
- down_first_grad: float32 [2048, 8192], P('seq', 'tp')
- memory_in_grad: float32 [2048, 4096], P('seq', 'tp')
- memory_out_grad: float32 [2048, 4096], P('seq', 'tp')
- gate_second_grad: float32 [2048, 8192], P('seq', 'tp')
- up_second_grad: float32 [2048, 8192], P('seq', 'tp')
- down_second_grad: float32 [2048, 8192], P('seq', 'tp')
- gains_grad: float32 [4, 2048], P(None, 'seq')
Inputs may be any that keep to these rules, and one draw needn't show every extreme that they name: `group_order`: each of the 16 group numbers appears once. A micro-batch's sequence fills its first seq_lengths token positions; later positions are padding whose keys no query sees. Exactly one micro-batch is full.
All inputs are finite; a program needn't handle non-finite values.
Results may differ from a plain program's by a relative error of at most 0.028.
Values may be sent and summed in bfloat16 or wider, within the bound.
No kernel may reach another device: no remote copies, remote signals or barrier semaphores. Data moves between devices by JAX's collectives and lax.ppermute only.
A program may use at most 256 MiB of HBM per device.

v0:
```python
import jax
import jax.numpy as jnp
from jax import lax
from jax.sharding import PartitionSpec as P

HD = 128


epsilon = 1e-05
masked_fill = -1e30


def from_behind(value, axis, steps):
    count = lax.axis_size(axis)
    pairs = [(source, (source + steps) % count) for source in range(count)]
    return lax.ppermute(value, axis, pairs)


def rms_apply(values_in, gain_row):
    return (
        values_in
        * lax.rsqrt(jnp.mean(values_in * values_in, axis=-1, keepdims=True) + epsilon)
        * gain_row
    )


def silu_slope(values_in):
    sigma = jax.nn.sigmoid(values_in)
    return sigma * (1.0 + values_in * (1.0 - sigma))


def project(operand, weight):
    return jnp.einsum("mtd,dk->mtk", operand, weight, preferred_element_type=jnp.float32)


def project_back(operand, weight):
    return jnp.einsum("mtk,dk->mtd", operand, weight, preferred_element_type=jnp.float32)


def tensor_total(partial_sum):
    return lax.psum(partial_sum.astype(jnp.bfloat16), "tp").astype(jnp.float32)


def gather_pair(first_mat, second_mat):
    return (
        lax.all_gather(first_mat, "seq", axis=0, tiled=True),
        lax.all_gather(second_mat, "seq", axis=0, tiled=True),
    )


def gather_triple(first_mat, second_mat, third_mat):
    return (
        lax.all_gather(first_mat, "seq", axis=0, tiled=True),
        lax.all_gather(second_mat, "seq", axis=0, tiled=True),
        lax.all_gather(third_mat, "seq", axis=0, tiled=True),
    )


def reduce_rows(row_source, col_source):
    return lax.psum_scatter(
        jnp.einsum(
            "mtd,mtk->dk", row_source, col_source, preferred_element_type=jnp.float32
        ).astype(jnp.bfloat16),
        "seq",
        scatter_dimension=0,
        tiled=True,
    ).astype(jnp.float32)


def row_positions(order_table, first_row, row_count, group_len):
    row_ids = first_row + jnp.arange(row_count, dtype=jnp.int32)
    slot_ids = jnp.arange(order_table.shape[0], dtype=jnp.int32)
    group_ids = jnp.sum(
        jnp.where((row_ids // group_len)[:, None] == slot_ids[None, :], order_table[None, :], 0),
        axis=1,
    )
    return group_ids * group_len + row_ids % group_len


def visible_mask(query_pos, key_pos, lengths):
    return (key_pos[None, None, None, :] <= query_pos[None, None, :, None]) & (
        key_pos[None, None, None, :] < lengths[:, None, None, None]
    )


def swiglu_forward(normed_low, gate_full, up_full, down_full):
    gate_pre = project(normed_low, gate_full)
    up_pre = project(normed_low, up_full)
    hidden = (jax.nn.silu(gate_pre) * up_pre).astype(jnp.bfloat16)
    return (tensor_total(project_back(hidden, down_full)), (gate_pre, up_pre, hidden))


def swiglu_backward(grad_low, normed_low, kept, gate_full, up_full, down_full):
    gate_pre, up_pre, hidden = kept
    grad_hidden = project(grad_low, down_full)
    grad_gate = (grad_hidden * up_pre * silu_slope(gate_pre)).astype(jnp.bfloat16)
    grad_up = (grad_hidden * jax.nn.silu(gate_pre)).astype(jnp.bfloat16)
    grad_normed = tensor_total(project_back(grad_gate, gate_full) + project_back(grad_up, up_full))
    gate_grad = reduce_rows(normed_low, grad_gate)
    up_grad = reduce_rows(normed_low, grad_up)
    down_grad = reduce_rows(grad_low, hidden)
    return (grad_normed, gate_grad, up_grad, down_grad)


def attend_forward(
    query_heads, cache_keys, cache_values, query_pos, lengths, order_table, group_len, scaling
):
    mbatch, row_count, head_count, head_dim = query_heads.shape
    row_best = jnp.full((mbatch, head_count, row_count), masked_fill, jnp.float32)
    key_part = lax.all_gather(cache_keys, "seq", axis=1, tiled=True)
    value_part = lax.all_gather(cache_values, "seq", axis=1, tiled=True)
    rows_in = key_part.shape[1]
    key_heads = key_part.reshape(mbatch, rows_in, head_count, head_dim)
    value_heads = value_part.reshape(mbatch, rows_in, head_count, head_dim)
    allowed = visible_mask(
        query_pos, row_positions(order_table, jnp.int32(0), rows_in, group_len), lengths
    )
    scores = (
        jnp.einsum("bqhd,bkhd->bhqk", query_heads, key_heads, preferred_element_type=jnp.float32)
        * scaling
    )
    scores = jnp.where(allowed, scores, masked_fill)
    new_best = jnp.maximum(row_best, jnp.max(scores, axis=3))
    weights = jnp.where(allowed, jnp.exp(scores - new_best[..., None]), 0.0)
    row_total = jnp.sum(weights, axis=3)
    weighted = jnp.einsum(
        "bhqk,bkhd->bqhd",
        weights.astype(jnp.bfloat16),
        value_heads,
        preferred_element_type=jnp.float32,
    )
    row_best, row_total, weighted = (new_best, row_total, weighted)
    attended = weighted / row_total.transpose(0, 2, 1)[..., None]
    return (attended, row_best + jnp.log(row_total))


def score_pieces(
    query_heads, grad_heads, lse_rows, delta_rows, key_heads, value_heads, allowed, scaling
):
    scores = (
        jnp.einsum("bqhd,bkhd->bhqk", query_heads, key_heads, preferred_element_type=jnp.float32)
        * scaling
    )
    probs = jnp.exp(jnp.where(allowed, scores, masked_fill) - lse_rows[..., None])
    grad_probs = jnp.einsum(
        "bqhd,bkhd->bhqk", grad_heads, value_heads, preferred_element_type=jnp.float32
    )
    grad_scores = (probs * (grad_probs - delta_rows[..., None])).astype(jnp.bfloat16)
    return (probs.astype(jnp.bfloat16), grad_scores)


def cycle_carry(
    query_heads,
    grad_heads,
    lse_rows,
    delta_rows,
    cache_keys,
    cache_values,
    query_pos,
    lengths,
    order_table,
    group_len,
    scaling,
):
    mbatch, row_count, head_count, head_dim = query_heads.shape
    flat_cols = head_count * head_dim
    cycle_size = lax.axis_size("seq")
    here = lax.axis_index("seq")

    def turn_step(turn, state):
        query_acc, cache_pair, grad_pair = state
        owner = (here - turn + cycle_size) % cycle_size
        offset = owner * row_count
        key_heads = cache_pair[0].reshape(mbatch, row_count, head_count, head_dim)
        value_heads = cache_pair[1].reshape(mbatch, row_count, head_count, head_dim)
        allowed = visible_mask(
            query_pos, row_positions(order_table, offset, row_count, group_len), lengths
        )
        probs_low, grad_scores = score_pieces(
            query_heads, grad_heads, lse_rows, delta_rows, key_heads, value_heads, allowed, scaling
        )
        query_acc = query_acc + jnp.einsum(
            "bhqk,bkhd->bqhd", grad_scores, key_heads, preferred_element_type=jnp.float32
        )
        keys_piece = (
            jnp.einsum(
                "bhqk,bqhd->bkhd", grad_scores, query_heads, preferred_element_type=jnp.float32
            ).reshape(mbatch, row_count, flat_cols)
            * scaling
        )
        values_piece = jnp.einsum(
            "bhqk,bqhd->bkhd", probs_low, grad_heads, preferred_element_type=jnp.float32
        ).reshape(mbatch, row_count, flat_cols)
        grad_pair = grad_pair + jnp.stack([keys_piece, values_piece])
        cache_pair = from_behind(cache_pair, "seq", 1)
        grad_pair = from_behind(grad_pair.astype(jnp.bfloat16), "seq", 1).astype(grad_pair.dtype)
        return (query_acc, cache_pair, grad_pair)

    initial = (
        jnp.zeros(query_heads.shape, jnp.float32),
        jnp.stack([cache_keys, cache_values]),
        jnp.zeros((2, mbatch, row_count, flat_cols), jnp.float32),
    )
    query_acc, cache_pair, grad_pair = lax.fori_loop(0, cycle_size, turn_step, initial)
    return (query_acc, grad_pair[0], grad_pair[1])


def shards(
    stream_in,
    cache_keys,
    cache_values,
    memory,
    cotangent,
    query_proj,
    output_proj,
    gate_first,
    up_first,
    down_first,
    memory_in,
    memory_out,
    gate_second,
    up_second,
    down_second,
    norm_gains,
    group_order,
    seq_lengths,
):
    mbatch = stream_in.shape[0]
    tok_rows = stream_in.shape[1]
    head_count = cache_keys.shape[2] // HD
    flat_cols = head_count * HD
    group_len = tok_rows // 2
    scaling = HD ** (-0.5)
    query_pos = row_positions(group_order, lax.axis_index("seq") * tok_rows, tok_rows, group_len)
    stream = stream_in.astype(jnp.float32)
    normed_one, pull_one = jax.vjp(rms_apply, stream, norm_gains[0])
    normed_one = normed_one.astype(jnp.bfloat16)
    query_full, outproj_full = gather_pair(query_proj, output_proj)
    queries = project(normed_one, query_full).astype(jnp.bfloat16)
    query_heads = queries.reshape(mbatch, tok_rows, head_count, HD)
    attended, lse_rows = attend_forward(
        query_heads,
        cache_keys,
        cache_values,
        query_pos,
        seq_lengths,
        group_order,
        group_len,
        scaling,
    )
    attn_low = attended.reshape(mbatch, tok_rows, flat_cols).astype(jnp.bfloat16)
    stream = stream + tensor_total(project_back(attn_low, outproj_full))
    normed_two, pull_two = jax.vjp(rms_apply, stream, norm_gains[1])
    normed_two = normed_two.astype(jnp.bfloat16)
    gate_one_full, up_one_full, down_one_full = gather_triple(gate_first, up_first, down_first)
    branch, kept_one = swiglu_forward(normed_two, gate_one_full, up_one_full, down_one_full)
    stream = stream + branch
    normed_three, pull_three = jax.vjp(rms_apply, stream, norm_gains[2])
    normed_three = normed_three.astype(jnp.bfloat16)
    mem_in_full, mem_out_full = gather_pair(memory_in, memory_out)
    drive = project(normed_three, mem_in_full)
    memory_wide = memory.astype(jnp.float32)
    gated = (memory_wide * jax.nn.silu(drive)).astype(jnp.bfloat16)
    stream = stream + tensor_total(project_back(gated, mem_out_full))
    normed_four, pull_four = jax.vjp(rms_apply, stream, norm_gains[3])
    normed_four = normed_four.astype(jnp.bfloat16)
    gate_two_full, up_two_full, down_two_full = gather_triple(gate_second, up_second, down_second)
    branch, kept_two = swiglu_forward(normed_four, gate_two_full, up_two_full, down_two_full)
    stream = stream + branch
    stream_out = stream.astype(jnp.bfloat16)
    grad_stream = cotangent.astype(jnp.float32)
    grad_normed, gate_second_grad, up_second_grad, down_second_grad = swiglu_backward(
        cotangent, normed_four, kept_two, gate_two_full, up_two_full, down_two_full
    )
    grad_part, gain_four = pull_four(grad_normed)
    grad_stream = grad_stream + grad_part
    grad_low = grad_stream.astype(jnp.bfloat16)
    grad_gated = project(grad_low, mem_out_full)
    memory_grad = grad_gated * jax.nn.silu(drive)
    grad_drive = (grad_gated * memory_wide * silu_slope(drive)).astype(jnp.bfloat16)
    grad_normed = tensor_total(project_back(grad_drive, mem_in_full))
    memory_in_grad = reduce_rows(normed_three, grad_drive)
    memory_out_grad = reduce_rows(grad_low, gated)
    grad_part, gain_three = pull_three(grad_normed)
    grad_stream = grad_stream + grad_part
    grad_low = grad_stream.astype(jnp.bfloat16)
    grad_normed, gate_first_grad, up_first_grad, down_first_grad = swiglu_backward(
        grad_low, normed_two, kept_one, gate_one_full, up_one_full, down_one_full
    )
    grad_part, gain_two = pull_two(grad_normed)
    grad_stream = grad_stream + grad_part
    grad_low = grad_stream.astype(jnp.bfloat16)
    grad_attn = project(grad_low, outproj_full).astype(jnp.bfloat16)
    output_grad = reduce_rows(grad_low, attn_low)
    grad_heads = grad_attn.reshape(mbatch, tok_rows, head_count, HD)
    delta_rows = jnp.einsum("bqhd,bqhd->bhq", grad_heads.astype(jnp.float32), attended)
    grad_queries, keys_grad, values_grad = cycle_carry(
        query_heads,
        grad_heads,
        lse_rows,
        delta_rows,
        cache_keys,
        cache_values,
        query_pos,
        seq_lengths,
        group_order,
        group_len,
        scaling,
    )
    grad_query_low = (
        (grad_queries * scaling).astype(jnp.bfloat16).reshape(mbatch, tok_rows, flat_cols)
    )
    grad_normed = tensor_total(project_back(grad_query_low, query_full))
    query_grad = reduce_rows(normed_one, grad_query_low)
    grad_part, gain_one = pull_one(grad_normed)
    grad_stream = grad_stream + grad_part
    gains_grad = lax.psum_scatter(
        jnp.stack([gain_one, gain_two, gain_three, gain_four]).astype(jnp.bfloat16),
        "seq",
        scatter_dimension=1,
        tiled=True,
    ).astype(jnp.float32)
    return (
        stream_out,
        grad_stream,
        keys_grad,
        values_grad,
        memory_grad,
        query_grad,
        output_grad,
        gate_first_grad,
        up_first_grad,
        down_first_grad,
        memory_in_grad,
        memory_out_grad,
        gate_second_grad,
        up_second_grad,
        down_second_grad,
        gains_grad,
    )


def solution(mesh):
    placed = (
        P(None, "seq", None),
        P(None, "seq", "tp"),
        P(None, "seq", "tp"),
        P(None, "seq", "tp"),
        P(None, "seq", None),
        P("seq", "tp"),
        P("seq", "tp"),
        P("seq", "tp"),
        P("seq", "tp"),
        P("seq", "tp"),
        P("seq", "tp"),
        P("seq", "tp"),
        P("seq", "tp"),
        P("seq", "tp"),
        P("seq", "tp"),
        P(),
        P(),
        P(),
    )
    return jax.shard_map(
        shards,
        mesh=mesh,
        in_specs=placed,
        out_specs=(
            P(None, "seq", None),
            P(None, "seq", None),
            P(None, "seq", "tp"),
            P(None, "seq", "tp"),
            P(None, "seq", "tp"),
            P("seq", "tp"),
            P("seq", "tp"),
            P("seq", "tp"),
            P("seq", "tp"),
            P("seq", "tp"),
            P("seq", "tp"),
            P("seq", "tp"),
            P("seq", "tp"),
            P("seq", "tp"),
            P("seq", "tp"),
            P(None, "seq"),
        ),
        check_vma=False,
    )
```

profile of v0, /device:TPU:0, one launch (start us, length us, event | category | flops | bytes accessed | tf_op | source)
XLA Modules:
  0.0 3281.3 jit_solution(14098418716838896394)
XLA Ops:
  18.1 44.2 %all-gather.13.cloned.1.call-done = bf16[2048,512]{1,0:T(8,128)(2,1)} async-done(((bf16[256,512]{1,0:T(8,128)(2,1)}), bf16[2048,512]{1,0:T(8,128)(2,1)}) %all-gather.13.cloned.1.call-update) | async-done | bytes 2097168 | tf_op jit(solution)/shard_map/all_gather | solution.py:46
  65.0 59.1 %all-gather.17.cloned.1.call-done = bf16[2,1536,512]{2,0,1:T(2,128)(2,1)} async-done(((bf16[2,192,512]{2,0,1:T(2,128)(2,1)}), bf16[2,1536,512]{2,0,1:T(2,128)(2,1)}) %all-gather.17.cloned.1.call-update) | async-done | bytes 3145744 | tf_op jit(solution)/shard_map/all_gather | solution.py:111
  132.7 53.2 %all-gather.15.cloned.1.call-done = bf16[2,1536,512]{2,0,1:T(2,128)(2,1)} async-done(((bf16[2,192,512]{2,0,1:T(2,128)(2,1)}), bf16[2,1536,512]{2,0,1:T(2,128)(2,1)}) %all-gather.15.cloned.1.call-update) | async-done | bytes 3145744 | tf_op jit(solution)/shard_map/all_gather | solution.py:110
  204.7 31.2 all-gather.19.cloned.1.call-done
  241.9 39.2 %all-reduce.9.cloned.1.call-done = bf16[2,192,2048]{2,1,0:T(8,128)(2,1)} async-done(((bf16[2,192,2048]{2,1,0:T(8,128)(2,1)}), bf16[2,192,2048]{2,1,0:T(8,128)(2,1)}) %all-reduce.9.cloned.1.call-update) | async-done | bytes 1572880 | tf_op jit(solution)/shard_map/psum | solution.py:41
  286.2 121.9 %all-gather.21.cloned.1.call-done = bf16[2048,2048]{1,0:T(8,128)(2,1)} async-done(((bf16[256,2048]{1,0:T(8,128)(2,1)}), bf16[2048,2048]{1,0:T(8,128)(2,1)}) %all-gather.21.cloned.1.call-update) | async-done | bytes 8388624 | tf_op jit(solution)/shard_map/all_gather | solution.py:53
  417.1 116.3 %all-gather.23.cloned.1.call-done = bf16[2048,2048]{1,0:T(8,128)(2,1)} async-done(((bf16[256,2048]{1,0:T(8,128)(2,1)}), bf16[2048,2048]{1,0:T(8,128)(2,1)}) %all-gather.23.cloned.1.call-update) | async-done | bytes 8388624 | tf_op jit(solution)/shard_map/all_gather | solution.py:54
  533.4 10.4 multiply_convert_fusion.8
  543.8 114.8 %all-gather.25.cloned.1.call-done = bf16[2048,2048]{1,0:T(8,128)(2,1)} async-done(((bf16[256,2048]{1,0:T(8,128)(2,1)}), bf16[2048,2048]{1,0:T(8,128)(2,1)}) %all-gather.25.cloned.1.call-update) | async-done | bytes 8388624 | tf_op jit(solution)/shard_map/all_gather | solution.py:55
  669.1 39.2 %all-reduce.11.cloned.1.call-done = bf16[2,192,2048]{2,1,0:T(8,128)(2,1)} async-done(((bf16[2,192,2048]{2,1,0:T(8,128)(2,1)}), bf16[2,192,2048]{2,1,0:T(8,128)(2,1)}) %all-reduce.11.cloned.1.call-update) | async-done | bytes 1572880 | tf_op jit(solution)/shard_map/psum | solution.py:41
  713.2 70.6 %all-gather.27.cloned.1.call-done = bf16[2048,1024]{1,0:T(8,128)(2,1)} async-done(((bf16[256,1024]{1,0:T(8,128)(2,1)}), bf16[2048,1024]{1,0:T(8,128)(2,1)}) %all-gather.27.cloned.1.call-update) | async-done | bytes 4194320 | tf_op jit(solution)/shard_map/all_gather | solution.py:46
  789.9 67.7 %all-gather.29.cloned.1.call-done = bf16[2048,1024]{1,0:T(8,128)(2,1)} async-done(((bf16[256,1024]{1,0:T(8,128)(2,1)}), bf16[2048,1024]{1,0:T(8,128)(2,1)}) %all-gather.29.cloned.1.call-update) | async-done | bytes 4194320 | tf_op jit(solution)/shard_map/all_gather | solution.py:47
  865.0 117.9 %all-gather.35.cloned.1.call-done = bf16[2048,2048]{1,0:T(8,128)(2,1)} async-done(((bf16[256,2048]{1,0:T(8,128)(2,1)}), bf16[2048,2048]{1,0:T(8,128)(2,1)}) %all-gather.35.cloned.1.call-update) | async-done | bytes 8388624 | tf_op jit(solution)/shard_map/all_gather | solution.py:55
  982.8 9.0 fusion.10
  991.8 35.0 %all-reduce.13.cloned.1.call-done = bf16[2,192,2048]{2,1,0:T(8,128)(2,1)} async-done(((bf16[2,192,2048]{2,1,0:T(8,128)(2,1)}), bf16[2,192,2048]{2,1,0:T(8,128)(2,1)}) %all-reduce.13.cloned.1.call-update) | async-done | bytes 1572880 | tf_op jit(solution)/shard_map/psum | solution.py:41
  1032.8 121.0 %all-gather.33.cloned.1.call-done = bf16[2048,2048]{1,0:T(8,128)(2,1)} async-done(((bf16[256,2048]{1,0:T(8,128)(2,1)}), bf16[2048,2048]{1,0:T(8,128)(2,1)}) %all-gather.33.cloned.1.call-update) | async-done | bytes 8388624 | tf_op jit(solution)/shard_map/all_gather | solution.py:54
  1162.8 116.2 %all-gather.31.cloned.1.call-done = bf16[2048,2048]{1,0:T(8,128)(2,1)} async-done(((bf16[256,2048]{1,0:T(8,128)(2,1)}), bf16[2048,2048]{1,0:T(8,128)(2,1)}) %all-gather.31.cloned.1.call-update) | async-done | bytes 8388624 | tf_op jit(solution)/shard_map/all_gather | solution.py:53
  1279.0 12.1 multiply_convert_fusion.4
  1301.6 41.1 %all-reduce.15.cloned.1.call-done = bf16[2,192,2048]{2,1,0:T(8,128)(2,1)} async-done(((bf16[2,192,2048]{2,1,0:T(8,128)(2,1)}), bf16[2,192,2048]{2,1,0:T(8,128)(2,1)}) %all-reduce.15.cloned.1.call-update) | async-done | bytes 1572880 | tf_op jit(solution)/shard_map/psum | solution.py:41
  1362.1 38.6 %all-reduce.17.cloned.1.call-done = bf16[2,192,2048]{2,1,0:T(8,128)(2,1)} async-done(((bf16[2,192,2048]{2,1,0:T(8,128)(2,1)}), bf16[2,192,2048]{2,1,0:T(8,128)(2,1)}) %all-reduce.17.cloned.1.call-update) | async-done | bytes 1572880 | tf_op jit(solution)/shard_map/psum | solution.py:41
  1407.8 10.3 multiply_convert_fusion.2
  1438.3 34.5 %all-reduce.19.cloned.1.call-done = bf16[2,192,2048]{2,1,0:T(8,128)(2,1)} async-done(((bf16[2,192,2048]{2,1,0:T(8,128)(2,1)}), bf16[2,192,2048]{2,1,0:T(8,128)(2,1)}) %all-reduce.19.cloned.1.call-update) | async-done | bytes 1572880 | tf_op jit(solution)/shard_map/psum | solution.py:41
  1484.0 411.6 %while.21 = (s32[]{:T(128)}, f32[2,192,4,128]{3,1,2,0:T(8,128)}, bf16[2,2,192,512]{3,2,1,0:T(8,128)(2,1)}, f32[2,2,192,512]{3,2,1,0:T(8,128)}, s32[]{:T(128)}, /...) while((s32[]{:T(128)}, f32[2,192,4,128]{3,1,2,0:T(8,128)}, ...), condition=%wide.region_20.21_spmd.clone, body=%wide.region_18.20_spmd.clone.sunk | while | flops 382231104 | bytes 41332012 | solution.py:204
  1503.4 19.2 collective-permute-done.1
  1523.9 14.3 collective-permute-done
  1557.4 19.8 collective-permute-done.1
  1578.6 13.4 collective-permute-done
  1610.1 21.0 collective-permute-done.1
  1632.5 12.4 collective-permute-done
  1663.0 21.0 collective-permute-done.1
  1685.3 11.5 collective-permute-done
  1715.0 21.0 collective-permute-done.1
  1737.3 10.6 collective-permute-done
  1766.0 21.0 collective-permute-done.1
  1788.4 9.7 collective-permute-done
  1816.2 21.0 collective-permute-done.1
  1865.4 21.0 collective-permute-done.1
  1899.8 68.4 %all-reduce.21.cloned.1.call-done = (bf16[2,192,2048]{2,1,0:T(8,128)(2,1)}, bf16[2,192,2048]{2,1,0:T(8,128)(2,1)}) async-done(((bf16[2,192,2048]{2,1,0:T(8,128)(2,1)}, bf16[2,192,2048]{2,1,0:T(8,128)(2,1)}), (bf16[2,192,2048]{2,1,0:T(8,128)(2,1)}, bf16[2,192,2048]{2,1,0:T(8,128)(2,1)})) %all-reduce.21.cloned.1.call-update) | async-done | bytes 3145744 | tf_op jit(solution)/shard_map/psum | solution.py:41
  2060.0 45.7 %reduce-scatter.14.cloned.1.call-done = bf16[256,512]{1,0:T(8,128)(2,1)} async-done(((bf16[2048,512]{1,0:T(8,128)(2,1)}), bf16[256,512]{1,0:T(8,128)(2,1)}) %reduce-scatter.14.cloned.1.call-update) | async-done | bytes 262160 | tf_op jit(solution)/shard_map/reduce_scatter | solution.py:60
  2107.5 69.7 %reduce-scatter.16.cloned.1.call-done = bf16[256,512]{1,0:T(8,128)(2,1)} async-done(((bf16[2048,512]{1,0:T(8,128)(2,1)}), bf16[256,512]{1,0:T(8,128)(2,1)}) %reduce-scatter.16.cloned.1.call-update) | async-done | bytes 262160 | tf_op jit(solution)/shard_map/reduce_scatter | solution.py:60
  2179.0 89.2 %reduce-scatter.24.cloned.1.call-done = bf16[256,1024]{1,0:T(8,128)(2,1)} async-done(((bf16[2048,1024]{1,0:T(8,128)(2,1)}), bf16[256,1024]{1,0:T(8,128)(2,1)}) %reduce-scatter.24.cloned.1.call-update) | async-done | bytes 524304 | tf_op jit(solution)/shard_map/reduce_scatter | solution.py:60
  2270.3 89.0 %reduce-scatter.26.cloned.1.call-done = bf16[256,1024]{1,0:T(8,128)(2,1)} async-done(((bf16[2048,1024]{1,0:T(8,128)(2,1)}), bf16[256,1024]{1,0:T(8,128)(2,1)}) %reduce-scatter.26.cloned.1.call-update) | async-done | bytes 524304 | tf_op jit(solution)/shard_map/reduce_scatter | solution.py:60
  2361.5 150.7 %reduce-scatter.28.cloned.1.call-done = bf16[256,2048]{1,0:T(8,128)(2,1)} async-done(((bf16[2048,2048]{1,0:T(8,128)(2,1)}), bf16[256,2048]{1,0:T(8,128)(2,1)}) %reduce-scatter.28.cloned.1.call-update) | async-done | bytes 1048592 | tf_op jit(solution)/shard_map/reduce_scatter | solution.py:60
  2515.0 148.7 %reduce-scatter.30.cloned.1.call-done = bf16[256,2048]{1,0:T(8,128)(2,1)} async-done(((bf16[2048,2048]{1,0:T(8,128)(2,1)}), bf16[256,2048]{1,0:T(8,128)(2,1)}) %reduce-scatter.30.cloned.1.call-update) | async-done | bytes 1048592 | tf_op jit(solution)/shard_map/reduce_scatter | solution.py:60
  2666.5 149.6 %reduce-scatter.32.cloned.1.call-done = bf16[256,2048]{0,1:T(8,128)(2,1)} async-done(((bf16[2048,2048]{0,1:T(8,128)(2,1)}), bf16[256,2048]{0,1:T(8,128)(2,1)}) %reduce-scatter.32.cloned.1.call-update) | async-done | bytes 1048592 | tf_op jit(solution)/shard_map/reduce_scatter | solution.py:60
  2818.7 149.1 %reduce-scatter.18.cloned.1.call-done = bf16[256,2048]{1,0:T(8,128)(2,1)} async-done(((bf16[2048,2048]{1,0:T(8,128)(2,1)}), bf16[256,2048]{1,0:T(8,128)(2,1)}) %reduce-scatter.18.cloned.1.call-update) | async-done | bytes 1048592 | tf_op jit(solution)/shard_map/reduce_scatter | solution.py:60
  2970.6 149.4 %reduce-scatter.20.cloned.1.call-done = bf16[256,2048]{1,0:T(8,128)(2,1)} async-done(((bf16[2048,2048]{1,0:T(8,128)(2,1)}), bf16[256,2048]{1,0:T(8,128)(2,1)}) %reduce-scatter.20.cloned.1.call-update) | async-done | bytes 1048592 | tf_op jit(solution)/shard_map/reduce_scatter | solution.py:60
  3122.7 148.7 %reduce-scatter.22.cloned.1.call-done = bf16[256,2048]{1,0:T(8,128)(2,1)} async-done(((bf16[2048,2048]{1,0:T(8,128)(2,1)}), bf16[256,2048]{1,0:T(8,128)(2,1)}) %reduce-scatter.22.cloned.1.call-update) | async-done | bytes 1048592 | tf_op jit(solution)/shard_map/reduce_scatter | solution.py:60
  (525 shorter events, 466.5 us)
Async XLA Ops:
  7.2 55.1 %all-gather.13.cloned.1.call-start = ((), (), s32[]{:S(2)}) async-start(), calls=%async_computation.11 | async-start | bytes 2359296 | tf_op jit(solution)/shard_map/all_gather | solution.py:46
  7.9 116.1 %all-gather.17.cloned.1.call-start = ((), (), s32[]{:S(2)}) async-start(), calls=%async_computation.13 | async-start | bytes 3538944 | tf_op jit(solution)/shard_map/all_gather | solution.py:111
  10.2 175.8 %all-gather.15.cloned.1.call-start = ((), (), s32[]{:S(2)}) async-start(), calls=%async_computation.12 | async-start | bytes 3538944 | tf_op jit(solution)/shard_map/all_gather | solution.py:110
  12.4 223.5 %all-gather.19.cloned.1.call-start = ((), (), s32[]{:S(2)}) async-start(), calls=%async_computation.14 | async-start | bytes 2359296 | tf_op jit(solution)/shard_map/all_gather | solution.py:47
  13.0 268.2 %all-reduce.9.cloned.1.call-start = ((), (), s32[]{:S(2)}) async-start(), calls=%async_computation.15 | async-start | bytes 3145728 | tf_op jit(solution)/shard_map/psum | solution.py:41
  239.6 168.5 %all-gather.21.cloned.1.call-start = ((), (), s32[]{:S(2)}) async-start(), calls=%async_computation.16 | async-start | bytes 9437184 | tf_op jit(solution)/shard_map/all_gather | solution.py:53
  240.2 293.2 %all-gather.23.cloned.1.call-start = ((), (), s32[]{:S(2)}) async-start(), calls=%async_computation.17 | async-start | bytes 9437184 | tf_op jit(solution)/shard_map/all_gather | solution.py:54
  241.0 417.7 %all-gather.25.cloned.1.call-start = ((), (), s32[]{:S(2)}) async-start(), calls=%async_computation.18 | async-start | bytes 9437184 | tf_op jit(solution)/shard_map/all_gather | solution.py:55
  241.7 466.6 %all-reduce.11.cloned.1.call-start = ((), (), s32[]{:S(2)}) async-start(), calls=%async_computation.19 | async-start | bytes 3145728 | tf_op jit(solution)/shard_map/psum | solution.py:41
  667.1 116.7 %all-gather.27.cloned.1.call-start = ((), (), s32[]{:S(2)}) async-start(), calls=%async_computation.20 | async-start | bytes 4718592 | tf_op jit(solution)/shard_map/all_gather | solution.py:46
  667.7 189.9 %all-gather.29.cloned.1.call-start = ((), (), s32[]{:S(2)}) async-start(), calls=%async_computation.21 | async-start | bytes 4718592 | tf_op jit(solution)/shard_map/all_gather | solution.py:47
  668.5 314.4 %all-gather.35.cloned.1.call-start = ((), (), s32[]{:S(2)}) async-start(), calls=%async_computation.25 | async-start | bytes 9437184 | tf_op jit(solution)/shard_map/all_gather | solution.py:55
  669.0 357.8 %all-reduce.13.cloned.1.call-start = ((), (), s32[]{:S(2)}) async-start(), calls=%async_computation.22 | async-start | bytes 3145728 | tf_op jit(solution)/shard_map/psum | solution.py:41
  863.6 290.3 %all-gather.33.cloned.1.call-start = ((), (), s32[]{:S(2)}) async-start(), calls=%async_computation.24 | async-start | bytes 9437184 | tf_op jit(solution)/shard_map/all_gather | solution.py:54
  864.1 414.9 %all-gather.31.cloned.1.call-start = ((), (), s32[]{:S(2)}) async-start(), calls=%async_computation.23 | async-start | bytes 9437184 | tf_op jit(solution)/shard_map/all_gather | solution.py:53
  864.7 478.0 %all-reduce.15.cloned.1.call-start = ((), (), s32[]{:S(2)}) async-start(), calls=%async_computation.26 | async-start | bytes 3145728 | tf_op jit(solution)/shard_map/psum | solution.py:41
  1301.5 99.1 %all-reduce.17.cloned.1.call-start = ((), (), s32[]{:S(2)}) async-start(), calls=%async_computation.27 | async-start | bytes 3145728 | tf_op jit(solution)/shard_map/psum | solution.py:41
  1357.6 115.3 %all-reduce.19.cloned.1.call-start = ((), (), s32[]{:S(2)}) async-start(), calls=%async_computation.28 | async-start | bytes 3145728 | tf_op jit(solution)/shard_map/psum | solution.py:41
  1429.8 538.5 %all-reduce.21.cloned.1.call-start = ((), (), s32[]{:S(2)}) async-start(), calls=%async_computation.40 | async-start | bytes 6291456 | tf_op jit(solution)/shard_map/psum | solution.py:41
  1499.2 23.4 collective-permute-start.1
  1500.7 37.5 %collective-permute-start = (bf16[2,2,192,512]{3,2,1,0:T(8,128)(2,1)S(1)}, bf16[2,2,192,512]{3,2,1,0:T(8,128)(2,1)}, u32[]{:S(2)}, u32[]{:S(2)}) collective-permute-start(bf16[2,2,192,512]{3,2,1,0:T(8,128)(2,1)S(1)} %copy.162), channel_id=1, source_target_pairs={{0,4},{4,8},{8,12},{12,16},{16,20},{20,24},{24,28},{28,0},{1,5},{5... | collective-permute-start | bytes 2359304 | tf_op jit(solution)/shard_map/while/body/eval_jaxpr/ppermute | solution.py:16
  1553.9 23.4 collective-permute-start.1
  1553.9 38.1 %collective-permute-start = (bf16[2,2,192,512]{3,2,1,0:T(8,128)(2,1)S(1)}, bf16[2,2,192,512]{3,2,1,0:T(8,128)(2,1)}, u32[]{:S(2)}, u32[]{:S(2)}) collective-permute-start(bf16[2,2,192,512]{3,2,1,0:T(8,128)(2,1)S(1)} %copy.162), channel_id=1, source_target_pairs={{0,4},{4,8},{8,12},{12,16},{16,20},{20,24},{24,28},{28,0},{1,5},{5... | collective-permute-start | bytes 2359304 | tf_op jit(solution)/shard_map/while/body/eval_jaxpr/ppermute | solution.py:16
  1607.7 23.4 collective-permute-start.1
  1607.7 37.2 %collective-permute-start = (bf16[2,2,192,512]{3,2,1,0:T(8,128)(2,1)S(1)}, bf16[2,2,192,512]{3,2,1,0:T(8,128)(2,1)}, u32[]{:S(2)}, u32[]{:S(2)}) collective-permute-start(bf16[2,2,192,512]{3,2,1,0:T(8,128)(2,1)S(1)} %copy.162), channel_id=1, source_target_pairs={{0,4},{4,8},{8,12},{12,16},{16,20},{20,24},{24,28},{28,0},{1,5},{5... | collective-permute-start | bytes 2359304 | tf_op jit(solution)/shard_map/while/body/eval_jaxpr/ppermute | solution.py:16
  1660.6 23.4 collective-permute-start.1
  1660.6 36.3 %collective-permute-start = (bf16[2,2,192,512]{3,2,1,0:T(8,128)(2,1)S(1)}, bf16[2,2,192,512]{3,2,1,0:T(8,128)(2,1)}, u32[]{:S(2)}, u32[]{:S(2)}) collective-permute-start(bf16[2,2,192,512]{3,2,1,0:T(8,128)(2,1)S(1)} %copy.162), channel_id=1, source_target_pairs={{0,4},{4,8},{8,12},{12,16},{16,20},{20,24},{24,28},{28,0},{1,5},{5... | collective-permute-start | bytes 2359304 | tf_op jit(solution)/shard_map/while/body/eval_jaxpr/ppermute | solution.py:16
  1712.6 23.4 collective-permute-start.1
  1712.6 35.3 %collective-permute-start = (bf16[2,2,192,512]{3,2,1,0:T(8,128)(2,1)S(1)}, bf16[2,2,192,512]{3,2,1,0:T(8,128)(2,1)}, u32[]{:S(2)}, u32[]{:S(2)}) collective-permute-start(bf16[2,2,192,512]{3,2,1,0:T(8,128)(2,1)S(1)} %copy.162), channel_id=1, source_target_pairs={{0,4},{4,8},{8,12},{12,16},{16,20},{20,24},{24,28},{28,0},{1,5},{5... | collective-permute-start | bytes 2359304 | tf_op jit(solution)/shard_map/while/body/eval_jaxpr/ppermute | solution.py:16
  1763.6 23.4 collective-permute-start.1
  1763.6 34.4 %collective-permute-start = (bf16[2,2,192,512]{3,2,1,0:T(8,128)(2,1)S(1)}, bf16[2,2,192,512]{3,2,1,0:T(8,128)(2,1)}, u32[]{:S(2)}, u32[]{:S(2)}) collective-permute-start(bf16[2,2,192,512]{3,2,1,0:T(8,128)(2,1)S(1)} %copy.162), channel_id=1, source_target_pairs={{0,4},{4,8},{8,12},{12,16},{16,20},{20,24},{24,28},{28,0},{1,5},{5... | collective-permute-start | bytes 2359304 | tf_op jit(solution)/shard_map/while/body/eval_jaxpr/ppermute | solution.py:16
  1813.8 23.4 collective-permute-start.1
  1813.8 33.5 %collective-permute-start = (bf16[2,2,192,512]{3,2,1,0:T(8,128)(2,1)S(1)}, bf16[2,2,192,512]{3,2,1,0:T(8,128)(2,1)}, u32[]{:S(2)}, u32[]{:S(2)}) collective-permute-start(bf16[2,2,192,512]{3,2,1,0:T(8,128)(2,1)S(1)} %copy.162), channel_id=1, source_target_pairs={{0,4},{4,8},{8,12},{12,16},{16,20},{20,24},{24,28},{28,0},{1,5},{5... | collective-permute-start | bytes 2359304 | tf_op jit(solution)/shard_map/while/body/eval_jaxpr/ppermute | solution.py:16
  1863.0 23.4 collective-permute-start.1
  1863.0 32.6 collective-permute-start
  1895.6 72.7 %copy-start.1 = (bf16[2,192,2048]{2,1,0:T(8,128)(2,1)S(1)}, bf16[2,192,2048]{2,1,0:T(8,128)(2,1)}, u32[]{:S(2)}) copy-start(bf16[2,192,2048]{2,1,0:T(8,128)(2,1)} %param.20) | copy-start | bytes 4718596
  1895.6 72.7 %copy-start.31 = (f32[1,2048]{1,0:T(1,128)S(1)}, f32[1,2048]{1,0:T(1,128)}, u32[]{:S(2)}) copy-start(f32[1,2048]{1,0:T(1,128)} %copy-done.30) | copy-start | bytes 24580
  1899.7 158.8 %reduce-scatter.34.cloned.1.call-start = ((), (), s32[]{:S(2)}) async-start(), calls=%async_computation.39 | async-start | bytes 589824
  1972.0 133.7 %reduce-scatter.14.cloned.1.call-start = ((), (), s32[]{:S(2)}) async-start(), calls=%async_computation.29 | async-start | bytes 2359296 | tf_op jit(solution)/shard_map/reduce_scatter | solution.py:60
  1974.9 202.3 %reduce-scatter.16.cloned.1.call-start = ((), (), s32[]{:S(2)}) async-start(), calls=%async_computation.30 | async-start | bytes 2359296 | tf_op jit(solution)/shard_map/reduce_scatter | solution.py:60
  1979.5 288.7 %reduce-scatter.24.cloned.1.call-start = ((), (), s32[]{:S(2)}) async-start(), calls=%async_computation.34 | async-start | bytes 4718592 | tf_op jit(solution)/shard_map/reduce_scatter | solution.py:60
  1986.2 373.1 %reduce-scatter.26.cloned.1.call-start = ((), (), s32[]{:S(2)}) async-start(), calls=%async_computation.35 | async-start | bytes 4718592 | tf_op jit(solution)/shard_map/reduce_scatter | solution.py:60
  1994.2 518.0 %reduce-scatter.28.cloned.1.call-start = ((), (), s32[]{:S(2)}) async-start(), calls=%async_computation.36 | async-start | bytes 9437184 | tf_op jit(solution)/shard_map/reduce_scatter | solution.py:60
  2003.8 659.9 %reduce-scatter.30.cloned.1.call-start = ((), (), s32[]{:S(2)}) async-start(), calls=%async_computation.37 | async-start | bytes 9437184 | tf_op jit(solution)/shard_map/reduce_scatter | solution.py:60
  2012.1 804.0 %reduce-scatter.32.cloned.1.call-start = ((), (), s32[]{:S(2)}) async-start(), calls=%async_computation.38 | async-start | bytes 9437184 | tf_op jit(solution)/shard_map/reduce_scatter | solution.py:60
  2021.7 946.0 %reduce-scatter.18.cloned.1.call-start = ((), (), s32[]{:S(2)}) async-start(), calls=%async_computation.31 | async-start | bytes 9437184 | tf_op jit(solution)/shard_map/reduce_scatter | solution.py:60
  2031.3 1088.6 %reduce-scatter.20.cloned.1.call-start = ((), (), s32[]{:S(2)}) async-start(), calls=%async_computation.32 | async-start | bytes 9437184 | tf_op jit(solution)/shard_map/reduce_scatter | solution.py:60
  2039.5 1231.9 %reduce-scatter.22.cloned.1.call-start = ((), (), s32[]{:S(2)}) async-start(), calls=%async_computation.33 | async-start | bytes 9437184 | tf_op jit(solution)/shard_map/reduce_scatter | solution.py:60
  (89 other events, 795.3 us)
Sparse Core Ops, SparseCore 0:
  10.2 52.1 all-gather.12
  65.1 58.9 all-gather.16
  126.8 59.0 all-gather.14
  187.9 47.8 all-gather.18
  239.8 41.3 all-reduce.8
  283.1 124.9 all-gather.20
  410.3 123.0 all-gather.22
  535.5 123.1 all-gather.24
  667.3 41.0 all-reduce.10
  710.3 73.4 all-gather.26
  785.9 71.6 all-gather.28
  859.6 123.1 all-gather.34
  985.8 41.0 all-reduce.12
  1028.8 124.9 all-gather.32
  1155.8 123.1 all-gather.30
  1301.7 41.0 all-reduce.14
  1357.7 42.8 all-reduce.16
  1429.9 42.8 all-reduce.18
  1899.8 68.3 all-reduce.20
  1972.2 62.0 reduce-scatter.33
  2038.8 66.9 reduce-scatter.13
  2110.2 66.9 reduce-scatter.15
  2181.3 86.8 reduce-scatter.23
  2271.7 87.6 reduce-scatter.25
  2363.4 148.7 reduce-scatter.27
  2515.7 147.9 reduce-scatter.29
  2667.7 148.4 reduce-scatter.31
  2819.7 147.9 reduce-scatter.17
  2971.8 148.0 reduce-scatter.19
  3123.4 147.9 reduce-scatter.21
where the time goes:
time: 3290 us; the launch traced here: 3280 us
  waiting for transfers between devices  2780 us (84%)
  matrix products  255 us (8%)
  other arithmetic  130 us (4%)
  local copies, waits for them, and re-layouts  93.9 us (3%)
    reduce_scatter x10, waiting for transfers between devices, reduce_rows(): lax.psum_scatter(jnp.einsum('mtd,mtk->dk', row_source, col_source, prefer...  1190 us
    psum x7, waiting for transfers between devices, tensor_total(): return lax.psum(partial_sum.astype(jnp.bfloat16), 'tp').astype(jnp.float32)  296 us
    ppermute x16, waiting for transfers between devices, from_behind(): return lax.ppermute(value, axis, pairs)  253 us
    all_gather x2, waiting for transfers between devices, gather_triple(): lax.all_gather(first_mat, 'seq', axis=0, tiled=True)  238 us
    all_gather x2, waiting for transfers between devices, gather_triple(): lax.all_gather(second_mat, 'seq', axis=0, tiled=True)  237 us
    all_gather x2, waiting for transfers between devices, gather_triple(): lax.all_gather(third_mat, 'seq', axis=0, tiled=True)  233 us
    all_gather x2, waiting for transfers between devices, gather_pair(): lax.all_gather(first_mat, 'seq', axis=0, tiled=True)  115 us
    all_gather x2, waiting for transfers between devices, gather_pair(): lax.all_gather(second_mat, 'seq', axis=0, tiled=True)  98.9 us
  transfers between devices with their start and end apart: 46, of which 45 were waited for; matrix products, arithmetic and copies ran while one was open for 7% of the time, Pallas kernels for 0%

commit v1 on v0

v1 whole, which is shorter than its diff:
```python
import jax
import jax.numpy as jnp
from jax import lax
from jax.sharding import Mesh
from jax.sharding import PartitionSpec as P

HD = 128
EPS = 1e-05
FILL = -1e30
BF = jnp.bfloat16
F32 = jnp.float32
SEQ = ("ze", "zh", "zl", "y")
TP = ("x", "c")


def swap(value, axis):
    return lax.ppermute(value, axis, [(0, 1), (1, 0)])


def dot(a, b):
    return jnp.dot(a, b, preferred_element_type=F32)


def dot_nt(a, b):
    return lax.dot_general(a, b, (((1,), (1,)), ((), ())), preferred_element_type=F32)


def dot_tn(a, b):
    return lax.dot_general(a, b, (((0,), (0,)), ((), ())), preferred_element_type=F32)


def in_order(bit, own, other, axis):
    return jnp.where(
        bit == 0,
        jnp.concatenate([own, other], axis),
        jnp.concatenate([other, own], axis),
    )


def half(value, bit, axis):
    size = value.shape[axis] // 2
    return lax.dynamic_slice_in_dim(value, bit * size, size, axis)


def over_ze(value):
    if lax.axis_size("ze") == 1:
        return value
    return lax.all_gather(value, "ze", axis=0, tiled=True)


def total_ze(value):
    if lax.axis_size("ze") == 1:
        return value
    return lax.psum_scatter(value.astype(BF), "ze", scatter_dimension=0, tiled=True).astype(F32)


class Place:
    def __init__(self, width):
        self.zh = lax.axis_index("zh")
        self.zl = lax.axis_index("zl")
        self.y = lax.axis_index("y")
        self.x = lax.axis_index("x")
        self.c = lax.axis_index("c")
        self.ze = lax.axis_size("ze")
        self.rows = width // (self.ze * 8)

    def turn(self, value):
        lead = value.shape[:-1]
        n = len(lead)
        v = value.reshape(lead + (self.ze, 2, 2, 2, self.rows))
        v = jnp.moveaxis(v, n + 3, n)
        v = jnp.where(self.y == 1, jnp.flip(v, n), v)
        v = jnp.where(self.zh == 1, jnp.flip(v, n + 2), v)
        return v.reshape(value.shape)

    def turn_back(self, value):
        lead = value.shape[:-1]
        n = len(lead)
        v = value.reshape(lead + (2, self.ze, 2, 2, self.rows))
        v = jnp.where(self.y == 1, jnp.flip(v, n), v)
        v = jnp.where(self.zh == 1, jnp.flip(v, n + 2), v)
        v = jnp.moveaxis(v, n, n + 3)
        return v.reshape(value.shape)

    def gather(self, w):
        a = in_order(self.zl, half(w, self.zl, 1), swap(half(w, 1 - self.zl, 1), "zl"), 0)
        b = jnp.concatenate([a, swap(a, "zh")], 0)
        b = over_ze(b)
        p = swap(b, "y")
        return jnp.concatenate(
            [
                jnp.concatenate([b, swap(b, "c")], 1),
                jnp.concatenate([p, swap(p, "c")], 1),
            ],
            0,
        )

    def scatter(self, left, right):
        d = left.shape[1] // 2
        k = right.shape[1] // 2
        l_own, l_far = left[:, :d], left[:, d:]
        r_own, r_far = right[:, :k], right[:, k:]
        got_far = swap(dot_tn(l_far, r_far).astype(BF), "c")
        got_own = swap(dot_tn(l_own, r_far).astype(BF), "c")
        t_far = (dot_tn(l_far, r_own) + got_far.astype(F32)).astype(BF)
        got_y = swap(t_far, "y")
        t = (dot_tn(l_own, r_own) + got_own.astype(F32) + got_y.astype(F32)).astype(BF)
        t = total_ze(t)
        m = t.shape[0] // 2
        u = (t[:m].astype(F32) + swap(t[m:].astype(BF), "zh").astype(F32)).astype(BF)
        own = half(u, self.zl, 0)
        got = swap(half(u, 1 - self.zl, 0), "zl")
        return in_order(self.zl, own, got, 1).astype(F32)

    def gather_rows(self, w):
        a = in_order(self.zl, w, swap(w, "zl"), 0)
        b = jnp.concatenate([a, swap(a, "zh")], 0)
        b = over_ze(b)
        return jnp.concatenate([b, swap(b, "y")], 0)

    def scatter_rows(self, left, right):
        d = left.shape[1] // 2
        got = swap(dot_tn(left[:, d:], right).astype(BF), "y")
        t = (dot_tn(left[:, :d], right) + got.astype(F32)).astype(BF)
        t = total_ze(t)
        m = t.shape[0] // 2
        u = t[:m].astype(F32) + swap(t[m:].astype(BF), "zh").astype(F32)
        own = half(u, self.zl, 0)
        return own + swap(half(u, 1 - self.zl, 0).astype(BF), "zl").astype(F32)

    def spread(self, v):
        h = v.shape[1] // 2
        vx = swap(v, "x")
        vz = swap(v, "zl")
        both = jnp.concatenate([swap(vz[:, :h], "x"), swap(vx[:, h:], "zl")], 1)
        return jnp.concatenate([v, vx, vz, both], 0)

    def collect(self, part):
        t, d = part.shape
        h = d // 2
        part = part.reshape(4, t // 4, d)
        a, b = part[..., :h], part[..., h:]
        got_a = swap(a[2:].astype(BF), "zl").astype(F32)
        got_b = swap(b[1::2].astype(BF), "x").astype(F32)
        a_x = (a[1] + got_a[1]).astype(BF)
        b_z = (b[2] + got_b[1]).astype(BF)
        a0 = a[0] + got_a[0] + swap(a_x, "x").astype(F32)
        b0 = b[0] + got_b[0] + swap(b_z, "zl").astype(F32)
        return jnp.concatenate([a0, b0], 1)

    def own_rows(self, v):
        mb, t, d = v.shape
        v = v.reshape(mb, 4, t // 4, d)
        v = lax.dynamic_slice_in_dim(v, self.x * 2 + self.c, 1, 1)
        return v.reshape(mb * t // 4, d)

    def spread_tp(self, v, mb):
        vc = swap(v, "c")
        pair = in_order(
            self.c, v.reshape(mb, 1, -1, v.shape[1]), vc.reshape(mb, 1, -1, v.shape[1]), 1
        )
        far = swap(pair, "x")
        full = in_order(self.x, pair, far, 1)
        return full.reshape(mb, -1, v.shape[1])

    def collect_tp(self, part, mb):
        t, d = part.shape
        part = part.reshape(mb, 2, 2, t // (4 * mb), d)
        mine = half(part, self.c, 2)
        mine = mine + swap(half(part, 1 - self.c, 2).astype(BF), "c").astype(F32)
        own = half(mine, self.x, 1)
        own = own + swap(half(mine, 1 - self.x, 1).astype(BF), "x").astype(F32)
        return own.reshape(t // 4, d)

    def memory_in(self, m):
        mb, t, k = m.shape
        v = m.reshape(mb, 2, 2, t // 4, 2, k // 2)
        keep = half(v, self.c, 2)
        got = swap(half(v, 1 - self.c, 2), "c")
        w = jnp.concatenate([keep, got], 2)
        keep = half(w, self.zl, 4)
        got = swap(half(w, 1 - self.zl, 4), "zl")
        out = jnp.concatenate([keep, got], 4)
        out = jnp.where(self.x == 1, jnp.flip(out, 1), out)
        return out.transpose(4, 1, 0, 3, 2, 5).reshape(4 * mb * t // 4, k)

    def memory_out(self, g, mb):
        t, k = g.shape
        v = g.reshape(2, 2, mb, t // (4 * mb), 2, k // 2).transpose(2, 1, 4, 3, 0, 5)
        v = jnp.where(self.x == 1, jnp.flip(v, 1), v)
        own, far = v[..., 0, :], v[..., 1, :]
        got = swap(far.astype(BF), "zl").astype(F32)
        w = in_order(self.zl, own[..., None, :], got[..., None, :], 4)
        own, far = w[:, :, 0], w[:, :, 1]
        got = swap(far.astype(BF), "c").astype(F32)
        full = in_order(self.c, own[:, :, None], got[:, :, None], 2)
        return full.reshape(mb, t // mb, k)


def rms(v, g):
    r = lax.rsqrt(jnp.mean(v * v, axis=-1, keepdims=True) + EPS)
    return v * r * g


def rms_back(v, g, dn):
    r = lax.rsqrt(jnp.mean(v * v, axis=-1, keepdims=True) + EPS)
    gain = jnp.sum(dn * v * r, axis=0)
    gd = g * dn
    return r * gd - v * (r * r * r) * jnp.mean(v * gd, axis=-1, keepdims=True), gain


def silu_parts(v):
    s = jax.nn.sigmoid(v)
    return v * s, s * (1.0 + v * (1.0 - s))


def to_pairs(v):
    mb, t, k = v.shape
    v = v.reshape(mb, t, k // HD, HD).transpose(0, 2, 1, 3).reshape(-1, t, HD)
    v = lax.all_to_all(v, ("zh", "zl", "y"), split_axis=0, concat_axis=0, tiled=True)
    return v.reshape(-1, HD)


def from_pairs(v, mb, t):
    v = v.reshape(8, t, HD)
    v = lax.all_to_all(v, ("zh", "zl", "y"), split_axis=0, concat_axis=0, tiled=True)
    return v.reshape(mb, -1, t, HD).transpose(0, 2, 1, 3).reshape(mb, t, -1)


def positions(order, first, count, group_len):
    ids = first + jnp.arange(count, dtype=jnp.int32)
    slots = jnp.arange(order.shape[0], dtype=jnp.int32)
    group = jnp.sum(
        jnp.where((ids // group_len)[:, None] == slots[None, :], order[None, :], 0), axis=1
    )
    return group * group_len + ids % group_len


def shards(
    stream_in,
    cache_keys,
    cache_values,
    memory,
    cotangent,
    query_proj,
    output_proj,
    gate_first,
    up_first,
    down_first,
    memory_in,
    memory_out,
    gate_second,
    up_second,
    down_second,
    norm_gains,
    group_order,
    seq_lengths,
):
    mb, tok, width = stream_in.shape
    at = Place(width)
    scaling = HD ** (-0.5)
    groups = group_order.shape[0]
    tokens = tok * at.ze * 8
    group_len = tokens // groups

    gains = at.turn(norm_gains)
    stream = at.turn(stream_in)
    cot = at.turn(cotangent)
    r0 = at.own_rows(stream).astype(F32)

    wq = at.gather_rows(query_proj)
    wo = at.gather_rows(output_proj)
    keys = over_ze(to_pairs(cache_keys))
    values = over_ze(to_pairs(cache_values))

    n1 = rms(stream.astype(F32).reshape(mb * tok, width), gains[0]).astype(BF)
    q = to_pairs(dot(n1, wq).astype(BF).reshape(mb, tok, -1))

    g1, u1, d1 = at.gather(gate_first), at.gather(up_first), at.gather(down_first)
    mi, mo = at.gather(memory_in), at.gather(memory_out)
    g2, u2, d2 = at.gather(gate_second), at.gather(up_second), at.gather(down_second)

    pair = (at.zh * 2 + at.zl) * 2 + at.y
    heads = cache_keys.shape[2] // HD
    batch = pair // heads
    length = lax.dynamic_slice_in_dim(seq_lengths, batch, 1, 0)
    q_rows = q.shape[0]
    k_rows = keys.shape[0]
    q_pos = positions(group_order, lax.axis_index("ze") * q_rows, q_rows, group_len)
    k_pos = positions(group_order, 0, k_rows, group_len)
    allowed = (k_pos[None, :] <= q_pos[:, None]) & (k_pos < length)[None, :]
    s = jnp.where(allowed, dot_nt(q, keys) * scaling, FILL)
    top = jnp.max(s, axis=1, keepdims=True)
    e = jnp.exp(s - top)
    total = jnp.sum(e, axis=1, keepdims=True)
    o = dot(e.astype(BF), values) / total
    lse = top + jnp.log(total)
    attn = from_pairs(o.astype(BF), mb, tok).reshape(mb * tok, -1)

    x1 = r0 + at.collect_tp(dot_nt(attn, wo), mb)

    n2 = at.spread(rms(x1, gains[1]).astype(BF))
    ga, ua = dot(n2, g1), dot(n2, u1)
    ha = (jax.nn.silu(ga) * ua).astype(BF)
    x2 = x1 + at.collect(dot_nt(ha, d1))

    mem = at.memory_in(memory).astype(F32)
    n3 = at.spread(rms(x2, gains[2]).astype(BF))
    za = dot(n3, mi)
    gm = (mem * jax.nn.silu(za)).astype(BF)
    x3 = x2 + at.collect(dot_nt(gm, mo))

    n4 = at.spread(rms(x3, gains[3]).astype(BF))
    gb, ub = dot(n4, g2), dot(n4, u2)
    hb = (jax.nn.silu(gb) * ub).astype(BF)
    x4 = x3 + at.collect(dot_nt(hb, d2))
    stream_out = at.spread_tp(at.turn_back(x4.astype(BF)), mb)

    cv = cot.reshape(mb, 2, 2, tok // 4, width)
    cv = half(cv, at.c, 2)
    cv = jnp.where(at.x == 1, jnp.flip(cv, 1), cv)
    cv = cv.transpose(1, 2, 0, 3, 4).reshape(mb * tok // 2, width)
    yb = jnp.concatenate([cv, swap(cv, "zl")], 0)

    def ffn_back(y, n, gate, up, hidden, wg, wu, wd):
        dh = dot(y, wd)
        act, slope = silu_parts(gate)
        dg = (dh * up * slope).astype(BF)
        du = (dh * act).astype(BF)
        dn = at.collect(dot_nt(dg, wg) + dot_nt(du, wu))
        return dn, at.scatter(n, dg), at.scatter(n, du), at.scatter(y, hidden)

    dn4, gate_second_grad, up_second_grad, down_second_grad = ffn_back(
        yb, n4, gb, ub, hb, g2, u2, d2
    )
    back, gain4 = rms_back(x3, gains[3], dn4)
    dx3 = at.own_rows(cot).astype(F32) + back

    yg = at.spread(dx3.astype(BF))
    dgm = dot(yg, mo)
    act, slope = silu_parts(za)
    memory_grad = at.memory_out(dgm * act, mb)
    dza = (dgm * mem * slope).astype(BF)
    dn3 = at.collect(dot_nt(dza, mi))
    memory_in_grad = at.scatter(n3, dza)
    memory_out_grad = at.scatter(yg, gm)
    back, gain3 = rms_back(x2, gains[2], dn3)
    dx2 = dx3 + back

    ya = at.spread(dx2.astype(BF))
    dn2, gate_first_grad, up_first_grad, down_first_grad = ffn_back(
        ya, n2, ga, ua, ha, g1, u1, d1
    )
    back, gain2 = rms_back(x1, gains[1], dn2)
    dx1 = dx2 + back

    yo = at.spread_tp(dx1.astype(BF), mb).reshape(mb * tok, width)
    do = to_pairs(dot(yo, wo).astype(BF).reshape(mb, tok, -1))
    output_grad = at.scatter_rows(yo, attn)
    delta = jnp.sum(do.astype(F32) * o, axis=1, keepdims=True)
    p = jnp.exp(s - lse)
    ds = (p * (dot_nt(do, values) - delta)).astype(BF)
    dq = from_pairs((dot(ds, keys) * scaling).astype(BF), mb, tok)
    dk = total_ze(dot_tn(ds, q) * scaling).astype(BF)
    dv = total_ze(dot_tn(p.astype(BF), do)).astype(BF)
    keys_grad = from_pairs(dk, mb, tok).astype(F32)
    values_grad = from_pairs(dv, mb, tok).astype(F32)
    dq = dq.reshape(mb * tok, -1)
    dn1 = at.collect_tp(dot_nt(dq, wq), mb)
    query_grad = at.scatter_rows(n1, dq)
    back, gain1 = rms_back(r0, gains[0], dn1)
    stream_grad = at.spread_tp(at.turn_back((dx1 + back).astype(BF)), mb).astype(F32)

    gain = at.turn_back(jnp.stack([gain1, gain2, gain3, gain4]))
    for axis in ("c", "x", "y", "zh", "zl"):
        gain = gain + swap(gain, axis)
    if at.ze > 1:
        gain = lax.psum(gain, "ze")
    spot = (lax.axis_index("ze") * 2 + at.zh) * 4 + at.zl * 2 + at.y
    gains_grad = lax.dynamic_slice_in_dim(gain, spot * at.rows, at.rows, 1)

    return (
        stream_out,
        stream_grad,
        keys_grad,
        values_grad,
        memory_grad,
        query_grad,
        output_grad,
        gate_first_grad,
        up_first_grad,
        down_first_grad,
        memory_in_grad,
        memory_out_grad,
        gate_second_grad,
        up_second_grad,
        down_second_grad,
        gains_grad,
    )


def solution(mesh):
    seq, tp = mesh.shape["seq"], mesh.shape["tp"]
    fine = Mesh(
        mesh.devices.reshape(seq // 8, 2, 2, 2, tp // 2, 2), ("ze", "zh", "zl", "y", "x", "c")
    )
    tokens = P(None, SEQ, None)
    both = P(None, SEQ, TP)
    weight = P(SEQ, TP)
    return jax.shard_map(
        shards,
        mesh=fine,
        in_specs=(tokens, both, both, both, tokens) + (weight,) * 10 + (P(), P(), P()),
        out_specs=(tokens, tokens, both, both, both) + (weight,) * 10 + (P(None, SEQ),),
        check_vma=False,
    )
```

time: 3290 us -> 1760 us (0.53)
  waiting for transfers between devices: 2780 us -> 836 us
  starting transfers between devices: 6.3 us -> 180 us
  other arithmetic: 130 us -> 245 us
  local copies, waits for them, and re-layouts: 93.9 us -> 179 us
  matrix products: 255 us -> 298 us
    reduce_scatter x10 -> x0, waiting for transfers between devices: 1190 us -> none  [reduce_rows(): lax.psum_scatter(jnp.einsum('mtd,mtk->dk', row_source, col_source, prefer...]
    all_gather x12 -> x0, waiting for transfers between devices: 1030 us -> none  [the longest x2 238 us: gather_triple(): lax.all_gather(first_mat, 'seq', axis=0, tiled=True)]
    ppermute x16 -> x156, waiting for transfers between devices: 253 us -> 681 us  [swap(): return lax.ppermute(value, axis, [(0, 1), (1, 0)])]
    psum x7 -> x0, waiting for transfers between devices: 296 us -> none  [tensor_total(): return lax.psum(partial_sum.astype(jnp.bfloat16), 'tp').astype(jnp.float32)]
    all_to_all x0 -> x8, waiting for transfers between devices: none -> 155 us  [the longest x4 147 us: from_pairs(): lax.all_to_all(v, ('zh', 'zl', 'y'), split_axis=0, concat_axis=0, tiled=T...]
    ppermute x16 -> x156, starting transfers between devices: 4.14 us -> 138 us  [swap(): return lax.ppermute(value, axis, [(0, 1), (1, 0)])]
    concatenate x0 -> x20, other arithmetic: none -> 95 us  [the longest x3 57.9 us: gather(): jnp.concatenate([jnp.concatenate([b, swap(b, 'c')], 1), jnp.concatenate([...]
    dot_general x72 -> x62, matrix products: 255 us -> 298 us  [the longest x38 113 us: dot_tn(): lax.dot_general(a, b, (((0,), (0,)), ((), ())), preferred_element_type=F32)]
  transfers between devices with their start and end apart: 46 -> 164, of which waited for: 45 -> 62; matrix products, arithmetic and copies ran while one was open for 7% -> 37% of each run, Pallas kernels for 0% -> 0%
where the time goes in v1:
time: 1760 us; the launch traced here: 1740 us
  waiting for transfers between devices  836 us (48%)
  matrix products  298 us (17%)
  other arithmetic  245 us (14%)
  starting transfers between devices  180 us (10%)
  local copies, waits for them, and re-layouts  179 us (10%)
    ppermute x156, waiting for transfers between devices, swap(): return lax.ppermute(value, axis, [(0, 1), (1, 0)])  681 us
    all_to_all x4, waiting for transfers between devices, from_pairs(): lax.all_to_all(v, ('zh', 'zl', 'y'), split_axis=0, concat_axis=0, tiled=T...  147 us
    ppermute x156, starting transfers between devices, swap(): return lax.ppermute(value, axis, [(0, 1), (1, 0)])  138 us
    dot_general x38, matrix products, dot_tn(): lax.dot_general(a, b, (((0,), (0,)), ((), ())), preferred_element_type=F32)  113 us
    dot_general x12, matrix products, dot(): return jnp.dot(a, b, preferred_element_type=F32)  93.1 us
    dot_general x12, matrix products, dot_nt(): lax.dot_general(a, b, (((1,), (1,)), ((), ())), preferred_element_type=F32)  92.8 us
    concatenate x3, other arithmetic, gather(): jnp.concatenate([jnp.concatenate([b, swap(b, 'c')], 1), jnp.concatenate([...  57.9 us
    unnamed x513, local copies, waits for them, and re-layouts  40.6 us
  transfers between devices with their start and end apart: 164, of which 62 were waited for; matrix products, arithmetic and copies ran while one was open for 37% of the time, Pallas kernels for 0%

profile of v1, /device:TPU:0, one launch (start us, length us, event | category | flops | bytes accessed | tf_op | source)
XLA Modules:
  0.0 1743.7 jit_solution(2794583254253227408)
XLA Ops:
  32.0 35.2 %collective-permute-done.1 = bf16[512,512]{1,0:T(8,128)(2,1)S(1)} collective-permute-done((bf16[512,512]{1,0:T(8,128)(2,1)S(1)}, bf16[512,512]{1,0:T(8,128)(2,1)S(1)}, u32[]{:S(2)}, u32[]{:S(2)}) %collective-permute-start.1) | collective-permute-done | bytes 524320 | tf_op jit(solution)/shard_map/ppermute | solution.py:17
  85.6 6.7 collective-permute-done.2
  103.4 9.9 collective-permute-done.4
  129.2 7.4 all-to-all-done.2
  143.2 10.3 all-to-all-start.3
  163.9 23.8 %all-to-all-done.3 = bf16[8,192,128]{2,1,0:T(8,128)(2,1)S(1)} async-done(((bf16[8,192,128]{2,1,0:T(8,128)(2,1)}), bf16[8,192,128]{2,1,0:T(8,128)(2,1)S(1)}, u32[]{:S(2)}, u32[]{:S(2)}) %all-to-all-start.3) | async-done | bytes 393248 | tf_op jit(solution)/shard_map/all_to_all | solution.py:226
  196.3 12.8 collective-permute-done.13
  225.2 38.1 %collective-permute-done.18 = bf16[512,1024]{1,0:T(8,128)(2,1)} collective-permute-done((bf16[512,1024]{1,0:T(8,128)(2,1)}, bf16[512,1024]{1,0:T(8,128)(2,1)}, u32[]{:S(2)}, u32[]{:S(2)}) %collective-permute-start.18) | collective-permute-done | bytes 1048608 | tf_op jit(solution)/shard_map/ppermute | solution.py:17
  285.7 14.9 collective-permute-done.65
  301.6 28.2 %collective-permute-done.23 = bf16[512,1024]{1,0:T(8,128)(2,1)} collective-permute-done((bf16[512,1024]{1,0:T(8,128)(2,1)}, bf16[512,1024]{1,0:T(8,128)(2,1)}, u32[]{:S(2)}, u32[]{:S(2)}) %collective-permute-start.23) | collective-permute-done | bytes 1048608 | tf_op jit(solution)/shard_map/ppermute | solution.py:17
  359.5 8.6 fusion.244
  369.8 12.9 collective-permute-done.25
  383.2 8.1 maximum_maximum_fusion.1
  398.1 24.3 %maximum_maximum_fusion.2 = bf16[2048,2048]{1,0:T(8,128)(2,1)S(1)} fusion(bf16[1024,1024]{1,0:T(8,128)(2,1)S(1)} %collective-permute-done.26, bf16[1024,1024]{1,0:T(8,128)(2,1)} %collective-permute-done.25, bf16[1024,1024]{1,0:T(8,128)(2,1)S(1)} %collective-permute-done.24, bf16[512,1024]{1,0:T(8,128)(2,1)} %collective-permute-done.23, ...), kind=kLoop, calls=%fused_computation.8 | loop fusion | flops 41943040 | bytes 16777216 | tf_op jit(solution)/shard_map/concatenate | solution.py:90
  439.9 8.2 collective-permute-done.27
  449.8 29.8 %collective-permute-done.38 = bf16[512,512]{1,0:T(8,128)(2,1)S(1)} collective-permute-done((bf16[512,512]{1,0:T(8,128)(2,1)S(1)}, bf16[512,512]{1,0:T(8,128)(2,1)S(1)}, u32[]{:S(2)}, u32[]{:S(2)}) %collective-permute-start.38) | collective-permute-done | bytes 524320 | tf_op jit(solution)/shard_map/ppermute | solution.py:17
  485.1 17.1 collective-permute-done.30
  515.9 42.4 %collective-permute-done.61 = bf16[512,1024]{1,0:T(8,128)(2,1)} collective-permute-done((bf16[512,1024]{1,0:T(8,128)(2,1)}, bf16[512,1024]{1,0:T(8,128)(2,1)}, u32[]{:S(2)}, u32[]{:S(2)}) %collective-permute-start.61) | collective-permute-done | bytes 1048608 | tf_op jit(solution)/shard_map/ppermute | solution.py:17
  569.8 11.0 collective-permute-done.56
  605.2 8.4 collective-permute-done.45
  628.4 30.1 %collective-permute-done.63 = bf16[1024,1024]{1,0:T(8,128)(2,1)} collective-permute-done((bf16[1024,1024]{1,0:T(8,128)(2,1)}, bf16[1024,1024]{1,0:T(8,128)(2,1)}, u32[]{:S(2)}, u32[]{:S(2)}) %collective-permute-start.63) | collective-permute-done | bytes 2097184 | tf_op jit(solution)/shard_map/ppermute | solution.py:17
  665.4 18.0 %fusion.26 = f32[384,2048]{1,0:T(8,128)} fusion(bf16[192,2048]{1,0:T(8,128)(2,1)} %collective-permute-done.76, bf16[192,2048]{1,0:T(8,128)(2,1)} %bitcast.45, bf16[1024,1024]{1,0:T(8,128)(2,1)} %collective-permute-done.69, bf16[1024,1024]{1,0:T(8,128)(2,1)} %collective-permute-done.68, bf16[1024,1024]{1,0:T(8,128)(2,1)S(1)} %collective-permute-done.67, ...), kind=kOutput, calls=%fused_computation.100 | convolution fusion | flops 3266314240 | bytes 13107200 | tf_op jit(solution)/shard_map/dot_general | solution.py:21
  683.3 18.9 %collective-permute-done.58 = bf16[1024,1024]{1,0:T(8,128)(2,1)} collective-permute-done((bf16[1024,1024]{1,0:T(8,128)(2,1)}, bf16[1024,1024]{1,0:T(8,128)(2,1)}, u32[]{:S(2)}, u32[]{:S(2)}) %collective-permute-start.58) | collective-permute-done | bytes 2097184 | tf_op jit(solution)/shard_map/ppermute | solution.py:17
  705.5 25.5 %maximum_maximum_fusion.4 = bf16[2048,2048]{1,0:T(8,128)(2,1)} fusion(bf16[1024,1024]{1,0:T(8,128)(2,1)S(1)} %collective-permute-done.64, bf16[1024,1024]{1,0:T(8,128)(2,1)} %collective-permute-done.63, bf16[1024,1024]{1,0:T(8,128)(2,1)S(1)} %collective-permute-done.62, bf16[512,1024]{1,0:T(8,128)(2,1)} %collective-permute-done.61, ...), kind=kLoop, calls=%fused_computation.10 | loop fusion | flops 41943040 | bytes 16777216 | tf_op jit(solution)/shard_map/concatenate | solution.py:90
  757.3 8.7 fusion.247
  766.1 13.8 multiply_convert_fusion.3
  779.9 9.6 fusion.260
  789.5 11.7 convolution_add_fusion.1
  822.7 23.7 %fusion.245 = f32[384,2048]{1,0:T(8,128)S(1)} fusion(bf16[384,2048]{1,0:T(8,128)(2,1)S(1)} %get-tuple-element.169, bf16[1024,1024]{1,0:T(8,128)(2,1)} %collective-permute-done.69, bf16[1024,1024]{1,0:T(8,128)(2,1)} %collective-permute-done.68, bf16[1024,1024]{1,0:T(8,128)(2,1)} %copy-done.237, bf16[512,1024]{1,0:T(8,128)(2,1)S(1)} %copy-done.136, ...), kind=kOutput, calls=%fused_computation.537 | convolution fusion | flops 3263168512 | bytes 13107200 | tf_op jit(solution)/shard_map/dot_general | solution.py:25
  918.5 10.2 fusion.241
  968.4 10.3 collective-permute-done.86
  1024.2 9.7 multiply_convert_fusion.1
  1039.0 11.5 convolution_add_fusion
  1094.1 16.7 collective-permute-done.133
  1114.5 18.8 %collective-permute-done.128 = bf16[1024,512]{0,1:T(8,128)(2,1)} collective-permute-done((bf16[1024,512]{0,1:T(8,128)(2,1)}, bf16[1024,512]{0,1:T(8,128)(2,1)}, u32[]{:S(2)}, u32[]{:S(2)}) %collective-permute-start.128) | collective-permute-done | bytes 1048608 | tf_op jit(solution)/shard_map/ppermute | solution.py:17
  1138.6 24.6 %collective-permute-done.134 = bf16[512,512]{0,1:T(8,128)(2,1)S(1)} collective-permute-done((bf16[512,512]{0,1:T(8,128)(2,1)S(1)}, bf16[512,512]{0,1:T(8,128)(2,1)S(1)}, u32[]{:S(2)}, u32[]{:S(2)}) %collective-permute-start.134) | collective-permute-done | bytes 524320 | tf_op jit(solution)/shard_map/ppermute | solution.py:17
  1166.5 7.3 collective-permute-done.129
  1210.9 15.4 collective-permute-done.143
  1238.9 30.4 %collective-permute-done.138 = bf16[1024,1024]{0,1:T(8,128)(2,1)} collective-permute-done((bf16[1024,1024]{0,1:T(8,128)(2,1)}, bf16[1024,1024]{0,1:T(8,128)(2,1)}, u32[]{:S(2)}, u32[]{:S(2)}) %collective-permute-start.138) | collective-permute-done | bytes 2097184 | tf_op jit(solution)/shard_map/ppermute | solution.py:17
  1311.9 104.3 %all-to-all-done.5 = bf16[8,192,128]{2,1,0:T(8,128)(2,1)S(1)} async-done(((bf16[8,192,128]{2,1,0:T(8,128)(2,1)}), bf16[8,192,128]{2,1,0:T(8,128)(2,1)S(1)}, u32[]{:S(2)}, u32[]{:S(2)}) %all-to-all-start.5) | async-done | bytes 393248 | tf_op jit(solution)/shard_map/all_to_all | solution.py:226
  1429.1 14.9 all-to-all-done.7
  1472.3 10.4 collective-permute-done.145
  1486.3 7.3 collective-permute-done.140
  1523.6 7.9 collective-permute-done.118
  1539.3 37.1 %collective-permute-done.113 = bf16[1024,1024]{0,1:T(8,128)(2,1)} collective-permute-done((bf16[1024,1024]{0,1:T(8,128)(2,1)}, bf16[1024,1024]{0,1:T(8,128)(2,1)}, u32[]{:S(2)}, u32[]{:S(2)}) %collective-permute-start.113) | collective-permute-done | bytes 2097184 | tf_op jit(solution)/shard_map/ppermute | solution.py:17
  1581.6 16.1 collective-permute-done.105
  1629.1 61.7 %collective-permute-done.154 = f32[4,2048]{1,0:T(4,128)S(1)} collective-permute-done((f32[4,2048]{1,0:T(4,128)S(1)}, f32[4,2048]{1,0:T(4,128)S(1)}, u32[]{:S(2)}, u32[]{:S(2)}) %collective-permute-start.154) | collective-permute-done | bytes 32800 | tf_op jit(solution)/shard_map/ppermute | solution.py:17
  1722.1 9.3 collective-permute-done.120
  (1184 shorter events, 796.9 us)
Async XLA Ops:
  5.6 90.6 %all-to-all-start.1 = ((bf16[8,192,128]{2,1,0:T(8,128)(2,1)}), bf16[8,192,128]{2,1,0:T(8,128)(2,1)}, u32[]{:S(2)}, u32[]{:S(2)}) async-start(bf16[8,192,128]{2,1,0:T(8,128)(2,1)} %bitcast.6), calls=%async_computation.1 | async-start | bytes 786432 | tf_op jit(solution)/shard_map/all_to_all | solution.py:220
  10.4 70.3 %collective-permute-start.3 = (bf16[256,512]{1,0:T(8,128)(2,1)}, bf16[256,512]{1,0:T(8,128)(2,1)}, u32[]{:S(2)}, u32[]{:S(2)}) collective-permute-start(bf16[256,512]{1,0:T(8,128)(2,1)} %param.24), channel_id=1, source_target_pairs={{0,8},{8,0},{1,9},{9,1},{2,10},{10,2},{3,11},{11,3},{4,12},{12,4},... | collective-permute-start | bytes 786440 | tf_op jit(solution)/shard_map/ppermute | solution.py:17
  13.5 142.8 %collective-permute-start.12 = (bf16[256,1024]{1,0:T(8,128)(2,1)}, bf16[256,1024]{1,0:T(8,128)(2,1)}, u32[]{:S(2)}, u32[]{:S(2)}) collective-permute-start(bf16[256,1024]{1,0:T(8,128)(2,1)} %get-tuple-element.215), channel_id=1, source_target_pairs={{0,8},{8,0},{1,9},{9,1},{2,10},{10,2},{3,11},{11,3},{4,12},{12,4},... | collective-permute-start | bytes 1572872 | tf_op jit(solution)/shard_map/ppermute | solution.py:17
  15.1 198.6 %collective-permute-start.17 = (bf16[256,1024]{1,0:T(8,128)(2,1)}, bf16[256,1024]{1,0:T(8,128)(2,1)}, u32[]{:S(2)}, u32[]{:S(2)}) collective-permute-start(bf16[256,1024]{1,0:T(8,128)(2,1)} %get-tuple-element.217), channel_id=1, source_target_pairs={{0,8},{8,0},{1,9},{9,1},{2,10},{10,2},{3,11},{11,3},{4,12},{12,4},... | collective-permute-start | bytes 1572872 | tf_op jit(solution)/shard_map/ppermute | solution.py:17
  17.6 250.1 %collective-permute-start.22 = (bf16[256,1024]{1,0:T(8,128)(2,1)}, bf16[256,1024]{1,0:T(8,128)(2,1)}, u32[]{:S(2)}, u32[]{:S(2)}) collective-permute-start(bf16[256,1024]{1,0:T(8,128)(2,1)} %get-tuple-element.213), channel_id=1, source_target_pairs={{0,8},{8,0},{1,9},{9,1},{2,10},{10,2},{3,11},{11,3},{4,12},{12,4},... | collective-permute-start | bytes 1572872 | tf_op jit(solution)/shard_map/ppermute | solution.py:17
  114.4 76.2 %collective-permute-start.5 = (bf16[1024,512]{1,0:T(8,128)(2,1)}, bf16[1024,512]{1,0:T(8,128)(2,1)}, u32[]{:S(2)}, u32[]{:S(2)}) collective-permute-start(bf16[1024,512]{1,0:T(8,128)(2,1)} %pad_maximum_fusion.11), channel_id=1, source_target_pairs={{0,4},{4,0},{1,5},{5,1},{2,6},{6,2},{3,7},{7,3},{8,12},{12,8},{9,1... | collective-permute-start | bytes 3145736 | tf_op jit(solution)/shard_map/ppermute | solution.py:17
  212.2 71.3 %collective-permute-start.15 = (bf16[1024,1024]{1,0:T(8,128)(2,1)}, bf16[1024,1024]{1,0:T(8,128)(2,1)}, u32[]{:S(2)}, u32[]{:S(2)}) collective-permute-start(bf16[1024,1024]{1,0:T(8,128)(2,1)} %pad_maximum_fusion.2), channel_id=1, source_target_pairs={{0,4},{4,0},{1,5},{5,1},{2,6},{6,2},{3,7},{7,3},{8,12},{12,8},{9,1... | collective-permute-start | bytes 6291464 | tf_op jit(solution)/shard_map/ppermute | solution.py:17
  221.7 112.6 %collective-permute-start.14 = (bf16[1024,1024]{1,0:T(8,128)(2,1)}, bf16[1024,1024]{1,0:T(8,128)(2,1)}, u32[]{:S(2)}, u32[]{:S(2)}) collective-permute-start(bf16[1024,1024]{1,0:T(8,128)(2,1)} %pad_maximum_fusion.2), channel_id=1, source_target_pairs={{0,1},{1,0},{2,3},{3,2},{4,5},{5,4},{6,7},{7,6},{8,9},{9,8},{10,11... | collective-permute-start | bytes 6291464 | tf_op jit(solution)/shard_map/ppermute | solution.py:17
  266.3 68.0 %collective-permute-start.20 = (bf16[1024,1024]{1,0:T(8,128)(2,1)}, bf16[1024,1024]{1,0:T(8,128)(2,1)}, u32[]{:S(2)}, u32[]{:S(2)}) collective-permute-start(bf16[1024,1024]{1,0:T(8,128)(2,1)} %pad_maximum_fusion.3), channel_id=1, source_target_pairs={{0,4},{4,0},{1,5},{5,1},{2,6},{6,2},{3,7},{7,3},{8,12},{12,8},{9,1... | collective-permute-start | bytes 6291464 | tf_op jit(solution)/shard_map/ppermute | solution.py:17
  283.5 75.5 %collective-permute-start.16 = (bf16[1024,1024]{1,0:T(8,128)(2,1)}, bf16[1024,1024]{1,0:T(8,128)(2,1)}, u32[]{:S(2)}, u32[]{:S(2)}) collective-permute-start(bf16[1024,1024]{1,0:T(8,128)(2,1)} %collective-permute-done.15), channel_id=1, source_target_pairs={{0,1},{1,0},{2,3},{3,2},{4,5},{5,4},{6,7},{7,6},{8,9},{9,8},{10,11... | collective-permute-start | bytes 6291464 | tf_op jit(solution)/shard_map/ppermute | solution.py:17
  359.1 67.9 %collective-permute-start.31 = (bf16[2,2,1,48,2,512]{5,4,3,2,1,0:T(2,128)(2,1)S(1)}, bf16[2,2,1,48,2,512]{5,4,3,2,1,0:T(2,128)(2,1)S(1)}, u32[]{:S(2)}, u32[]{:S(2)}) collective-permute-start(bf16[2,2,1,48,2,512]{5,4,3,2,1,0:T(2,128)(2,1)S(1)} %get-tuple-element.223), channel_id=1, source_target_pairs={{0,1},{1,0},{2,3},{3,2},{4,5},{5,4},{6,7},{7,6},{8,9},{9,8},{10,11... | collective-permute-start | bytes 1179656 | tf_op jit(solution)/shard_map/ppermute | solution.py:17
  359.1 73.3 %collective-permute-start.60 = (bf16[256,1024]{1,0:T(8,128)(2,1)S(1)}, bf16[256,1024]{1,0:T(8,128)(2,1)S(1)}, u32[]{:S(2)}, u32[]{:S(2)}) collective-permute-start(bf16[256,1024]{1,0:T(8,128)(2,1)S(1)} %copy-done.156), channel_id=1, source_target_pairs={{0,8},{8,0},{1,9},{9,1},{2,10},{10,2},{3,11},{11,3},{4,12},{12,4},... | collective-permute-start | bytes 1572872 | tf_op jit(solution)/shard_map/ppermute | solution.py:17
  368.1 66.5 %collective-permute-start.55 = (bf16[256,1024]{1,0:T(8,128)(2,1)S(1)}, bf16[256,1024]{1,0:T(8,128)(2,1)S(1)}, u32[]{:S(2)}, u32[]{:S(2)}) collective-permute-start(bf16[256,1024]{1,0:T(8,128)(2,1)S(1)} %get-tuple-element.211), channel_id=1, source_target_pairs={{0,8},{8,0},{1,9},{9,1},{2,10},{10,2},{3,11},{11,3},{4,12},{12,4},... | collective-permute-start | bytes 1572872 | tf_op jit(solution)/shard_map/ppermute | solution.py:17
  398.0 82.7 %collective-permute-start.66 = (bf16[512,1024]{1,0:T(8,128)(2,1)S(1)}, bf16[512,1024]{1,0:T(8,128)(2,1)S(1)}, u32[]{:S(2)}, u32[]{:S(2)}) collective-permute-start(bf16[512,1024]{1,0:T(8,128)(2,1)S(1)} %maximum_select_fusion.10), channel_id=1, source_target_pairs={{0,16},{16,0},{1,17},{17,1},{2,18},{18,2},{3,19},{19,3},{4,20},{20... | collective-permute-start | bytes 3145736 | tf_op jit(solution)/shard_map/ppermute | solution.py:17
  434.6 77.9 %collective-permute-start.76 = (bf16[192,2048]{1,0:T(8,128)(2,1)}, bf16[192,2048]{1,0:T(8,128)(2,1)}, u32[]{:S(2)}, u32[]{:S(2)}) collective-permute-start(bf16[192,2048]{1,0:T(8,128)(2,1)} %bitcast.45), channel_id=1, source_target_pairs={{0,8},{8,0},{1,9},{9,1},{2,10},{10,2},{3,11},{11,3},{4,12},{12,4},... | collective-permute-start | bytes 2359304 | tf_op jit(solution)/shard_map/ppermute | solution.py:17
  438.1 65.8 %collective-permute-start.43 = (bf16[512,512]{1,0:T(8,128)(2,1)S(1)}, bf16[512,512]{1,0:T(8,128)(2,1)S(1)}, u32[]{:S(2)}, u32[]{:S(2)}) collective-permute-start(bf16[512,512]{1,0:T(8,128)(2,1)S(1)} %maximum_select_fusion.23), channel_id=1, source_target_pairs={{0,16},{16,0},{1,17},{17,1},{2,18},{18,2},{3,19},{19,3},{4,20},{20... | collective-permute-start | bytes 1572872 | tf_op jit(solution)/shard_map/ppermute | solution.py:17
  484.2 74.1 %collective-permute-start.61 = (bf16[512,1024]{1,0:T(8,128)(2,1)}, bf16[512,1024]{1,0:T(8,128)(2,1)}, u32[]{:S(2)}, u32[]{:S(2)}) collective-permute-start(bf16[512,1024]{1,0:T(8,128)(2,1)} %maximum_select_fusion.9), channel_id=1, source_target_pairs={{0,16},{16,0},{1,17},{17,1},{2,18},{18,2},{3,19},{19,3},{4,20},{20... | collective-permute-start | bytes 3145736 | tf_op jit(solution)/shard_map/ppermute | solution.py:17
  502.1 78.7 %collective-permute-start.56 = (bf16[512,1024]{1,0:T(8,128)(2,1)}, bf16[512,1024]{1,0:T(8,128)(2,1)}, u32[]{:S(2)}, u32[]{:S(2)}) collective-permute-start(bf16[512,1024]{1,0:T(8,128)(2,1)} %maximum_select_fusion.8), channel_id=1, source_target_pairs={{0,16},{16,0},{1,17},{17,1},{2,18},{18,2},{3,19},{19,3},{4,20},{20... | collective-permute-start | bytes 3145736 | tf_op jit(solution)/shard_map/ppermute | solution.py:17
  504.7 82.5 %collective-permute-start.40 = (bf16[1024,512]{1,0:T(8,128)(2,1)}, bf16[1024,512]{1,0:T(8,128)(2,1)}, u32[]{:S(2)}, u32[]{:S(2)}) collective-permute-start(bf16[1024,512]{1,0:T(8,128)(2,1)} %pad_maximum_fusion.12), channel_id=1, source_target_pairs={{0,4},{4,0},{1,5},{5,1},{2,6},{6,2},{3,7},{7,3},{8,12},{12,8},{9,1... | collective-permute-start | bytes 3145736 | tf_op jit(solution)/shard_map/ppermute | solution.py:17
  510.5 78.1 %collective-permute-start.39 = (bf16[1024,512]{1,0:T(8,128)(2,1)}, bf16[1024,512]{1,0:T(8,128)(2,1)}, u32[]{:S(2)}, u32[]{:S(2)}) collective-permute-start(bf16[1024,512]{1,0:T(8,128)(2,1)} %pad_maximum_fusion.12), channel_id=1, source_target_pairs={{0,1},{1,0},{2,3},{3,2},{4,5},{5,4},{6,7},{7,6},{8,9},{9,8},{10,11... | collective-permute-start | bytes 3145736 | tf_op jit(solution)/shard_map/ppermute | solution.py:17
  512.5 101.1 %collective-permute-start.68 = (bf16[1024,1024]{1,0:T(8,128)(2,1)}, bf16[1024,1024]{1,0:T(8,128)(2,1)}, u32[]{:S(2)}, u32[]{:S(2)}) collective-permute-start(bf16[1024,1024]{1,0:T(8,128)(2,1)} %pad_maximum_fusion.7), channel_id=1, source_target_pairs={{0,4},{4,0},{1,5},{5,1},{2,6},{6,2},{3,7},{7,3},{8,12},{12,8},{9,1... | collective-permute-start | bytes 6291464 | tf_op jit(solution)/shard_map/ppermute | solution.py:17
  592.2 66.4 %collective-permute-start.63 = (bf16[1024,1024]{1,0:T(8,128)(2,1)}, bf16[1024,1024]{1,0:T(8,128)(2,1)}, u32[]{:S(2)}, u32[]{:S(2)}) collective-permute-start(bf16[1024,1024]{1,0:T(8,128)(2,1)} %pad_maximum_fusion.6), channel_id=1, source_target_pairs={{0,4},{4,0},{1,5},{5,1},{2,6},{6,2},{3,7},{7,3},{8,12},{12,8},{9,1... | collective-permute-start | bytes 6291464 | tf_op jit(solution)/shard_map/ppermute | solution.py:17
  621.0 81.2 %collective-permute-start.58 = (bf16[1024,1024]{1,0:T(8,128)(2,1)}, bf16[1024,1024]{1,0:T(8,128)(2,1)}, u32[]{:S(2)}, u32[]{:S(2)}) collective-permute-start(bf16[1024,1024]{1,0:T(8,128)(2,1)} %pad_maximum_fusion.5), channel_id=1, source_target_pairs={{0,4},{4,0},{1,5},{5,1},{2,6},{6,2},{3,7},{7,3},{8,12},{12,8},{9,1... | collective-permute-start | bytes 6291464 | tf_op jit(solution)/shard_map/ppermute | solution.py:17
  627.9 77.5 %collective-permute-start.62 = (bf16[1024,1024]{1,0:T(8,128)(2,1)}, bf16[1024,1024]{1,0:T(8,128)(2,1)S(1)}, u32[]{:S(2)}, u32[]{:S(2)}) collective-permute-start(bf16[1024,1024]{1,0:T(8,128)(2,1)} %pad_maximum_fusion.6), channel_id=1, source_target_pairs={{0,1},{1,0},{2,3},{3,2},{4,5},{5,4},{6,7},{7,6},{8,9},{9,8},{10,11... | collective-permute-start | bytes 6291464 | tf_op jit(solution)/shard_map/ppermute | solution.py:17
  855.9 145.9 %collective-permute-start.147 = (bf16[1024,1024]{0,1:T(8,128)(2,1)}, bf16[1024,1024]{0,1:T(8,128)(2,1)}, u32[]{:S(2)}, u32[]{:S(2)}) collective-permute-start(bf16[1024,1024]{0,1:T(8,128)(2,1)} %convolution_convert_fusion), channel_id=1, source_target_pairs={{0,1},{1,0},{2,3},{3,2},{4,5},{5,4},{6,7},{7,6},{8,9},{9,8},{10,11... | collective-permute-start | bytes 6291464 | tf_op jit(solution)/shard_map/ppermute | solution.py:17
  855.9 139.8 %collective-permute-start.142 = (bf16[1024,1024]{0,1:T(8,128)(2,1)}, bf16[1024,1024]{0,1:T(8,128)(2,1)}, u32[]{:S(2)}, u32[]{:S(2)}) collective-permute-start(bf16[1024,1024]{0,1:T(8,128)(2,1)} %convolution_convert_fusion.2), channel_id=1, source_target_pairs={{0,1},{1,0},{2,3},{3,2},{4,5},{5,4},{6,7},{7,6},{8,9},{9,8},{10,11... | collective-permute-start | bytes 6291464 | tf_op jit(solution)/shard_map/ppermute | solution.py:17
  1007.8 157.0 %collective-permute-start.146 = (bf16[1024,1024]{0,1:T(8,128)(2,1)}, bf16[1024,1024]{0,1:T(8,128)(2,1)}, u32[]{:S(2)}, u32[]{:S(2)}) collective-permute-start(bf16[1024,1024]{0,1:T(8,128)(2,1)} %convolution_convert_fusion.1), channel_id=1, source_target_pairs={{0,1},{1,0},{2,3},{3,2},{4,5},{5,4},{6,7},{7,6},{8,9},{9,8},{10,11... | collective-permute-start | bytes 6291464 | tf_op jit(solution)/shard_map/ppermute | solution.py:17
  1012.2 81.8 %collective-permute-start.131 = (bf16[1024,512]{0,1:T(8,128)(2,1)}, bf16[1024,512]{0,1:T(8,128)(2,1)}, u32[]{:S(2)}, u32[]{:S(2)}) collective-permute-start(bf16[1024,512]{0,1:T(8,128)(2,1)} %convolution_convert_fusion.13), channel_id=1, source_target_pairs={{0,1},{1,0},{2,3},{3,2},{4,5},{5,4},{6,7},{7,6},{8,9},{9,8},{10,11... | collective-permute-start | bytes 3145736 | tf_op jit(solution)/shard_map/ppermute | solution.py:17
  1012.9 100.2 %collective-permute-start.126 = (bf16[1024,512]{0,1:T(8,128)(2,1)}, bf16[1024,512]{0,1:T(8,128)(2,1)}, u32[]{:S(2)}, u32[]{:S(2)}) collective-permute-start(bf16[1024,512]{0,1:T(8,128)(2,1)} %convolution_convert_fusion.15), channel_id=1, source_target_pairs={{0,1},{1,0},{2,3},{3,2},{4,5},{5,4},{6,7},{7,6},{8,9},{9,8},{10,11... | collective-permute-start | bytes 3145736 | tf_op jit(solution)/shard_map/ppermute | solution.py:17
  1094.0 103.4 %collective-permute-start.141 = (bf16[1024,1024]{0,1:T(8,128)(2,1)}, bf16[1024,1024]{0,1:T(8,128)(2,1)}, u32[]{:S(2)}, u32[]{:S(2)}) collective-permute-start(bf16[1024,1024]{0,1:T(8,128)(2,1)} %convolution_convert_fusion.3), channel_id=1, source_target_pairs={{0,1},{1,0},{2,3},{3,2},{4,5},{5,4},{6,7},{7,6},{8,9},{9,8},{10,11... | collective-permute-start | bytes 6291464 | tf_op jit(solution)/shard_map/ppermute | solution.py:17
  1113.0 94.9 %collective-permute-start.148 = (bf16[1024,1024]{0,1:T(8,128)(2,1)}, bf16[1024,1024]{0,1:T(8,128)(2,1)}, u32[]{:S(2)}, u32[]{:S(2)}) collective-permute-start(bf16[1024,1024]{0,1:T(8,128)(2,1)} %add_convert_fusion.1), channel_id=1, source_target_pairs={{0,4},{4,0},{1,5},{5,1},{2,6},{6,2},{3,7},{7,3},{8,12},{12,8},{9,1... | collective-permute-start | bytes 6291464 | tf_op jit(solution)/shard_map/ppermute | solution.py:17
  1188.7 80.5 %collective-permute-start.138 = (bf16[1024,1024]{0,1:T(8,128)(2,1)}, bf16[1024,1024]{0,1:T(8,128)(2,1)}, u32[]{:S(2)}, u32[]{:S(2)}) collective-permute-start(bf16[1024,1024]{0,1:T(8,128)(2,1)} %add_convert_fusion.5), channel_id=1, source_target_pairs={{0,4},{4,0},{1,5},{5,1},{2,6},{6,2},{3,7},{7,3},{8,12},{12,8},{9,1... | collective-permute-start | bytes 6291464 | tf_op jit(solution)/shard_map/ppermute | solution.py:17
  1197.4 78.0 %collective-permute-start.122 = (bf16[1024,1024]{0,1:T(8,128)(2,1)}, bf16[1024,1024]{0,1:T(8,128)(2,1)}, u32[]{:S(2)}, u32[]{:S(2)}) collective-permute-start(bf16[1024,1024]{0,1:T(8,128)(2,1)} %convolution_convert_fusion.6), channel_id=1, source_target_pairs={{0,1},{1,0},{2,3},{3,2},{4,5},{5,4},{6,7},{7,6},{8,9},{9,8},{10,11... | collective-permute-start | bytes 6291464 | tf_op jit(solution)/shard_map/ppermute | solution.py:17
  1203.8 85.7 %all-to-all-start.4 = ((bf16[8,192,128]{2,1,0:T(8,128)(2,1)}), bf16[8,192,128]{2,1,0:T(8,128)(2,1)S(1)}, u32[]{:S(2)}, u32[]{:S(2)}) async-start(bf16[8,192,128]{2,1,0:T(8,128)(2,1)} %bitcast.422), calls=%async_computation.4 | async-start | bytes 786432 | tf_op jit(solution)/shard_map/all_to_all | solution.py:220
  1207.9 73.1 %collective-permute-start.117 = (bf16[1024,1024]{0,1:T(8,128)(2,1)}, bf16[1024,1024]{0,1:T(8,128)(2,1)S(1)}, u32[]{:S(2)}, u32[]{:S(2)}) collective-permute-start(bf16[1024,1024]{0,1:T(8,128)(2,1)} %convolution_convert_fusion.8), channel_id=1, source_target_pairs={{0,1},{1,0},{2,3},{3,2},{4,5},{5,4},{6,7},{7,6},{8,9},{9,8},{10,11... | collective-permute-start | bytes 6291464 | tf_op jit(solution)/shard_map/ppermute | solution.py:17
  1238.4 231.2 %collective-permute-start.121 = (bf16[1024,1024]{0,1:T(8,128)(2,1)}, bf16[1024,1024]{0,1:T(8,128)(2,1)}, u32[]{:S(2)}, u32[]{:S(2)}) collective-permute-start(bf16[1024,1024]{0,1:T(8,128)(2,1)} %convolution_convert_fusion.7), channel_id=1, source_target_pairs={{0,1},{1,0},{2,3},{3,2},{4,5},{5,4},{6,7},{7,6},{8,9},{9,8},{10,11... | collective-permute-start | bytes 6291464 | tf_op jit(solution)/shard_map/ppermute | solution.py:17
  1275.4 147.8 %collective-permute-start.149 = (bf16[512,1024]{0,1:T(8,128)(2,1)}, bf16[512,1024]{0,1:T(8,128)(2,1)}, u32[]{:S(2)}, u32[]{:S(2)}) collective-permute-start(bf16[512,1024]{0,1:T(8,128)(2,1)} %slice.775), channel_id=1, source_target_pairs={{0,16},{16,0},{1,17},{17,1},{2,18},{18,2},{3,19},{19,3},{4,20},{20... | collective-permute-start | bytes 3145736 | tf_op jit(solution)/shard_map/ppermute | solution.py:17
  1281.0 167.1 %collective-permute-start.144 = (bf16[512,1024]{0,1:T(8,128)(2,1)}, bf16[512,1024]{0,1:T(8,128)(2,1)}, u32[]{:S(2)}, u32[]{:S(2)}) collective-permute-start(bf16[512,1024]{0,1:T(8,128)(2,1)} %slice.767), channel_id=1, source_target_pairs={{0,16},{16,0},{1,17},{17,1},{2,18},{18,2},{3,19},{19,3},{4,20},{20... | collective-permute-start | bytes 3145736 | tf_op jit(solution)/shard_map/ppermute | solution.py:17
  1285.3 167.5 %collective-permute-start.139 = (bf16[512,1024]{0,1:T(8,128)(2,1)}, bf16[512,1024]{0,1:T(8,128)(2,1)}, u32[]{:S(2)}, u32[]{:S(2)}) collective-permute-start(bf16[512,1024]{0,1:T(8,128)(2,1)} %slice.763), channel_id=1, source_target_pairs={{0,16},{16,0},{1,17},{17,1},{2,18},{18,2},{3,19},{19,3},{4,20},{20... | collective-permute-start | bytes 3145736 | tf_op jit(solution)/shard_map/ppermute | solution.py:17
  1298.0 118.2 %all-to-all-start.5 = ((bf16[8,192,128]{2,1,0:T(8,128)(2,1)}), bf16[8,192,128]{2,1,0:T(8,128)(2,1)S(1)}, u32[]{:S(2)}, u32[]{:S(2)}) async-start(bf16[8,192,128]{2,1,0:T(8,128)(2,1)} %bitcast.87), calls=%async_computation.5 | async-start | bytes 786432 | tf_op jit(solution)/shard_map/all_to_all | solution.py:226
  1309.9 206.2 %collective-permute-start.123 = (bf16[1024,1024]{0,1:T(8,128)(2,1)}, bf16[1024,1024]{0,1:T(8,128)(2,1)}, u32[]{:S(2)}, u32[]{:S(2)}) collective-permute-start(bf16[1024,1024]{0,1:T(8,128)(2,1)} %add_convert_fusion.7), channel_id=1, source_target_pairs={{0,4},{4,0},{1,5},{5,1},{2,6},{6,2},{3,7},{7,3},{8,12},{12,8},{9,1... | collective-permute-start | bytes 6291464 | tf_op jit(solution)/shard_map/ppermute | solution.py:17
  1502.9 73.6 %collective-permute-start.113 = (bf16[1024,1024]{0,1:T(8,128)(2,1)}, bf16[1024,1024]{0,1:T(8,128)(2,1)}, u32[]{:S(2)}, u32[]{:S(2)}) collective-permute-start(bf16[1024,1024]{0,1:T(8,128)(2,1)} %add_convert_fusion.11), channel_id=1, source_target_pairs={{0,4},{4,0},{1,5},{5,1},{2,6},{6,2},{3,7},{7,3},{8,12},{12,8},{9,1... | collective-permute-start | bytes 6291464 | tf_op jit(solution)/shard_map/ppermute | solution.py:17
  1516.1 81.6 %collective-permute-start.105 = (bf16[1024,512]{1,0:T(8,128)(2,1)S(1)}, bf16[1024,512]{1,0:T(8,128)(2,1)S(1)}, u32[]{:S(2)}, u32[]{:S(2)}) collective-permute-start(bf16[1024,512]{1,0:T(8,128)(2,1)S(1)} %copy-done.241), channel_id=1, source_target_pairs={{0,4},{4,0},{1,5},{5,1},{2,6},{6,2},{3,7},{7,3},{8,12},{12,8},{9,1... | collective-permute-start | bytes 3145736 | tf_op jit(solution)/shard_map/ppermute | solution.py:17
  1522.3 77.2 %collective-permute-start.100 = (bf16[2,1,1,48,2048]{4,3,0,2,1:T(8,128)(2,1)S(1)}, bf16[2,1,1,48,2048]{4,3,0,2,1:T(8,128)(2,1)S(1)}, u32[]{:S(2)}, u32[]{:S(2)}) collective-permute-start(bf16[2,1,1,48,2048]{4,3,0,2,1:T(8,128)(2,1)S(1)} %dynamic-slice_convert_fusion.2), channel_id=1, source_target_pairs={{0,2},{2,0},{1,3},{3,1},{4,6},{6,4},{5,7},{7,5},{8,10},{10,8},{9,1... | collective-permute-start | bytes 1179656 | tf_op jit(solution)/shard_map/ppermute | solution.py:17
  1531.5 171.7 %collective-permute-start.124 = (bf16[512,1024]{0,1:T(8,128)(2,1)}, bf16[512,1024]{0,1:T(8,128)(2,1)}, u32[]{:S(2)}, u32[]{:S(2)}) collective-permute-start(bf16[512,1024]{0,1:T(8,128)(2,1)} %slice.745), channel_id=1, source_target_pairs={{0,16},{16,0},{1,17},{17,1},{2,18},{18,2},{3,19},{19,3},{4,20},{20... | collective-permute-start | bytes 3145736 | tf_op jit(solution)/shard_map/ppermute | solution.py:17
  1536.9 169.0 %collective-permute-start.119 = (bf16[512,1024]{0,1:T(8,128)(2,1)}, bf16[512,1024]{0,1:T(8,128)(2,1)}, u32[]{:S(2)}, u32[]{:S(2)}) collective-permute-start(bf16[512,1024]{0,1:T(8,128)(2,1)} %slice.739), channel_id=1, source_target_pairs={{0,16},{16,0},{1,17},{17,1},{2,18},{18,2},{3,19},{19,3},{4,20},{20... | collective-permute-start | bytes 3145736 | tf_op jit(solution)/shard_map/ppermute | solution.py:17
  1581.1 128.6 %collective-permute-start.114 = (bf16[512,1024]{0,1:T(8,128)(2,1)}, bf16[512,1024]{0,1:T(8,128)(2,1)}, u32[]{:S(2)}, u32[]{:S(2)}) collective-permute-start(bf16[512,1024]{0,1:T(8,128)(2,1)} %slice.735), channel_id=1, source_target_pairs={{0,16},{16,0},{1,17},{17,1},{2,18},{18,2},{3,19},{19,3},{4,20},{20... | collective-permute-start | bytes 3145736 | tf_op jit(solution)/shard_map/ppermute | solution.py:17
  1599.4 91.4 %collective-permute-start.106 = (bf16[512,512]{1,0:T(8,128)(2,1)}, bf16[512,512]{1,0:T(8,128)(2,1)}, u32[]{:S(2)}, u32[]{:S(2)}) collective-permute-start(bf16[512,512]{1,0:T(8,128)(2,1)} %slice.725), channel_id=1, source_target_pairs={{0,16},{16,0},{1,17},{17,1},{2,18},{18,2},{3,19},{19,3},{4,20},{20... | collective-permute-start | bytes 1572872 | tf_op jit(solution)/shard_map/ppermute | solution.py:17
  (369 other events, 7578.6 us)

commit v2 on v1

v2 whole, which is shorter than its diff:
```python
import jax
import jax.numpy as jnp
from jax import lax
from jax.sharding import Mesh
from jax.sharding import PartitionSpec as P

HD = 128
EPS = 1e-05
FILL = -1e30
BF = jnp.bfloat16
F32 = jnp.float32
SEQ = ("ze", "zh", "zl", "y")
TP = ("x", "c")
GROUP = ("zh", "zl", "y")
UNIT = ("zl", "y", "x", "c")


def swap(value, axis):
    return lax.ppermute(value, axis, [(0, 1), (1, 0)])


def after(value, earlier):
    return lax.optimization_barrier((value, earlier))[0]


def dot(a, b):
    return jnp.dot(a, b, preferred_element_type=F32)


def dot_nt(a, b):
    return lax.dot_general(a, b, (((1,), (1,)), ((), ())), preferred_element_type=F32)


def dot_tn(a, b):
    return lax.dot_general(a, b, (((0,), (0,)), ((), ())), preferred_element_type=F32)


def in_order(bit, own, other, axis):
    return jnp.where(
        bit == 0,
        jnp.concatenate([own, other], axis),
        jnp.concatenate([other, own], axis),
    )


def half(value, bit, axis):
    size = value.shape[axis] // 2
    return lax.dynamic_slice_in_dim(value, bit * size, size, axis)


def trade(value, axes):
    return lax.all_to_all(value, axes, split_axis=0, concat_axis=0, tiled=True)


def copies(value, n):
    return jnp.broadcast_to(value[None], (n,) + value.shape)


def over_ze(value):
    if lax.axis_size("ze") == 1:
        return value
    return lax.all_gather(value, "ze", axis=0, tiled=True)


def total_ze(value):
    if lax.axis_size("ze") == 1:
        return value
    return lax.psum_scatter(value.astype(BF), "ze", scatter_dimension=0, tiled=True).astype(F32)


class Place:
    def __init__(self, width):
        self.zl = lax.axis_index("zl")
        self.x = lax.axis_index("x")
        self.y = lax.axis_index("y")
        self.c = lax.axis_index("c")
        self.ze = lax.axis_size("ze")
        self.rows = width // (self.ze * 8)
        self.line = []
        self.first = []

    def ordered(self, value, axes):
        if self.line:
            value = after(value, self.line[-1])
        if self.first:
            value = after(value, tuple(self.first))
            self.first = []
        self.line.append(trade(value, axes))
        return self.line[-1]

    def gather(self, w):
        r, k = w.shape
        w = w.reshape(r, 4, k // 4).transpose(1, 0, 2)
        w = self.ordered(jnp.concatenate([w, w]), GROUP)
        w = over_ze(w.reshape(8 * r, k // 4))
        own = lax.all_gather(w, "x", axis=1, tiled=True)
        return own, swap(own, "c")

    def open_grad(self, left, far):
        part = dot_tn(left, far).astype(BF)
        return part, swap(part, "c")

    def close_grad(self, left, own, got):
        part = (dot_tn(left, own) + got.astype(F32)).astype(BF)
        t = lax.psum_scatter(part, "x", scatter_dimension=1, tiled=True)
        t = total_ze(t).astype(BF).reshape(8, self.rows, -1)
        t = self.ordered(t, GROUP).astype(F32)
        t = t[:4] + t[4:]
        return part, t.transpose(1, 0, 2).reshape(self.rows, -1)

    def gather_rows(self, w):
        a = self.ordered(copies(w, 4), ("zh", "zl"))
        a = over_ze(a)
        return lax.all_gather(a, "y", axis=1, tiled=True).reshape(-1, w.shape[1])

    def scatter_rows(self, left, right):
        part = dot_tn(left, right).astype(BF)
        t = part.reshape(-1, 2 * self.rows, right.shape[1])
        t = lax.psum_scatter(t, "y", scatter_dimension=1, tiled=True)
        t = self.ordered(total_ze(t).astype(BF), ("zh", "zl")).astype(F32)
        return part, (t[0] + t[1]) + (t[2] + t[3])

    def spread(self, v):
        h = v.shape[1] // 2
        vy = swap(v, "y")
        vz = swap(v, "zl")
        both = jnp.concatenate([swap(vz[:, :h], "y"), swap(vy[:, h:], "zl")], 1)
        return jnp.concatenate([v, vy, vz, both], 0)

    def collect(self, part):
        t, d = part.shape
        h = d // 2
        part = part.reshape(4, t // 4, d)
        a, b = part[..., :h], part[..., h:]
        got_a = swap(a[2:].astype(BF), "zl").astype(F32)
        got_b = swap(b[1::2].astype(BF), "y").astype(F32)
        a_y = (a[1] + got_a[1]).astype(BF)
        b_z = (b[2] + got_b[1]).astype(BF)
        a0 = a[0] + got_a[0] + swap(a_y, "y").astype(F32)
        b0 = b[0] + got_b[0] + swap(b_z, "zl").astype(F32)
        return jnp.concatenate([a0, b0], 1)

    def own_rows(self, v):
        mb, t, d = v.shape
        v = v.reshape(mb, 4, t // 4, d)
        v = lax.dynamic_slice_in_dim(v, self.x * 2 + self.c, 1, 1)
        return v.reshape(mb * t // 4, d)

    def spread_tp(self, v, mb):
        d = v.shape[1]
        v = v.reshape(mb, 1, -1, d)
        pair = in_order(self.c, v, swap(v, "c"), 1)
        full = in_order(self.x, pair, swap(pair, "x"), 1)
        return full.reshape(mb, -1, d)

    def collect_tp(self, part, mb):
        t, d = part.shape
        part = part.reshape(mb, 2, 2, t // (4 * mb), d)
        mine = half(part, self.c, 2)
        mine = mine + swap(half(part, 1 - self.c, 2).astype(BF), "c").astype(F32)
        own = half(mine, self.x, 1)
        own = own + swap(half(mine, 1 - self.x, 1).astype(BF), "x").astype(F32)
        return own.reshape(t // 4, d)

    def flips(self, v, axis):
        v = jnp.where(self.zl == 1, jnp.flip(v, axis), v)
        return jnp.where(self.y == 1, jnp.flip(v, axis + 1), v)

    def memory_in(self, m):
        mb, t, k = m.shape
        v = m.reshape(mb, 4, t // 4, 4, k // 4).transpose(3, 1, 0, 2, 4)
        v = trade(v.reshape(16, mb * t // 4, k // 4), UNIT)
        v = self.flips(v.reshape(2, 2, 2, 2, mb * t // 4, k // 4), 0)
        v = v.transpose(3, 0, 1, 4, 2, 5).reshape(2, mb * t, k // 2)
        return jnp.where(self.c == 0, v[0], v[1]), jnp.where(self.c == 0, v[1], v[0])

    def memory_out(self, own, far, mb):
        t, k = own.shape[0], own.shape[1] * 2
        v = in_order(self.c, own.astype(BF)[None], far.astype(BF)[None], 0)
        v = v.reshape(2, 2, 2, t // 4, 2, k // 4).transpose(1, 2, 4, 0, 3, 5)
        v = self.flips(v, 0).reshape(16, t // 4, k // 4)
        v = trade(v, UNIT).reshape(4, 4, mb, t // (4 * mb), k // 4)
        return v.transpose(2, 1, 3, 0, 4).reshape(mb, t // mb, k).astype(F32)


def rms(v, g):
    r = lax.rsqrt(jnp.mean(v * v, axis=-1, keepdims=True) + EPS)
    return v * r * g


def rms_back(v, g, dn):
    r = lax.rsqrt(jnp.mean(v * v, axis=-1, keepdims=True) + EPS)
    gain = jnp.sum(dn * v * r, axis=0)
    gd = g * dn
    return r * gd - v * (r * r * r) * jnp.mean(v * gd, axis=-1, keepdims=True), gain


def silu_parts(v):
    s = jax.nn.sigmoid(v)
    return v * s, s * (1.0 + v * (1.0 - s))


def exchange(v):
    here = lax.axis_index(GROUP)
    out = []
    for k in range(8):
        block = lax.dynamic_index_in_dim(v, here ^ k, 0, keepdims=False)
        out.append(block if k == 0 else lax.ppermute(block, GROUP, [(i, i ^ k) for i in range(8)]))
    return out


def to_pairs(v):
    n, mb, t, k = v.shape
    v = v.reshape(n, mb, t, k // HD, HD).transpose(1, 3, 0, 2, 4).reshape(-1, n, t, HD)
    return jnp.concatenate(exchange(v), 1)


def from_pairs(v, mb, t):
    n = v.shape[0]
    here = lax.axis_index(GROUP)
    v = v.reshape(n, 8, t, HD)
    got = [v[:, 0]]
    for k in range(1, 8):
        got.append(lax.ppermute(v[:, k], GROUP, [(i, i ^ k) for i in range(8)]))
    v = jnp.stack(got)
    v = jnp.stack([lax.dynamic_index_in_dim(v, here ^ k, 0, keepdims=False) for k in range(8)])
    return v.reshape(mb, -1, n, t, HD).transpose(2, 0, 3, 1, 4).reshape(n, mb, t, -1)


def positions(order, ids, group_len):
    slots = jnp.arange(order.shape[0], dtype=jnp.int32)
    group = jnp.sum(
        jnp.where((ids // group_len)[:, None] == slots[None, :], order[None, :], 0), axis=1
    )
    return group * group_len + ids % group_len


def shards(
    stream_in,
    cache_keys,
    cache_values,
    memory,
    cotangent,
    query_proj,
    output_proj,
    gate_first,
    up_first,
    down_first,
    memory_in,
    memory_out,
    gate_second,
    up_second,
    down_second,
    norm_gains,
    group_order,
    seq_lengths,
):
    mb, tok, width = stream_in.shape
    at = Place(width)
    scaling = HD ** (-0.5)
    groups = group_order.shape[0]
    tokens = tok * at.ze * 8
    group_len = tokens // groups

    gains = norm_gains
    stream = stream_in
    r0 = at.own_rows(stream).astype(F32)

    wq = at.gather_rows(query_proj)
    cache = to_pairs(jnp.stack([cache_keys, cache_values], 0))
    keys, values = over_ze(cache[0]), over_ze(cache[1])
    g1 = at.gather(gate_first)
    wo = at.gather_rows(output_proj)
    at.first = [cache]
    u1 = at.gather(up_first)
    n1 = rms(stream.astype(F32).reshape(mb * tok, width), gains[0]).astype(BF)
    q = to_pairs(dot(n1, wq).astype(BF).reshape(1, mb, tok, -1))[0]
    q = after(q, wo)
    at.first = [q]
    d1 = at.gather(down_first)

    pair = lax.axis_index(("zh", "zl", "y"))
    heads = cache_keys.shape[2] // HD
    batch = pair // heads
    length = lax.dynamic_slice_in_dim(seq_lengths, batch, 1, 0)
    q_rows = q.shape[0]
    k_rows = keys.shape[0]
    rows = jnp.arange(k_rows, dtype=jnp.int32)
    ids = rows // q_rows * q_rows + (rows % q_rows // tok ^ pair) * tok + rows % tok
    k_pos = positions(group_order, ids, group_len)
    q_pos = lax.dynamic_slice_in_dim(k_pos, lax.axis_index("ze") * q_rows, q_rows, 0)
    allowed = (k_pos[None, :] <= q_pos[:, None]) & (k_pos < length)[None, :]
    s = jnp.where(allowed, dot_nt(q, keys) * scaling, FILL)
    top = jnp.max(s, axis=1, keepdims=True)
    e = jnp.exp(s - top)
    total = jnp.sum(e, axis=1, keepdims=True)
    o = dot(e.astype(BF), values) / total
    lse = top + jnp.log(total)
    attn = from_pairs(o.astype(BF)[None], mb, tok).reshape(mb * tok, -1)

    at.first = [attn]
    mi, mo = at.gather(memory_in), at.gather(memory_out)
    x1 = r0 + at.collect_tp(dot_nt(attn, wo), mb)
    at.first = [x1]
    g2 = at.gather(gate_second)

    def ffn(x, gain, wg, wu, wd, pins):
        n = after(at.spread(rms(x, gain).astype(BF)), pins)
        gate = [dot(n, w) for w in wg]
        up = [dot(n, w) for w in wu]
        hidden = [(jax.nn.silu(g) * u).astype(BF) for g, u in zip(gate, up)]
        out = at.collect(dot_nt(hidden[0], wd[0]) + dot_nt(hidden[1], wd[1]))
        return x + out, (n, gate, up, hidden)

    x2, kept1 = ffn(x1, gains[1], g1, u1, d1, ())
    at.first = [kept1[0]]
    u2 = at.gather(up_second)
    at.first = [kept1[3][1]]
    d2 = at.gather(down_second)

    mem = at.memory_in(memory)
    n3 = at.spread(rms(x2, gains[2]).astype(BF))
    za = [dot(n3, w) for w in mi]
    gm = [(m.astype(F32) * jax.nn.silu(z)).astype(BF) for m, z in zip(mem, za)]
    x3 = x2 + at.collect(dot_nt(gm[0], mo[0]) + dot_nt(gm[1], mo[1]))

    x4, kept2 = ffn(x3, gains[3], g2, u2, d2, ())
    stream_out = at.spread_tp(x4.astype(BF), mb)

    cot = at.own_rows(cotangent)
    yb = at.spread(cot)

    zline = at.line

    def ffn_back(y, kept, wg, wu, wd, pins):
        n, gate, up, hidden = kept
        far_d, got_d = at.open_grad(y, hidden[1])
        y2 = after(y, far_d)
        dg, du = [], []
        for g, u, w in zip(gate, up, wd):
            dh = dot(y2, w)
            act, slope = silu_parts(g)
            dg.append((dh * u * slope).astype(BF))
            du.append((dh * act).astype(BF))
        part_d, down_grad = at.close_grad(y, hidden[0], got_d)
        dg, du = after((dg, du), (part_d,) + pins)
        dn = dot_nt(dg[0], wg[0]) + dot_nt(dg[1], wg[1])
        dn = dn + dot_nt(du[0], wu[0]) + dot_nt(du[1], wu[1])
        far_g, got_g = at.open_grad(n, dg[1])
        far_u, got_u = at.open_grad(n, du[1])
        dn = after(at.collect(dn), (far_g, far_u))
        return dn, down_grad, (n, dg[0], got_g), (n, du[0], got_u)

    dn4, down_second_grad, open_g, open_u = ffn_back(yb, kept2, g2, u2, d2, ())
    back, gain4 = rms_back(x3, gains[3], dn4)
    dx3 = cot.astype(F32) + back

    part_g, gate_second_grad = at.close_grad(*open_g)
    yg = after(at.spread(dx3.astype(BF)), part_g)
    part_u, up_second_grad = at.close_grad(*open_u)
    far, got = at.open_grad(yg, gm[1])
    dz, dm = [], []
    for w, z, m in zip(mo, za, mem):
        dgm = dot(yg, w)
        act, slope = silu_parts(z)
        dm.append(dgm * act)
        dz.append((dgm * m.astype(F32) * slope).astype(BF))
    dz = after(dz, (part_u, far))
    dn3 = dot_nt(dz[0], mi[0]) + dot_nt(dz[1], mi[1])
    part_o, memory_out_grad = at.close_grad(yg, gm[0], got)
    far, got = at.open_grad(n3, dz[1])
    dn3 = after(at.collect(dn3), (part_o, far, zline[10]))
    memory_grad = at.memory_out(dm[0], dm[1], mb)
    back, gain3 = rms_back(x2, gains[2], dn3)
    dx2 = dx3 + back

    part_i, memory_in_grad = at.close_grad(n3, dz[0], got)
    ya = after(at.spread(dx2.astype(BF)), (part_i, zline[11]))
    dn2, down_first_grad, open_g, open_u = ffn_back(ya, kept1, g1, u1, d1, (zline[12],))
    dn2 = after(dn2, (zline[13], zline[14]))
    back, gain2 = rms_back(x1, gains[1], dn2)
    dx1 = dx2 + back

    part_g, gate_first_grad = at.close_grad(*open_g)
    yo = after(at.spread_tp(dx1.astype(BF), mb), (part_g, zline[15])).reshape(mb * tok, width)
    part_u, up_first_grad = at.close_grad(*open_u)
    do = to_pairs(dot(yo, wo).astype(BF).reshape(1, mb, tok, -1))[0]
    do = after(do, part_u)
    part_w, output_grad = at.scatter_rows(yo, attn)
    delta = jnp.sum(do.astype(F32) * o, axis=1, keepdims=True)
    p = jnp.exp(s - lse)
    ds = (p * (dot_nt(do, values) - delta)).astype(BF)
    dq = after((dot(ds, keys) * scaling).astype(BF)[None], (part_w, zline[16]))
    dq = from_pairs(dq, mb, tok)
    dk = total_ze(dot_tn(ds, q) * scaling).astype(BF)
    dv = total_ze(dot_tn(p.astype(BF), do)).astype(BF)
    dkv = from_pairs(after(jnp.stack([dk, dv]), dq), mb, tok).astype(F32)
    keys_grad, values_grad = dkv[0], dkv[1]
    dq = dq.reshape(mb * tok, -1)
    dn1 = at.collect_tp(dot_nt(dq, wq), mb)
    _, query_grad = at.scatter_rows(n1, dq)
    back, gain1 = rms_back(r0, gains[0], dn1)
    stream_grad = at.spread_tp((dx1 + back).astype(BF), mb).astype(F32)

    gain = jnp.stack([gain1, gain2, gain3, gain4])
    for axis in ("c", "x", "y", "zh", "zl"):
        gain = gain + swap(gain, axis)
    if at.ze > 1:
        gain = lax.psum(gain, "ze")
    spot = lax.axis_index(SEQ)
    gains_grad = lax.dynamic_slice_in_dim(gain, spot * at.rows, at.rows, 1)

    return (
        stream_out,
        stream_grad,
        keys_grad,
        values_grad,
        memory_grad,
        query_grad,
        output_grad,
        gate_first_grad,
        up_first_grad,
        down_first_grad,
        memory_in_grad,
        memory_out_grad,
        gate_second_grad,
        up_second_grad,
        down_second_grad,
        gains_grad,
    )


def solution(mesh):
    seq, tp = mesh.shape["seq"], mesh.shape["tp"]
    fine = Mesh(
        mesh.devices.reshape(seq // 8, 2, 2, 2, tp // 2, 2), ("ze", "zh", "zl", "y", "x", "c")
    )
    tokens = P(None, SEQ, None)
    both = P(None, SEQ, TP)
    weight = P(SEQ, TP)
    return jax.shard_map(
        shards,
        mesh=fine,
        in_specs=(tokens, both, both, both, tokens) + (weight,) * 10 + (P(), P(), P()),
        out_specs=(tokens, tokens, both, both, both) + (weight,) * 10 + (P(None, SEQ),),
        check_vma=False,
    )
```

time: 1760 us -> 1410 us (0.80)
  waiting for transfers between devices: 836 us -> 588 us
  other arithmetic: 245 us -> 107 us
  starting transfers between devices: 180 us -> 265 us
  matrix products: 298 us -> 241 us
  blocking collectives: 0 us -> 29.3 us
  local copies, waits for them, and re-layouts: 179 us -> 151 us
    ppermute x156 -> x79, waiting for transfers between devices: 681 us -> 255 us  [swap(): return lax.ppermute(value, axis, [(0, 1), (1, 0)])]
    ppermute x0 -> x42, waiting for transfers between devices: none -> 110 us  [the longest x21 99 us: from_pairs(): got.append(lax.ppermute(v[:, k], GROUP, [(i, i ^ k) for i in range(8)]))]
    ppermute x0 -> x42, starting transfers between devices: none -> 78.4 us  [the longest x21 40.6 us: from_pairs(): got.append(lax.ppermute(v[:, k], GROUP, [(i, i ^ k) for i in range(8)]))]
    concatenate x20 -> x16, other arithmetic: 95 us -> 24.4 us  [the longest x8 18.9 us: gather(): w = self.ordered(jnp.concatenate([w, w]), GROUP)]
    all_to_all x8 -> x21, starting transfers between devices: 42.2 us -> 96.3 us  [trade(): return lax.all_to_all(value, axes, split_axis=0, concat_axis=0, tiled=True)]
    ppermute x156 -> x79, starting transfers between devices: 138 us -> 87.8 us  [swap(): return lax.ppermute(value, axis, [(0, 1), (1, 0)])]
    convert_element_type x48 -> x31, other arithmetic: 73.1 us -> 37.3 us  [the longest x8 15.5 us: close_grad(): t = self.ordered(t, GROUP).astype(F32)]
    all_gather x0 -> x10, waiting for transfers between devices: none -> 34.2 us  [the longest x8 34.1 us: gather(): own = lax.all_gather(w, 'x', axis=1, tiled=True)]
  transfers between devices with their start and end apart: 164 -> 162, of which waited for: 62 -> 58; matrix products, arithmetic and copies ran while one was open for 37% -> 34% of each run, Pallas kernels for 0% -> 0%
where the time goes in v2:
time: 1410 us; the launch traced here: 1400 us
  waiting for transfers between devices  588 us (42%)
  starting transfers between devices  265 us (19%)
  matrix products  241 us (17%)
  local copies, waits for them, and re-layouts  151 us (11%)
  other arithmetic  107 us (8%)
  blocking collectives  29.3 us (2%)
  between operations  18 us (1%)
    ppermute x79, waiting for transfers between devices, swap(): return lax.ppermute(value, axis, [(0, 1), (1, 0)])  255 us
    all_to_all x21, waiting for transfers between devices, trade(): return lax.all_to_all(value, axes, split_axis=0, concat_axis=0, tiled=True)  188 us
    ppermute x21, waiting for transfers between devices, from_pairs(): got.append(lax.ppermute(v[:, k], GROUP, [(i, i ^ k) for i in range(8)]))  99 us
    all_to_all x21, starting transfers between devices, trade(): return lax.all_to_all(value, axes, split_axis=0, concat_axis=0, tiled=True)  96.3 us
    ppermute x79, starting transfers between devices, swap(): return lax.ppermute(value, axis, [(0, 1), (1, 0)])  87.8 us
    dot_general x20, matrix products, dot(): return jnp.dot(a, b, preferred_element_type=F32)  82.4 us
    dot_general x20, matrix products, dot_tn(): lax.dot_general(a, b, (((0,), (0,)), ((), ())), preferred_element_type=F32)  81.3 us
    dot_general x20, matrix products, dot_nt(): lax.dot_general(a, b, (((1,), (1,)), ((), ())), preferred_element_type=F32)  77.3 us
  transfers between devices with their start and end apart: 162, of which 58 were waited for; matrix products, arithmetic and copies ran while one was open for 34% of the time, Pallas kernels for 0%

profile of v2, /device:TPU:0, one launch (start us, length us, event | category | flops | bytes accessed | tf_op | source)
XLA Modules:
  0.0 1400.0 jit_solution(374037726647468854)
XLA Ops:
  9.3 6.3 all-to-all-start
  18.6 22.8 %all-to-all-done = bf16[4,256,512]{2,1,0:T(8,128)(2,1)} async-done(((bf16[4,256,512]{2,1,0:T(8,128)(2,1)}), bf16[4,256,512]{2,1,0:T(8,128)(2,1)}, u32[]{:S(2)}, u32[]{:S(2)}) %all-to-all-start) | async-done | bytes 1048608 | tf_op jit(solution)/shard_map/all_to_all | solution.py:52
  46.8 47.0 %all-to-all-done.1 = bf16[8,256,512]{1,2,0:T(8,128)(2,1)} async-done(((bf16[8,256,512]{1,2,0:T(8,128)(2,1)}), bf16[8,256,512]{1,2,0:T(8,128)(2,1)}, u32[]{:S(2)}, u32[]{:S(2)}) %all-to-all-start.1) | async-done | bytes 2097184 | tf_op jit(solution)/shard_map/all_to_all | solution.py:52
  93.9 29.3 %all_to_all.110 = bf16[4,256,512]{2,1,0:T(8,128)(2,1)} all-to-all(bf16[4,256,512]{2,1,0:T(8,128)(2,1)S(1)} %broadcast_in_dim.25), channel_id=1, replica_groups=mesh['ze'=1,'zh'=2,'zl'=2,'y'=2,'x'=2,'c'=2] {'zh','zl'}, dimensions={0} | all-to-all | bytes 2097152 | tf_op jit(solution)/shard_map/all_to_all | solution.py:52
  182.4 10.2 collective-permute-done.1
  197.6 12.1 all-to-all-done.3
  251.6 6.4 collective-permute-done.15
  262.3 13.0 collective-permute-done.17
  303.2 9.2 all-to-all-done.6
  326.8 12.7 collective-permute-done.22
  346.5 5.8 all-to-all-start.8
  358.8 39.4 %all-to-all-done.8 = bf16[8,256,512]{1,2,0:T(8,128)(2,1)} async-done(((bf16[8,256,512]{1,2,0:T(8,128)(2,1)}), bf16[8,256,512]{1,2,0:T(8,128)(2,1)}, u32[]{:S(2)}, u32[]{:S(2)}) %all-to-all-start.8) | async-done | bytes 2097184 | tf_op jit(solution)/shard_map/all_to_all | solution.py:52
  436.4 6.1 multiply_convert_fusion.10
  442.5 26.1 %all-to-all-done.9 = bf16[8,256,512]{1,2,0:T(8,128)(2,1)} async-done(((bf16[8,256,512]{1,2,0:T(8,128)(2,1)}), bf16[8,256,512]{1,2,0:T(8,128)(2,1)}, u32[]{:S(2)}, u32[]{:S(2)}) %all-to-all-start.9) | async-done | bytes 2097184 | tf_op jit(solution)/shard_map/all_to_all | solution.py:52
  517.1 6.9 collective-permute-done.34
  556.9 33.6 %collective-permute-done.40 = bf16[2,96,1024]{2,1,0:T(8,128)(2,1)S(1)} collective-permute-done((bf16[2,96,1024]{2,1,0:T(8,128)(2,1)S(1)}, bf16[2,96,1024]{2,1,0:T(8,128)(2,1)S(1)}, u32[]{:S(2)}, u32[]{:S(2)}) %collective-permute-start.40) | collective-permute-done | bytes 393248 | tf_op jit(solution)/shard_map/ppermute | solution.py:19
  606.1 8.2 collective-permute-done.44
  639.3 6.3 multiply_convert_fusion.8
  645.7 5.8 convolution_convert_fusion.5
  656.7 32.3 %all-gather.29.cloned.1.call-done = bf16[2048,1024]{1,0:T(8,128)(2,1)} async-done(((bf16[2048,512]{1,0:T(8,128)(2,1)}), bf16[2048,1024]{1,0:T(8,128)(2,1)}) %all-gather.29.cloned.1.call-update) | async-done | bytes 4194320 | tf_op jit(solution)/shard_map/all_gather | solution.py:96
  697.7 6.9 add_convert_fusion.5
  704.7 5.8 multiply_convert_fusion.4
  714.4 6.8 collective-permute-done.70
  728.6 6.8 collective-permute-done.71
  758.9 8.3 collective-permute-done.62
  785.5 25.1 %collective-permute-done.66 = bf16[96,2048]{1,0:T(8,128)(2,1)S(1)} collective-permute-done((bf16[96,2048]{1,0:T(8,128)(2,1)S(1)}, bf16[96,2048]{1,0:T(8,128)(2,1)S(1)}, u32[]{:S(2)}, u32[]{:S(2)}) %collective-permute-start.66) | collective-permute-done | bytes 393248 | tf_op jit(solution)/shard_map/ppermute | solution.py:19
  811.0 13.7 collective-permute-done.67
  874.3 7.8 collective-permute-done.73
  882.1 12.0 collective-permute-done.75
  901.6 5.6 collective-permute-done.77
  917.5 5.5 convolution_convert_fusion.2
  930.5 6.5 add_convert_fusion.2
  938.4 6.1 multiply_convert_fusion.1
  944.6 5.7 multiply_convert_fusion
  950.2 26.5 %all-to-all-done.13 = bf16[8,256,512]{2,1,0:T(8,128)(2,1)} async-done(((bf16[8,256,512]{2,1,0:T(8,128)(2,1)}), bf16[8,256,512]{2,1,0:T(8,128)(2,1)}, u32[]{:S(2)}, u32[]{:S(2)}) %all-to-all-start.13) | async-done | bytes 2097184 | tf_op jit(solution)/shard_map/all_to_all | solution.py:52
  980.4 7.1 collective-permute-done.89
  1015.5 15.1 %collective-permute-done.51 = bf16[2,96,1024]{2,1,0:T(8,128)(2,1)S(1)} collective-permute-done((bf16[2,96,1024]{2,1,0:T(8,128)(2,1)S(1)}, bf16[2,96,1024]{2,1,0:T(8,128)(2,1)S(1)}, u32[]{:S(2)}, u32[]{:S(2)}) %collective-permute-start.51) | collective-permute-done | bytes 393248 | tf_op jit(solution)/shard_map/ppermute | solution.py:19
  1042.3 7.5 add_convert_fusion
  1051.0 5.8 fusion.156
  1060.3 5.7 fusion.155
  1070.8 7.6 add_add_fusion
  1084.4 6.3 collective-permute-done.83
  1123.8 20.2 %collective-permute-done.88 = bf16[2,2,48,2048]{3,2,0,1:T(8,128)(2,1)S(1)} collective-permute-done((bf16[2,2,48,2048]{3,2,0,1:T(8,128)(2,1)S(1)}, bf16[2,2,48,2048]{3,2,0,1:T(8,128)(2,1)S(1)}, u32[]{:S(2)}, u32[]{:S(2)}) %collective-permute-start.88) | collective-permute-done | bytes 786464 | tf_op jit(solution)/shard_map/ppermute | solution.py:19
  1199.9 16.3 %collective-permute-done.109 = bf16[2,192,128]{2,1,0:T(8,128)(2,1)S(1)} collective-permute-done((bf16[2,192,128]{2,1,0:T(8,128)(2,1)S(1)}, bf16[2,192,128]{2,1,0:T(8,128)(2,1)S(1)}, u32[]{:S(2)}, u32[]{:S(2)}) %collective-permute-start.109) | collective-permute-done | bytes 98336 | tf_op jit(solution)/shard_map/ppermute | solution.py:224
  1222.1 17.7 %collective-permute-done.112 = bf16[2,192,128]{2,1,0:T(8,128)(2,1)S(1)} collective-permute-done((bf16[2,192,128]{2,1,0:T(8,128)(2,1)S(1)}, bf16[2,192,128]{2,1,0:T(8,128)(2,1)S(1)}, u32[]{:S(2)}, u32[]{:S(2)}) %collective-permute-start.112) | collective-permute-done | bytes 98336 | tf_op jit(solution)/shard_map/ppermute | solution.py:224
  1257.7 44.8 %collective-permute-done.102 = bf16[1,192,128]{2,1,0:T(8,128)(2,1)S(1)} collective-permute-done((bf16[1,192,128]{2,1,0:T(8,128)(2,1)S(1)}, bf16[1,192,128]{2,1,0:T(8,128)(2,1)S(1)}, u32[]{:S(2)}, u32[]{:S(2)}) %collective-permute-start.102) | collective-permute-done | bytes 49184 | tf_op jit(solution)/shard_map/ppermute | solution.py:224
  1316.6 6.8 collective-permute-done.106
  1372.7 8.1 collective-permute-done.108
  (940 shorter events, 724.3 us)
Async XLA Ops:
  41.5 52.3 %all-to-all-start.1 = ((bf16[8,256,512]{1,2,0:T(8,128)(2,1)}), bf16[8,256,512]{1,2,0:T(8,128)(2,1)}, u32[]{:S(2)}, u32[]{:S(2)}) async-start(bf16[8,256,512]{1,2,0:T(8,128)(2,1)} %pad_maximum_fusion), calls=%async_computation.1 | async-start | bytes 4194304 | tf_op jit(solution)/shard_map/all_to_all | solution.py:52
  46.0 119.1 %all-gather.11.cloned.1.call-start = ((), (), s32[]{:S(2)}) async-start(), calls=%async_computation.32 | async-start | bytes 3145728 | tf_op jit(solution)/shard_map/all_gather | solution.py:114
  46.7 171.7 %all-gather.13.cloned.1.call-start = ((), (), s32[]{:S(2)}) async-start(), calls=%async_computation.33 | async-start | bytes 3145728 | tf_op jit(solution)/shard_map/all_gather | solution.py:114
  123.2 229.2 %all-gather.15.cloned.1.call-start = ((), (), s32[]{:S(2)}) async-start(), calls=%async_computation.34 | async-start | bytes 6291456 | tf_op jit(solution)/shard_map/all_gather | solution.py:96
  152.9 56.9 %all-to-all-start.3 = ((bf16[8,256,512]{1,2,0:T(8,128)(2,1)}), bf16[8,256,512]{1,2,0:T(8,128)(2,1)}, u32[]{:S(2)}, u32[]{:S(2)}) async-start(bf16[8,256,512]{1,2,0:T(8,128)(2,1)} %pad_maximum_fusion.1), calls=%async_computation.3 | async-start | bytes 4194304 | tf_op jit(solution)/shard_map/all_to_all | solution.py:52
  157.4 197.4 %all-gather.17.cloned.1.call-start = ((), (), s32[]{:S(2)}) async-start(), calls=%async_computation.35 | async-start | bytes 6291456 | tf_op jit(solution)/shard_map/all_gather | solution.py:96
  218.4 57.0 %all-to-all-start.4 = ((bf16[8,256,512]{1,2,0:T(8,128)(2,1)}), bf16[8,256,512]{1,2,0:T(8,128)(2,1)}, u32[]{:S(2)}, u32[]{:S(2)}) async-start(bf16[8,256,512]{1,2,0:T(8,128)(2,1)} %pad_maximum_fusion.2), calls=%async_computation.4 | async-start | bytes 4194304 | tf_op jit(solution)/shard_map/all_to_all | solution.py:52
  222.9 179.3 %all-gather.19.cloned.1.call-start = ((), (), s32[]{:S(2)}) async-start(), calls=%async_computation.36 | async-start | bytes 6291456 | tf_op jit(solution)/shard_map/all_gather | solution.py:96
  316.7 188.1 %all-gather.21.cloned.1.call-start = ((), (), s32[]{:S(2)}) async-start(), calls=%async_computation.37 | async-start | bytes 3145728 | tf_op jit(solution)/shard_map/all_gather | solution.py:96
  346.5 51.7 %all-to-all-start.8 = ((bf16[8,256,512]{1,2,0:T(8,128)(2,1)}), bf16[8,256,512]{1,2,0:T(8,128)(2,1)}, u32[]{:S(2)}, u32[]{:S(2)}) async-start(bf16[8,256,512]{1,2,0:T(8,128)(2,1)} %pad_maximum_fusion.3), calls=%async_computation.8 | async-start | bytes 4194304 | tf_op jit(solution)/shard_map/all_to_all | solution.py:52
  352.3 152.5 %all-gather.23.cloned.1.call-start = ((), (), s32[]{:S(2)}) async-start(), calls=%async_computation.38 | async-start | bytes 3145728 | tf_op jit(solution)/shard_map/all_gather | solution.py:96
  352.4 72.9 %collective-permute-start.27 = (bf16[2048,1024]{1,0:T(8,128)(2,1)}, bf16[2048,1024]{1,0:T(8,128)(2,1)}, u32[]{:S(2)}, u32[]{:S(2)}) collective-permute-start(bf16[2048,1024]{1,0:T(8,128)(2,1)} %all-gather.15.cloned.1.call-done), channel_id=1, source_target_pairs={{0,1},{1,0},{2,3},{3,2},{4,5},{5,4},{6,7},{7,6},{8,9},{9,8},{10,11... | collective-permute-start | bytes 12582920 | tf_op jit(solution)/shard_map/ppermute | solution.py:19
  354.8 182.5 %all-gather.25.cloned.1.call-start = ((), (), s32[]{:S(2)}) async-start(), calls=%async_computation.39 | async-start | bytes 6291456 | tf_op jit(solution)/shard_map/all_gather | solution.py:96
  354.8 81.6 %collective-permute-start.28 = (bf16[2048,1024]{1,0:T(8,128)(2,1)}, bf16[2048,1024]{1,0:T(8,128)(2,1)}, u32[]{:S(2)}, u32[]{:S(2)}) collective-permute-start(bf16[2048,1024]{1,0:T(8,128)(2,1)} %all-gather.17.cloned.1.call-done), channel_id=1, source_target_pairs={{0,1},{1,0},{2,3},{3,2},{4,5},{5,4},{6,7},{7,6},{8,9},{9,8},{10,11... | collective-permute-start | bytes 12582920 | tf_op jit(solution)/shard_map/ppermute | solution.py:19
  355.4 46.9 %collective-permute-start.23 = (bf16[96,2048]{1,0:T(8,128)(2,1)S(1)}, bf16[96,2048]{1,0:T(8,128)(2,1)}, u32[]{:S(2)}, u32[]{:S(2)}) collective-permute-start(bf16[96,2048]{1,0:T(8,128)(2,1)S(1)} %get-tuple-element.129), channel_id=1, source_target_pairs={{0,4},{4,0},{1,5},{5,1},{2,6},{6,2},{3,7},{7,3},{8,12},{12,8},{9,1... | collective-permute-start | bytes 1179656 | tf_op jit(solution)/shard_map/ppermute | solution.py:19
  357.3 46.6 %collective-permute-start.24 = (bf16[96,2048]{1,0:T(8,128)(2,1)S(1)}, bf16[96,2048]{1,0:T(8,128)(2,1)}, u32[]{:S(2)}, u32[]{:S(2)}) collective-permute-start(bf16[96,2048]{1,0:T(8,128)(2,1)S(1)} %get-tuple-element.129), channel_id=1, source_target_pairs={{0,8},{8,0},{1,9},{9,1},{2,10},{10,2},{3,11},{11,3},{4,12},{12,4},... | collective-permute-start | bytes 1179656 | tf_op jit(solution)/shard_map/ppermute | solution.py:19
  402.2 70.3 %collective-permute-start.29 = (bf16[2048,1024]{1,0:T(8,128)(2,1)}, bf16[2048,1024]{1,0:T(8,128)(2,1)}, u32[]{:S(2)}, u32[]{:S(2)}) collective-permute-start(bf16[2048,1024]{1,0:T(8,128)(2,1)} %all-gather.19.cloned.1.call-done), channel_id=1, source_target_pairs={{0,1},{1,0},{2,3},{3,2},{4,5},{5,4},{6,7},{7,6},{8,9},{9,8},{10,11... | collective-permute-start | bytes 12582920 | tf_op jit(solution)/shard_map/ppermute | solution.py:19
  415.8 52.8 %all-to-all-start.9 = ((bf16[8,256,512]{1,2,0:T(8,128)(2,1)}), bf16[8,256,512]{1,2,0:T(8,128)(2,1)}, u32[]{:S(2)}, u32[]{:S(2)}) async-start(bf16[8,256,512]{1,2,0:T(8,128)(2,1)} %pad_maximum_fusion.4), calls=%async_computation.9 | async-start | bytes 4194304 | tf_op jit(solution)/shard_map/all_to_all | solution.py:52
  420.2 127.7 %all-gather.27.cloned.1.call-start = ((), (), s32[]{:S(2)}) async-start(), calls=%async_computation.40 | async-start | bytes 6291456 | tf_op jit(solution)/shard_map/all_gather | solution.py:96
  504.8 46.0 %collective-permute-start.39 = (bf16[2048,512]{1,0:T(8,128)(2,1)}, bf16[2048,512]{1,0:T(8,128)(2,1)}, u32[]{:S(2)}, u32[]{:S(2)}) collective-permute-start(bf16[2048,512]{1,0:T(8,128)(2,1)} %all-gather.23.cloned.1.call-done), channel_id=1, source_target_pairs={{0,1},{1,0},{2,3},{3,2},{4,5},{5,4},{6,7},{7,6},{8,9},{9,8},{10,11... | collective-permute-start | bytes 6291464 | tf_op jit(solution)/shard_map/ppermute | solution.py:19
  537.3 98.0 %collective-permute-start.48 = (bf16[2048,1024]{1,0:T(8,128)(2,1)}, bf16[2048,1024]{1,0:T(8,128)(2,1)}, u32[]{:S(2)}, u32[]{:S(2)}) collective-permute-start(bf16[2048,1024]{1,0:T(8,128)(2,1)} %all-gather.25.cloned.1.call-done), channel_id=1, source_target_pairs={{0,1},{1,0},{2,3},{3,2},{4,5},{5,4},{6,7},{7,6},{8,9},{9,8},{10,11... | collective-permute-start | bytes 12582920 | tf_op jit(solution)/shard_map/ppermute | solution.py:19
  541.7 89.3 %all-to-all-start.10 = ((bf16[8,256,512]{1,2,0:T(8,128)(2,1)}), bf16[8,256,512]{1,2,0:T(8,128)(2,1)}, u32[]{:S(2)}, u32[]{:S(2)}) async-start(bf16[8,256,512]{1,2,0:T(8,128)(2,1)} %pad_maximum_fusion.5), calls=%async_computation.10 | async-start | bytes 4194304 | tf_op jit(solution)/shard_map/all_to_all | solution.py:52
  546.1 143.0 %all-gather.29.cloned.1.call-start = ((), (), s32[]{:S(2)}) async-start(), calls=%async_computation.41 | async-start | bytes 6291456 | tf_op jit(solution)/shard_map/all_gather | solution.py:96
  547.9 91.4 %collective-permute-start.49 = (bf16[2048,1024]{1,0:T(8,128)(2,1)}, bf16[2048,1024]{1,0:T(8,128)(2,1)}, u32[]{:S(2)}, u32[]{:S(2)}) collective-permute-start(bf16[2048,1024]{1,0:T(8,128)(2,1)} %all-gather.27.cloned.1.call-done), channel_id=1, source_target_pairs={{0,1},{1,0},{2,3},{3,2},{4,5},{5,4},{6,7},{7,6},{8,9},{9,8},{10,11... | collective-permute-start | bytes 12582920 | tf_op jit(solution)/shard_map/ppermute | solution.py:19
  634.9 142.4 %reduce-scatter.11.cloned.1.call-start = ((), (), s32[]{:S(2)}) async-start(), calls=%async_computation.42 | async-start | bytes 6291456 | tf_op jit(solution)/shard_map/reduce_scatter | solution.py:105
  651.5 45.3 %collective-permute-start.61 = (bf16[2048,1024]{1,0:T(8,128)(2,1)}, bf16[2048,1024]{1,0:T(8,128)(2,1)}, u32[]{:S(2)}, u32[]{:S(2)}) collective-permute-start(bf16[2048,1024]{1,0:T(8,128)(2,1)} %convolution_convert_fusion.5), channel_id=1, source_target_pairs={{0,1},{1,0},{2,3},{3,2},{4,5},{5,4},{6,7},{7,6},{8,9},{9,8},{10,11... | collective-permute-start | bytes 12582920 | tf_op jit(solution)/shard_map/ppermute | solution.py:19
  704.7 144.9 %reduce-scatter.13.cloned.1.call-start = ((), (), s32[]{:S(2)}) async-start(), calls=%async_computation.43 | async-start | bytes 6291456 | tf_op jit(solution)/shard_map/reduce_scatter | solution.py:105
  725.7 197.3 %reduce-scatter.15.cloned.1.call-start = ((), (), s32[]{:S(2)}) async-start(), calls=%async_computation.44 | async-start | bytes 6291456 | tf_op jit(solution)/shard_map/reduce_scatter | solution.py:105
  777.2 72.4 %all-to-all-start.11 = ((bf16[8,256,512]{2,1,0:T(8,128)(2,1)}), bf16[8,256,512]{2,1,0:T(8,128)(2,1)}, u32[]{:S(2)}, u32[]{:S(2)}) async-start(bf16[8,256,512]{2,1,0:T(8,128)(2,1)} %bitcast.665), calls=%async_computation.12 | async-start | bytes 4194304 | tf_op jit(solution)/shard_map/all_to_all | solution.py:52
  849.6 67.9 %all-to-all-start.12 = ((bf16[8,256,512]{2,1,0:T(8,128)(2,1)}), bf16[8,256,512]{2,1,0:T(8,128)(2,1)}, u32[]{:S(2)}, u32[]{:S(2)}) async-start(bf16[8,256,512]{2,1,0:T(8,128)(2,1)} %bitcast.664), calls=%async_computation.14 | async-start | bytes 4194304 | tf_op jit(solution)/shard_map/all_to_all | solution.py:52
  854.4 143.2 %reduce-scatter.17.cloned.1.call-start = ((), (), s32[]{:S(2)}) async-start(), calls=%async_computation.45 | async-start | bytes 3145728 | tf_op jit(solution)/shard_map/reduce_scatter | solution.py:105
  858.9 178.6 %reduce-scatter.19.cloned.1.call-start = ((), (), s32[]{:S(2)}) async-start(), calls=%async_computation.46 | async-start | bytes 3145728 | tf_op jit(solution)/shard_map/reduce_scatter | solution.py:105
  862.6 49.9 %collective-permute-start.81 = (bf16[2048,512]{1,0:T(8,128)(2,1)S(1)}, bf16[2048,512]{1,0:T(8,128)(2,1)S(1)}, u32[]{:S(2)}, u32[]{:S(2)}) collective-permute-start(bf16[2048,512]{1,0:T(8,128)(2,1)S(1)} %convolution_convert_fusion.8), channel_id=1, source_target_pairs={{0,1},{1,0},{2,3},{3,2},{4,5},{5,4},{6,7},{7,6},{8,9},{9,8},{10,11... | collective-permute-start | bytes 6291464 | tf_op jit(solution)/shard_map/ppermute | solution.py:19
  923.0 53.7 %all-to-all-start.13 = ((bf16[8,256,512]{2,1,0:T(8,128)(2,1)}), bf16[8,256,512]{2,1,0:T(8,128)(2,1)}, u32[]{:S(2)}, u32[]{:S(2)}) async-start(bf16[8,256,512]{2,1,0:T(8,128)(2,1)} %bitcast.662), calls=%async_computation.16 | async-start | bytes 4194304 | tf_op jit(solution)/shard_map/all_to_all | solution.py:52
  927.5 168.3 %reduce-scatter.21.cloned.1.call-start = ((), (), s32[]{:S(2)}) async-start(), calls=%async_computation.47 | async-start | bytes 6291456 | tf_op jit(solution)/shard_map/reduce_scatter | solution.py:105
  937.0 238.5 %reduce-scatter.23.cloned.1.call-start = ((), (), s32[]{:S(2)}) async-start(), calls=%async_computation.48 | async-start | bytes 6291456 | tf_op jit(solution)/shard_map/reduce_scatter | solution.py:105
  1034.4 47.8 %collective-permute-start.52 = (bf16[96,1024]{1,0:T(8,128)(2,1)}, bf16[96,1024]{1,0:T(8,128)(2,1)}, u32[]{:S(2)}, u32[]{:S(2)}) collective-permute-start(bf16[96,1024]{1,0:T(8,128)(2,1)} %get-tuple-element.158), channel_id=1, source_target_pairs={{0,4},{4,0},{1,5},{5,1},{2,6},{6,2},{3,7},{7,3},{8,12},{12,8},{9,1... | collective-permute-start | bytes 589832 | tf_op jit(solution)/shard_map/ppermute | solution.py:19
  1035.3 47.0 %collective-permute-start.54 = (bf16[96,1024]{1,0:T(8,128)(2,1)}, bf16[96,1024]{1,0:T(8,128)(2,1)}, u32[]{:S(2)}, u32[]{:S(2)}) collective-permute-start(bf16[96,1024]{1,0:T(8,128)(2,1)} %get-tuple-element.159), channel_id=1, source_target_pairs={{0,8},{8,0},{1,9},{9,1},{2,10},{10,2},{3,11},{11,3},{4,12},{12,4},... | collective-permute-start | bytes 589832 | tf_op jit(solution)/shard_map/ppermute | solution.py:19
  1042.2 202.1 %reduce-scatter.29.cloned.1.call-start = ((), (), s32[]{:S(2)}) async-start(), calls=%async_computation.51 | async-start | bytes 6291456 | tf_op jit(solution)/shard_map/reduce_scatter | solution.py:105
  1095.9 51.7 %all-to-all-start.16 = ((bf16[8,256,512]{2,1,0:T(8,128)(2,1)}), bf16[8,256,512]{2,1,0:T(8,128)(2,1)}, u32[]{:S(2)}, u32[]{:S(2)}) async-start(bf16[8,256,512]{2,1,0:T(8,128)(2,1)} %bitcast.663), calls=%async_computation.22 | async-start | bytes 4194304 | tf_op jit(solution)/shard_map/all_to_all | solution.py:52
  1100.3 228.4 %reduce-scatter.27.cloned.1.call-start = ((), (), s32[]{:S(2)}) async-start(), calls=%async_computation.50 | async-start | bytes 3145728 | tf_op jit(solution)/shard_map/reduce_scatter | solution.py:119
  1175.5 65.0 %all-to-all-start.17 = ((bf16[8,256,512]{2,1,0:T(8,128)(2,1)}), bf16[8,256,512]{2,1,0:T(8,128)(2,1)}, u32[]{:S(2)}, u32[]{:S(2)}) async-start(bf16[8,256,512]{2,1,0:T(8,128)(2,1)} %bitcast.660), calls=%async_computation.24 | async-start | bytes 4194304 | tf_op jit(solution)/shard_map/all_to_all | solution.py:52
  1220.1 86.7 %collective-permute-start.115 = (bf16[2,192,128]{2,1,0:T(8,128)(2,1)S(1)}, bf16[2,192,128]{2,1,0:T(8,128)(2,1)S(1)}, u32[]{:S(2)}, u32[]{:S(2)}) collective-permute-start(bf16[2,192,128]{2,1,0:T(8,128)(2,1)S(1)} %get-tuple-element.175), channel_id=1, source_target_pairs={{0,28},{4,24},{8,20},{12,16},{16,12},{20,8},{24,4},{28,0},{1,29},{... | collective-permute-start | bytes 294920 | tf_op jit(solution)/shard_map/ppermute | solution.py:224
  1244.3 84.3 %all-to-all-start.19 = ((bf16[8,256,512]{2,1,0:T(8,128)(2,1)}), bf16[8,256,512]{2,1,0:T(8,128)(2,1)}, u32[]{:S(2)}, u32[]{:S(2)}) async-start(bf16[8,256,512]{2,1,0:T(8,128)(2,1)} %bitcast.658), calls=%async_computation.29 | async-start | bytes 4194304 | tf_op jit(solution)/shard_map/all_to_all | solution.py:52
  1249.8 110.4 %reduce-scatter.25.cloned.1.call-start = ((), (), s32[]{:S(2)}) async-start(), calls=%async_computation.49 | async-start | bytes 3145728 | tf_op jit(solution)/shard_map/reduce_scatter | solution.py:119
  1249.8 52.7 %collective-permute-start.102 = (bf16[1,192,128]{2,1,0:T(8,128)(2,1)S(1)}, bf16[1,192,128]{2,1,0:T(8,128)(2,1)S(1)}, u32[]{:S(2)}, u32[]{:S(2)}) collective-permute-start(bf16[1,192,128]{2,1,0:T(8,128)(2,1)S(1)} %get-tuple-element.195), channel_id=1, source_target_pairs={{0,20},{4,16},{8,28},{12,24},{16,4},{20,0},{24,12},{28,8},{1,21},{... | collective-permute-start | bytes 147464 | tf_op jit(solution)/shard_map/ppermute | solution.py:224
  1253.7 48.8 %collective-permute-start.103 = (bf16[1,192,128]{2,1,0:T(8,128)(2,1)S(1)}, bf16[1,192,128]{2,1,0:T(8,128)(2,1)S(1)}, u32[]{:S(2)}, u32[]{:S(2)}) collective-permute-start(bf16[1,192,128]{2,1,0:T(8,128)(2,1)S(1)} %get-tuple-element.194), channel_id=1, source_target_pairs={{0,24},{4,28},{8,16},{12,20},{16,8},{20,12},{24,0},{28,4},{1,25},{... | collective-permute-start | bytes 147464 | tf_op jit(solution)/shard_map/ppermute | solution.py:224
  1255.2 47.3 %collective-permute-start.104 = (bf16[1,192,128]{2,1,0:T(8,128)(2,1)S(1)}, bf16[1,192,128]{2,1,0:T(8,128)(2,1)S(1)}, u32[]{:S(2)}, u32[]{:S(2)}) collective-permute-start(bf16[1,192,128]{2,1,0:T(8,128)(2,1)S(1)} %get-tuple-element.193), channel_id=1, source_target_pairs={{0,28},{4,24},{8,20},{12,16},{16,12},{20,8},{24,4},{28,0},{1,29},{... | collective-permute-start | bytes 147464 | tf_op jit(solution)/shard_map/ppermute | solution.py:224
  (256 other events, 3937.2 us)
Sparse Core Ops, SparseCore 0:
  48.4 45.5 all-gather.10
  123.3 46.3 all-gather.12
  171.8 59.1 all-gather.14
  232.9 56.7 all-gather.16
  291.7 65.1 all-gather.18
  358.9 33.0 all-gather.20
  394.1 33.0 all-gather.22
  429.3 56.7 all-gather.24
  488.2 59.6 all-gather.26
  635.0 53.9 all-gather.28
  704.8 54.4 reduce-scatter.10
  761.5 54.3 reduce-scatter.12
  818.2 54.2 reduce-scatter.14
  875.2 31.8 reduce-scatter.16
  923.1 29.6 reduce-scatter.18
  955.1 54.3 reduce-scatter.20
  1011.6 54.2 reduce-scatter.22
  1068.2 65.9 reduce-scatter.28
  1165.3 57.1 reduce-scatter.26
  1311.2 30.0 reduce-scatter.24

commit v3 on v2

--- a/solution.py
+++ b/solution.py
@@ -1,6 +1,7 @@
 import jax
 import jax.numpy as jnp
 from jax import lax
+from jax.experimental import pallas as pl
 from jax.sharding import Mesh
 from jax.sharding import PartitionSpec as P
 
@@ -23,6 +24,25 @@
     return lax.optimization_barrier((value, earlier))[0]
 
 
+def held(value, *earlier):
+    earlier = jax.tree.leaves(earlier)
+    if not earlier:
+        return value
+    anywhere = pl.BlockSpec(memory_space=pl.ANY)
+
+    def body(*refs):
+        pass
+
+    return pl.pallas_call(
+        body,
+        in_specs=[anywhere] * (1 + len(earlier)),
+        out_specs=anywhere,
+        out_shape=jax.ShapeDtypeStruct(value.shape, value.dtype),
+        input_output_aliases={0: 0},
+        cost_estimate=pl.CostEstimate(flops=0, bytes_accessed=0, transcendentals=0),
+    )(value, *earlier)
+
+
 def dot(a, b):
     return jnp.dot(a, b, preferred_element_type=F32)
 
@@ -68,8 +88,44 @@
     return lax.psum_scatter(value.astype(BF), "ze", scatter_dimension=0, tiled=True).astype(F32)
 
 
+def cut(w):
+    r, k = w.shape[0], w.shape[1] // 4
+
+    def body(w_ref, out_ref):
+        out_ref[0] = w_ref[...]
+
+    return pl.pallas_call(
+        body,
+        grid=(8,),
+        in_specs=[pl.BlockSpec((r, k), lambda i: (0, i % 4))],
+        out_specs=pl.BlockSpec((1, r, k), lambda i: (i, 0, 0)),
+        out_shape=jax.ShapeDtypeStruct((8, r, k), w.dtype),
+        cost_estimate=pl.CostEstimate(flops=0, bytes_accessed=24 * r * k, transcendentals=0),
+    )(w)
+
+
+def fold(t):
+    r, k = t.shape[1:]
+
+    def body(a_ref, b_ref, out_ref):
+        out_ref[...] = a_ref[0].astype(F32) + b_ref[0].astype(F32)
+
+    return pl.pallas_call(
+        body,
+        grid=(4,),
+        in_specs=[
+            pl.BlockSpec((1, r, k), lambda i: (i, 0, 0)),
+            pl.BlockSpec((1, r, k), lambda i: (i + 4, 0, 0)),
+        ],
+        out_specs=pl.BlockSpec((r, k), lambda i: (0, i)),
+        out_shape=jax.ShapeDtypeStruct((r, 4 * k), F32),
+        cost_estimate=pl.CostEstimate(flops=0, bytes_accessed=32 * r * k, transcendentals=0),
+    )(t, t)
+
+
 class Place:
     def __init__(self, width):
+        self.zh = lax.axis_index("zh")
         self.zl = lax.axis_index("zl")
         self.x = lax.axis_index("x")
         self.y = lax.axis_index("y")
@@ -90,8 +146,7 @@
 
     def gather(self, w):
         r, k = w.shape
-        w = w.reshape(r, 4, k // 4).transpose(1, 0, 2)
-        w = self.ordered(jnp.concatenate([w, w]), GROUP)
+        w = self.ordered(cut(w), GROUP)
         w = over_ze(w.reshape(8 * r, k // 4))
         own = lax.all_gather(w, "x", axis=1, tiled=True)
         return own, swap(own, "c")
@@ -104,13 +159,13 @@
         part = (dot_tn(left, own) + got.astype(F32)).astype(BF)
         t = lax.psum_scatter(part, "x", scatter_dimension=1, tiled=True)
         t = total_ze(t).astype(BF).reshape(8, self.rows, -1)
-        t = self.ordered(t, GROUP).astype(F32)
-        t = t[:4] + t[4:]
-        return part, t.transpose(1, 0, 2).reshape(self.rows, -1)
-
-    def gather_rows(self, w):
+        return part, fold(self.ordered(t, GROUP))
+
+    def gather_rows(self, w, swapped=False):
         a = self.ordered(copies(w, 4), ("zh", "zl"))
         a = over_ze(a)
+        if swapped:
+            return in_order(self.y, a, swap(a, "y"), 1).reshape(-1, w.shape[1])
         return lax.all_gather(a, "y", axis=1, tiled=True).reshape(-1, w.shape[1])
 
     def scatter_rows(self, left, right):
@@ -149,8 +204,8 @@
     def spread_tp(self, v, mb):
         d = v.shape[1]
         v = v.reshape(mb, 1, -1, d)
-        pair = in_order(self.c, v, swap(v, "c"), 1)
-        full = in_order(self.x, pair, swap(pair, "x"), 1)
+        pair = in_order(self.x, v, swap(v, "x"), 1)[:, :, None]
+        full = in_order(self.c, pair, swap(pair, "c"), 2)
         return full.reshape(mb, -1, d)
 
     def collect_tp(self, part, mb):
@@ -162,25 +217,32 @@
         own = own + swap(half(mine, 1 - self.x, 1).astype(BF), "x").astype(F32)
         return own.reshape(t // 4, d)
 
-    def flips(self, v, axis):
-        v = jnp.where(self.zl == 1, jnp.flip(v, axis), v)
-        return jnp.where(self.y == 1, jnp.flip(v, axis + 1), v)
+    def trade_half(self, v, bit, axis, name):
+        return jnp.stack([half(v, bit, axis), swap(half(v, 1 - bit, axis), name)])
 
     def memory_in(self, m):
         mb, t, k = m.shape
-        v = m.reshape(mb, 4, t // 4, 4, k // 4).transpose(3, 1, 0, 2, 4)
-        v = trade(v.reshape(16, mb * t // 4, k // 4), UNIT)
-        v = self.flips(v.reshape(2, 2, 2, 2, mb * t // 4, k // 4), 0)
+        v = m.reshape(mb, 2, 2, t // 4, 2, 2, k // 4).transpose(4, 5, 1, 2, 0, 3, 6)
+        v = self.trade_half(v, self.c, 3, "c")
+        v = self.trade_half(v, self.x, 3, "x")
+        v = jnp.where(self.x == 1, jnp.flip(v, 0), v)
+        v = self.trade_half(v, self.y, 3, "y")
+        v = self.trade_half(v, self.zl, 3, "zl")
+        v = v.reshape(2, 2, 2, 2, mb * t // 4, k // 4)
         v = v.transpose(3, 0, 1, 4, 2, 5).reshape(2, mb * t, k // 2)
-        return jnp.where(self.c == 0, v[0], v[1]), jnp.where(self.c == 0, v[1], v[0])
+        return v[0], v[1]
 
     def memory_out(self, own, far, mb):
         t, k = own.shape[0], own.shape[1] * 2
-        v = in_order(self.c, own.astype(BF)[None], far.astype(BF)[None], 0)
-        v = v.reshape(2, 2, 2, t // 4, 2, k // 4).transpose(1, 2, 4, 0, 3, 5)
-        v = self.flips(v, 0).reshape(16, t // 4, k // 4)
-        v = trade(v, UNIT).reshape(4, 4, mb, t // (4 * mb), k // 4)
-        return v.transpose(2, 1, 3, 0, 4).reshape(mb, t // mb, k).astype(F32)
+        v = jnp.stack([own, far]).astype(BF).reshape(2, 2, 2, t // 4, 2, k // 4)
+        v = v.transpose(0, 4, 1, 2, 3, 5)
+        v = in_order(self.zl, v[:, :, :1], swap(v[:, :, 1:], "zl"), 2)
+        v = in_order(self.y, v[:, :, :, :1], swap(v[:, :, :, 1:], "y"), 3)
+        v = in_order(self.c, v[:1][None], swap(v[1:], "c")[None], 0)
+        v = v[:, 0]
+        v = in_order(self.x, half(v, self.x, 1)[None], swap(half(v, 1 - self.x, 1), "x")[None], 0)
+        v = v.reshape(2, 2, 2, 2, mb, t // (4 * mb), k // 4)
+        return v.transpose(4, 0, 1, 5, 2, 3, 6).reshape(mb, t // mb, k).astype(F32)
 
 
 def rms(v, g):
@@ -270,12 +332,10 @@
     cache = to_pairs(jnp.stack([cache_keys, cache_values], 0))
     keys, values = over_ze(cache[0]), over_ze(cache[1])
     g1 = at.gather(gate_first)
-    wo = at.gather_rows(output_proj)
-    at.first = [cache]
     u1 = at.gather(up_first)
+    wo = at.gather_rows(output_proj, True)
     n1 = rms(stream.astype(F32).reshape(mb * tok, width), gains[0]).astype(BF)
     q = to_pairs(dot(n1, wq).astype(BF).reshape(1, mb, tok, -1))[0]
-    q = after(q, wo)
     at.first = [q]
     d1 = at.gather(down_first)
 
@@ -315,9 +375,9 @@
     x2, kept1 = ffn(x1, gains[1], g1, u1, d1, ())
     at.first = [kept1[0]]
     u2 = at.gather(up_second)
-    at.first = [kept1[3][1]]
     d2 = at.gather(down_second)
 
+    x2 = held(x2, at.line[9])
     mem = at.memory_in(memory)
     n3 = at.spread(rms(x2, gains[2]).astype(BF))
     za = [dot(n3, w) for w in mi]
@@ -391,13 +451,13 @@
     p = jnp.exp(s - lse)
     ds = (p * (dot_nt(do, values) - delta)).astype(BF)
     dq = after((dot(ds, keys) * scaling).astype(BF)[None], (part_w, zline[16]))
-    dq = from_pairs(dq, mb, tok)
+    dq = from_pairs(held(dq, zline[16]), mb, tok)
     dk = total_ze(dot_tn(ds, q) * scaling).astype(BF)
     dv = total_ze(dot_tn(p.astype(BF), do)).astype(BF)
-    dkv = from_pairs(after(jnp.stack([dk, dv]), dq), mb, tok).astype(F32)
+    dkv = from_pairs(held(jnp.stack([dk, dv]), dq), mb, tok).astype(F32)
     keys_grad, values_grad = dkv[0], dkv[1]
     dq = dq.reshape(mb * tok, -1)
-    dn1 = at.collect_tp(dot_nt(dq, wq), mb)
+    dn1 = at.collect_tp(held(dot_nt(dq, wq), zline[17]), mb)
     _, query_grad = at.scatter_rows(n1, dq)
     back, gain1 = rms_back(r0, gains[0], dn1)
     stream_grad = at.spread_tp((dx1 + back).astype(BF), mb).astype(F32)

time: 1410 us -> 1380 us (0.979)
  Pallas kernels: 0 us -> 74 us
  local copies, waits for them, and re-layouts: 151 us -> 98.8 us
  blocking collectives: 29.3 us -> 0 us
  other arithmetic: 107 us -> 78.2 us
  starting transfers between devices: 265 us -> 289 us
  waiting for transfers between devices: 588 us -> 573 us
    pallas_call x0 -> x20, Pallas kernels: none -> 74 us  [the longest x8 44.3 us: cut(): pl.pallas_call(body, grid=(8,), in_specs=[pl.BlockSpec((r, k), lambda i:...]
    all_to_all x21 -> x20, waiting for transfers between devices: 188 us -> 114 us  [trade(): return lax.all_to_all(value, axes, split_axis=0, concat_axis=0, tiled=True)]
    ppermute x21, waiting for transfers between devices: 11.5 us -> 67.5 us  [exchange(): lax.ppermute(block, GROUP, [(i, i ^ k) for i in range(8)])]
    ppermute x79 -> x88, waiting for transfers between devices: 255 us -> 298 us  [swap(): return lax.ppermute(value, axis, [(0, 1), (1, 0)])]
    ppermute x21, waiting for transfers between devices: 99 us -> 57.4 us  [from_pairs(): got.append(lax.ppermute(v[:, k], GROUP, [(i, i ^ k) for i in range(8)]))]
    all_to_all x1 -> x0, blocking collectives: 29.3 us -> none  [trade(): return lax.all_to_all(value, axes, split_axis=0, concat_axis=0, tiled=True)]
    all_to_all x8 -> x0, local copies, waits for them, and re-layouts: 28.1 us -> none  [trade(): return lax.all_to_all(value, axes, split_axis=0, concat_axis=0, tiled=True)]
    concatenate x8 -> x0, other arithmetic: 18.9 us -> none  [gather(): w = self.ordered(jnp.concatenate([w, w]), GROUP)]
  transfers between devices with their start and end apart: 162 -> 169, of which waited for: 58 -> 73; matrix products, arithmetic and copies ran while one was open for 34% -> 28% of each run, Pallas kernels for 0% -> 5%
where the time goes in v3:
time: 1380 us; the launch traced here: 1360 us
  waiting for transfers between devices  573 us (42%)
  starting transfers between devices  289 us (21%)
  matrix products  234 us (17%)
  local copies, waits for them, and re-layouts  98.8 us (7%)
  other arithmetic  78.2 us (6%)
  Pallas kernels  74 us (5%)
  between operations  17.2 us (1%)
    ppermute x88, waiting for transfers between devices, swap(): return lax.ppermute(value, axis, [(0, 1), (1, 0)])  298 us
    all_to_all x20, waiting for transfers between devices, trade(): return lax.all_to_all(value, axes, split_axis=0, concat_axis=0, tiled=True)  114 us
    ppermute x88, starting transfers between devices, swap(): return lax.ppermute(value, axis, [(0, 1), (1, 0)])  93.8 us
    all_to_all x20, starting transfers between devices, trade(): return lax.all_to_all(value, axes, split_axis=0, concat_axis=0, tiled=True)  93.1 us
    dot_general x20, matrix products, dot(): return jnp.dot(a, b, preferred_element_type=F32)  86.2 us
    dot_general x20, matrix products, dot_tn(): lax.dot_general(a, b, (((0,), (0,)), ((), ())), preferred_element_type=F32)  80.7 us
    ppermute x21, waiting for transfers between devices, exchange(): lax.ppermute(block, GROUP, [(i, i ^ k) for i in range(8)])  67.5 us
    dot_general x20, matrix products, dot_nt(): lax.dot_general(a, b, (((1,), (1,)), ((), ())), preferred_element_type=F32)  67.5 us
  transfers between devices with their start and end apart: 169, of which 73 were waited for; matrix products, arithmetic and copies ran while one was open for 28% of the time, Pallas kernels for 5%

profile of v3, /device:TPU:0, one launch (start us, length us, event | category | flops | bytes accessed | tf_op | source)
XLA Modules:
  0.0 1364.1 jit_solution(4270094082622089285)
XLA Ops:
  9.3 6.3 all-to-all-start
  21.3 20.1 %all-to-all-done = bf16[4,256,512]{2,1,0:T(8,128)(2,1)S(1)} async-done(((bf16[4,256,512]{2,1,0:T(8,128)(2,1)}), bf16[4,256,512]{2,1,0:T(8,128)(2,1)S(1)}, u32[]{:S(2)}, u32[]{:S(2)}) %all-to-all-start) | async-done | bytes 1048608 | tf_op jit(solution)/shard_map/all_to_all | solution.py:72
  53.1 41.4 %all-to-all-done.1 = bf16[8,256,512]{2,1,0:T(8,128)(2,1)} async-done(((bf16[8,256,512]{2,1,0:T(8,128)(2,1)}), bf16[8,256,512]{2,1,0:T(8,128)(2,1)}, u32[]{:S(2)}, u32[]{:S(2)}) %all-to-all-start.1) | async-done | bytes 2097184 | tf_op jit(solution)/shard_map/all_to_all | solution.py:72
  128.5 8.2 collective-permute-done.8
  144.0 15.1 %collective-permute-done.10 = bf16[2,192,128]{2,1,0:T(8,128)(2,1)} collective-permute-done((bf16[2,192,128]{2,1,0:T(8,128)(2,1)}, bf16[2,192,128]{2,1,0:T(8,128)(2,1)}, u32[]{:S(2)}, u32[]{:S(2)}) %collective-permute-start.10) | collective-permute-done | bytes 98336 | tf_op jit(solution)/shard_map/ppermute | solution.py:270
  190.9 7.5 collective-permute-done.3
  234.7 6.3 collective-permute-done.15
  245.7 13.0 collective-permute-done.17
  272.7 20.3 %collective-permute-done.21 = bf16[4,256,512]{2,1,0:T(8,128)(2,1)} collective-permute-done((bf16[4,256,512]{2,1,0:T(8,128)(2,1)}, bf16[4,256,512]{2,1,0:T(8,128)(2,1)}, u32[]{:S(2)}, u32[]{:S(2)}) %collective-permute-start.21) | collective-permute-done | bytes 1048608 | tf_op jit(solution)/shard_map/ppermute | solution.py:20
  319.6 7.5 collective-permute-done.23
  345.0 24.2 %collective-permute-done.24 = bf16[96,2048]{1,0:T(8,128)(2,1)S(1)} collective-permute-done((bf16[96,2048]{1,0:T(8,128)(2,1)S(1)}, bf16[96,2048]{1,0:T(8,128)(2,1)S(1)}, u32[]{:S(2)}, u32[]{:S(2)}) %collective-permute-start.24) | collective-permute-done | bytes 393248 | tf_op jit(solution)/shard_map/ppermute | solution.py:20
  372.7 12.2 collective-permute-done.25
  430.4 15.3 %all-to-all-done.8 = bf16[8,256,512]{2,1,0:T(8,128)(2,1)} async-done(((bf16[8,256,512]{2,1,0:T(8,128)(2,1)}), bf16[8,256,512]{2,1,0:T(8,128)(2,1)}, u32[]{:S(2)}, u32[]{:S(2)}) %all-to-all-start.8) | async-done | bytes 2097184 | tf_op jit(solution)/shard_map/all_to_all | solution.py:72
  454.7 5.8 multiply_convert_fusion.10
  460.6 8.8 all-gather.26.cloned.1.call-start
  515.6 9.7 collective-permute-done.39
  548.5 8.5 collective-permute-done.45
  568.0 8.7 collective-permute-done.49
  596.4 6.4 multiply_convert_fusion.8
  613.7 32.4 %all-gather.26.cloned.1.call-done = bf16[2048,1024]{1,0:T(8,128)(2,1)} async-done(((bf16[2048,512]{1,0:T(8,128)(2,1)}), bf16[2048,1024]{1,0:T(8,128)(2,1)}) %all-gather.26.cloned.1.call-update) | async-done | bytes 4194320 | tf_op jit(solution)/shard_map/all_gather | solution.py:151
  654.8 6.9 add_convert_fusion.5
  661.8 6.7 multiply_convert_fusion.4
  672.3 6.8 collective-permute-done.75
  753.1 22.1 %collective-permute-done.71 = bf16[96,2048]{1,0:T(8,128)(2,1)S(1)} collective-permute-done((bf16[96,2048]{1,0:T(8,128)(2,1)S(1)}, bf16[96,2048]{1,0:T(8,128)(2,1)S(1)}, u32[]{:S(2)}, u32[]{:S(2)}) %collective-permute-start.71) | collective-permute-done | bytes 393248 | tf_op jit(solution)/shard_map/ppermute | solution.py:20
  775.6 14.2 %collective-permute-done.72 = bf16[96,2048]{1,0:T(8,128)(2,1)S(1)} collective-permute-done((bf16[96,2048]{1,0:T(8,128)(2,1)S(1)}, bf16[96,2048]{1,0:T(8,128)(2,1)S(1)}, u32[]{:S(2)}, u32[]{:S(2)}) %collective-permute-start.72) | collective-permute-done | bytes 393248 | tf_op jit(solution)/shard_map/ppermute | solution.py:20
  839.3 7.9 collective-permute-done.78
  847.2 12.1 collective-permute-done.80
  866.2 5.8 collective-permute-done.82
  883.6 6.1 convolution_convert_fusion.2
  897.1 6.6 add_convert_fusion.2
  904.0 6.6 multiply_convert_fusion.1
  910.6 5.9 multiply_convert_fusion
  916.5 26.9 %all-to-all-done.12.a_ref.b_ref = bf16[8,256,512]{2,1,0:T(8,128)(2,1)} async-done(((bf16[8,256,512]{2,1,0:T(8,128)(2,1)}), bf16[8,256,512]{2,1,0:T(8,128)(2,1)}, u32[]{:S(2)}, u32[]{:S(2)}) %all-to-all-start.12) | async-done | bytes 2097184 | tf_op jit(solution)/shard_map/all_to_all | solution.py:72
  947.1 7.1 collective-permute-done.94
  970.5 6.8 add_convert_fusion
  979.8 5.8 fusion.154
  1014.7 10.7 collective-permute-done.88
  1043.6 12.1 collective-permute-done.60
  1057.0 12.6 collective-permute-done.92
  1073.0 18.1 %collective-permute-done.124 = bf16[2,1,2,2,96,256]{5,4,3,2,0,1:T(8,128)(2,1)S(1)} collective-permute-done((bf16[2,1,2,2,96,256]{5,4,3,2,0,1:T(8,128)(2,1)S(1)}, bf16[2,1,2,2,96,256]{5,4,3,2,0,1:T(8,128)(2,1)S(1)}, u32[]{:S(2)}, u32[]{:S(2)}) %collective-permute-start.124) | collective-permute-done | bytes 393248 | tf_op jit(solution)/shard_map/ppermute | solution.py:20
  1118.1 6.3 all-to-all-start.16
  1139.1 8.3 collective-permute-done.95
  1148.3 13.3 collective-permute-done.96
  1167.0 12.5 collective-permute-done.98
  1216.4 28.1 %collective-permute-done.108 = bf16[1,192,128]{2,1,0:T(8,128)(2,1)S(1)} collective-permute-done((bf16[1,192,128]{2,1,0:T(8,128)(2,1)S(1)}, bf16[1,192,128]{2,1,0:T(8,128)(2,1)S(1)}, u32[]{:S(2)}, u32[]{:S(2)}) %collective-permute-start.108) | collective-permute-done | bytes 49184 | tf_op jit(solution)/shard_map/ppermute | solution.py:286
  1255.4 13.0 collective-permute-start.115
  1277.0 6.8 collective-permute-done.117
  1310.8 8.1 collective-permute-done.112
  (942 shorter events, 765.4 us)
Async XLA Ops:
  42.3 52.2 %all-to-all-start.1 = ((bf16[8,256,512]{2,1,0:T(8,128)(2,1)}), bf16[8,256,512]{2,1,0:T(8,128)(2,1)}, u32[]{:S(2)}, u32[]{:S(2)}) async-start(bf16[8,256,512]{2,1,0:T(8,128)(2,1)} %shard_map.298), calls=%async_computation.1 | async-start | bytes 4194304 | tf_op jit(solution)/shard_map/all_to_all | solution.py:72
  46.7 124.6 %all-gather.10.cloned.1.call-start = ((), (), s32[]{:S(2)}) async-start(), calls=%async_computation.30 | async-start | bytes 3145728 | tf_op jit(solution)/shard_map/all_gather | solution.py:169
  94.5 68.3 %all-to-all-start.2 = ((bf16[8,256,512]{2,1,0:T(8,128)(2,1)}), bf16[8,256,512]{2,1,0:T(8,128)(2,1)}, u32[]{:S(2)}, u32[]{:S(2)}) async-start(bf16[8,256,512]{2,1,0:T(8,128)(2,1)} %shard_map.297), calls=%async_computation.2 | async-start | bytes 4194304 | tf_op jit(solution)/shard_map/all_to_all | solution.py:72
  98.9 246.1 %all-gather.12.cloned.1.call-start = ((), (), s32[]{:S(2)}) async-start(), calls=%async_computation.31 | async-start | bytes 6291456 | tf_op jit(solution)/shard_map/all_gather | solution.py:151
  106.9 52.2 %collective-permute-start.10 = (bf16[2,192,128]{2,1,0:T(8,128)(2,1)}, bf16[2,192,128]{2,1,0:T(8,128)(2,1)}, u32[]{:S(2)}, u32[]{:S(2)}) collective-permute-start(bf16[2,192,128]{2,1,0:T(8,128)(2,1)} %get-tuple-element.195), channel_id=1, source_target_pairs={{0,16},{4,20},{8,24},{12,28},{16,0},{20,4},{24,8},{28,12},{1,17},{... | collective-permute-start | bytes 294920 | tf_op jit(solution)/shard_map/ppermute | solution.py:270
  109.7 51.6 %collective-permute-start.11 = (bf16[2,192,128]{2,1,0:T(8,128)(2,1)}, bf16[2,192,128]{2,1,0:T(8,128)(2,1)}, u32[]{:S(2)}, u32[]{:S(2)}) collective-permute-start(bf16[2,192,128]{2,1,0:T(8,128)(2,1)} %get-tuple-element.194), channel_id=1, source_target_pairs={{0,20},{4,16},{8,28},{12,24},{16,4},{20,0},{24,12},{28,8},{1,21},{... | collective-permute-start | bytes 294920 | tf_op jit(solution)/shard_map/ppermute | solution.py:270
  123.6 44.6 %collective-permute-start.12 = (bf16[2,192,128]{2,1,0:T(8,128)(2,1)}, bf16[2,192,128]{2,1,0:T(8,128)(2,1)}, u32[]{:S(2)}, u32[]{:S(2)}) collective-permute-start(bf16[2,192,128]{2,1,0:T(8,128)(2,1)} %get-tuple-element.193), channel_id=1, source_target_pairs={{0,24},{4,28},{8,16},{12,20},{16,8},{20,12},{24,0},{28,4},{1,25},{... | collective-permute-start | bytes 294920 | tf_op jit(solution)/shard_map/ppermute | solution.py:270
  168.2 230.4 %all-gather.14.cloned.1.call-start = ((), (), s32[]{:S(2)}) async-start(), calls=%async_computation.32 | async-start | bytes 6291456 | tf_op jit(solution)/shard_map/all_gather | solution.py:151
  201.0 63.0 %all-to-all-start.4 = ((bf16[8,256,512]{2,1,0:T(8,128)(2,1)}), bf16[8,256,512]{2,1,0:T(8,128)(2,1)}, u32[]{:S(2)}, u32[]{:S(2)}) async-start(bf16[8,256,512]{2,1,0:T(8,128)(2,1)} %shard_map.299), calls=%async_computation.4 | async-start | bytes 4194304 | tf_op jit(solution)/shard_map/all_to_all | solution.py:72
  205.5 194.7 %all-gather.16.cloned.1.call-start = ((), (), s32[]{:S(2)}) async-start(), calls=%async_computation.33 | async-start | bytes 6291456 | tf_op jit(solution)/shard_map/all_gather | solution.py:151
  264.6 40.4 %all-to-all-start.5 = ((bf16[8,256,256]{2,1,0:T(8,128)(2,1)}), bf16[8,256,256]{2,1,0:T(8,128)(2,1)}, u32[]{:S(2)}, u32[]{:S(2)}) async-start(bf16[8,256,256]{2,1,0:T(8,128)(2,1)} %shard_map.304), calls=%async_computation.5 | async-start | bytes 2097152 | tf_op jit(solution)/shard_map/all_to_all | solution.py:72
  336.0 57.4 %all-to-all-start.7 = ((bf16[8,256,512]{2,1,0:T(8,128)(2,1)}), bf16[8,256,512]{2,1,0:T(8,128)(2,1)}, u32[]{:S(2)}, u32[]{:S(2)}) async-start(bf16[8,256,512]{2,1,0:T(8,128)(2,1)} %shard_map.302), calls=%async_computation.7 | async-start | bytes 4194304 | tf_op jit(solution)/shard_map/all_to_all | solution.py:72
  340.4 167.6 %all-gather.18.cloned.1.call-start = ((), (), s32[]{:S(2)}) async-start(), calls=%async_computation.34 | async-start | bytes 3145728 | tf_op jit(solution)/shard_map/all_gather | solution.py:151
  341.0 173.5 %all-gather.20.cloned.1.call-start = ((), (), s32[]{:S(2)}) async-start(), calls=%async_computation.35 | async-start | bytes 3145728 | tf_op jit(solution)/shard_map/all_gather | solution.py:151
  343.5 41.4 %collective-permute-start.25 = (bf16[96,2048]{1,0:T(8,128)(2,1)S(1)}, bf16[96,2048]{1,0:T(8,128)(2,1)S(1)}, u32[]{:S(2)}, u32[]{:S(2)}) collective-permute-start(bf16[96,2048]{1,0:T(8,128)(2,1)S(1)} %get-tuple-element.121), channel_id=1, source_target_pairs={{0,8},{8,0},{1,9},{9,1},{2,10},{10,2},{3,11},{11,3},{4,12},{12,4},... | collective-permute-start | bytes 1179656 | tf_op jit(solution)/shard_map/ppermute | solution.py:20
  345.0 105.2 %collective-permute-start.28 = (bf16[2048,1024]{1,0:T(8,128)(2,1)}, bf16[2048,1024]{1,0:T(8,128)(2,1)}, u32[]{:S(2)}, u32[]{:S(2)}) collective-permute-start(bf16[2048,1024]{1,0:T(8,128)(2,1)} %all-gather.12.cloned.1.call-done), channel_id=1, source_target_pairs={{0,1},{1,0},{2,3},{3,2},{4,5},{5,4},{6,7},{7,6},{8,9},{9,8},{10,11... | collective-permute-start | bytes 12582920 | tf_op jit(solution)/shard_map/ppermute | solution.py:20
  393.4 52.3 %all-to-all-start.8 = ((bf16[8,256,512]{2,1,0:T(8,128)(2,1)}), bf16[8,256,512]{2,1,0:T(8,128)(2,1)}, u32[]{:S(2)}, u32[]{:S(2)}) async-start(bf16[8,256,512]{2,1,0:T(8,128)(2,1)} %shard_map.301), calls=%async_computation.8 | async-start | bytes 4194304 | tf_op jit(solution)/shard_map/all_to_all | solution.py:72
  398.5 130.9 %all-gather.22.cloned.1.call-start = ((), (), s32[]{:S(2)}) async-start(), calls=%async_computation.36 | async-start | bytes 6291456 | tf_op jit(solution)/shard_map/all_gather | solution.py:151
  398.6 56.2 %collective-permute-start.29 = (bf16[2048,1024]{1,0:T(8,128)(2,1)}, bf16[2048,1024]{1,0:T(8,128)(2,1)}, u32[]{:S(2)}, u32[]{:S(2)}) collective-permute-start(bf16[2048,1024]{1,0:T(8,128)(2,1)} %all-gather.14.cloned.1.call-done), channel_id=1, source_target_pairs={{0,1},{1,0},{2,3},{3,2},{4,5},{5,4},{6,7},{7,6},{8,9},{9,8},{10,11... | collective-permute-start | bytes 12582920 | tf_op jit(solution)/shard_map/ppermute | solution.py:20
  400.2 73.4 %collective-permute-start.30 = (bf16[2048,1024]{1,0:T(8,128)(2,1)}, bf16[2048,1024]{1,0:T(8,128)(2,1)}, u32[]{:S(2)}, u32[]{:S(2)}) collective-permute-start(bf16[2048,1024]{1,0:T(8,128)(2,1)} %all-gather.16.cloned.1.call-done), channel_id=1, source_target_pairs={{0,1},{1,0},{2,3},{3,2},{4,5},{5,4},{6,7},{7,6},{8,9},{9,8},{10,11... | collective-permute-start | bytes 12582920 | tf_op jit(solution)/shard_map/ppermute | solution.py:20
  445.7 64.8 %all-to-all-start.9 = ((bf16[8,256,512]{2,1,0:T(8,128)(2,1)}), bf16[8,256,512]{2,1,0:T(8,128)(2,1)}, u32[]{:S(2)}, u32[]{:S(2)}) async-start(bf16[8,256,512]{2,1,0:T(8,128)(2,1)} %shard_map.300), calls=%async_computation.9 | async-start | bytes 4194304 | tf_op jit(solution)/shard_map/all_to_all | solution.py:72
  450.1 79.4 %all-gather.24.cloned.1.call-start = ((), (), s32[]{:S(2)}) async-start(), calls=%async_computation.37 | async-start | bytes 6291456 | tf_op jit(solution)/shard_map/all_gather | solution.py:151
  460.6 185.5 %all-gather.26.cloned.1.call-start = ((), (), s32[]{:S(2)}) async-start(), calls=%async_computation.38 | async-start | bytes 6291456 | tf_op jit(solution)/shard_map/all_gather | solution.py:151
  529.4 62.5 %collective-permute-start.53 = (bf16[2048,1024]{1,0:T(8,128)(2,1)}, bf16[2048,1024]{1,0:T(8,128)(2,1)}, u32[]{:S(2)}, u32[]{:S(2)}) collective-permute-start(bf16[2048,1024]{1,0:T(8,128)(2,1)} %all-gather.22.cloned.1.call-done), channel_id=1, source_target_pairs={{0,1},{1,0},{2,3},{3,2},{4,5},{5,4},{6,7},{7,6},{8,9},{9,8},{10,11... | collective-permute-start | bytes 12582920 | tf_op jit(solution)/shard_map/ppermute | solution.py:20
  533.0 63.5 %collective-permute-start.54 = (bf16[2048,1024]{1,0:T(8,128)(2,1)}, bf16[2048,1024]{1,0:T(8,128)(2,1)}, u32[]{:S(2)}, u32[]{:S(2)}) collective-permute-start(bf16[2048,1024]{1,0:T(8,128)(2,1)} %all-gather.24.cloned.1.call-done), channel_id=1, source_target_pairs={{0,1},{1,0},{2,3},{3,2},{4,5},{5,4},{6,7},{7,6},{8,9},{9,8},{10,11... | collective-permute-start | bytes 12582920 | tf_op jit(solution)/shard_map/ppermute | solution.py:20
  588.8 153.1 %reduce-scatter.11.cloned.1.call-start = ((), (), s32[]{:S(2)}) async-start(), calls=%async_computation.39 | async-start | bytes 6291456 | tf_op jit(solution)/shard_map/reduce_scatter | solution.py:160
  608.5 45.4 %collective-permute-start.66 = (bf16[2048,1024]{1,0:T(8,128)(2,1)}, bf16[2048,1024]{1,0:T(8,128)(2,1)}, u32[]{:S(2)}, u32[]{:S(2)}) collective-permute-start(bf16[2048,1024]{1,0:T(8,128)(2,1)} %convolution_convert_fusion.5), channel_id=1, source_target_pairs={{0,1},{1,0},{2,3},{3,2},{4,5},{5,4},{6,7},{7,6},{8,9},{9,8},{10,11... | collective-permute-start | bytes 12582920 | tf_op jit(solution)/shard_map/ppermute | solution.py:20
  661.8 152.9 %reduce-scatter.13.cloned.1.call-start = ((), (), s32[]{:S(2)}) async-start(), calls=%async_computation.40 | async-start | bytes 6291456 | tf_op jit(solution)/shard_map/reduce_scatter | solution.py:160
  683.7 206.0 %reduce-scatter.15.cloned.1.call-start = ((), (), s32[]{:S(2)}) async-start(), calls=%async_computation.41 | async-start | bytes 6291456 | tf_op jit(solution)/shard_map/reduce_scatter | solution.py:160
  741.9 72.7 %all-to-all-start.10 = ((bf16[8,256,512]{2,1,0:T(8,128)(2,1)}), bf16[8,256,512]{2,1,0:T(8,128)(2,1)}, u32[]{:S(2)}, u32[]{:S(2)}) async-start(bf16[8,256,512]{2,1,0:T(8,128)(2,1)} %bitcast.616), calls=%async_computation.11 | async-start | bytes 4194304 | tf_op jit(solution)/shard_map/all_to_all | solution.py:72
  751.7 38.1 %collective-permute-start.72 = (bf16[96,2048]{1,0:T(8,128)(2,1)S(1)}, bf16[96,2048]{1,0:T(8,128)(2,1)S(1)}, u32[]{:S(2)}, u32[]{:S(2)}) collective-permute-start(bf16[96,2048]{1,0:T(8,128)(2,1)S(1)} %get-tuple-element.117), channel_id=1, source_target_pairs={{0,8},{8,0},{1,9},{9,1},{2,10},{10,2},{3,11},{11,3},{4,12},{12,4},... | collective-permute-start | bytes 1179656 | tf_op jit(solution)/shard_map/ppermute | solution.py:20
  814.7 68.9 %all-to-all-start.11 = ((bf16[8,256,512]{2,1,0:T(8,128)(2,1)}), bf16[8,256,512]{2,1,0:T(8,128)(2,1)}, u32[]{:S(2)}, u32[]{:S(2)}) async-start(bf16[8,256,512]{2,1,0:T(8,128)(2,1)} %bitcast.613), calls=%async_computation.13 | async-start | bytes 4194304 | tf_op jit(solution)/shard_map/all_to_all | solution.py:72
  819.4 143.8 %reduce-scatter.17.cloned.1.call-start = ((), (), s32[]{:S(2)}) async-start(), calls=%async_computation.42 | async-start | bytes 3145728 | tf_op jit(solution)/shard_map/reduce_scatter | solution.py:160
  823.9 165.2 %reduce-scatter.19.cloned.1.call-start = ((), (), s32[]{:S(2)}) async-start(), calls=%async_computation.43 | async-start | bytes 3145728 | tf_op jit(solution)/shard_map/reduce_scatter | solution.py:160
  827.5 49.7 %collective-permute-start.86 = (bf16[2048,512]{1,0:T(8,128)(2,1)S(1)}, bf16[2048,512]{1,0:T(8,128)(2,1)S(1)}, u32[]{:S(2)}, u32[]{:S(2)}) collective-permute-start(bf16[2048,512]{1,0:T(8,128)(2,1)S(1)} %convolution_convert_fusion.8), channel_id=1, source_target_pairs={{0,1},{1,0},{2,3},{3,2},{4,5},{5,4},{6,7},{7,6},{8,9},{9,8},{10,11... | collective-permute-start | bytes 6291464 | tf_op jit(solution)/shard_map/ppermute | solution.py:20
  889.7 53.7 %all-to-all-start.12 = ((bf16[8,256,512]{2,1,0:T(8,128)(2,1)}), bf16[8,256,512]{2,1,0:T(8,128)(2,1)}, u32[]{:S(2)}, u32[]{:S(2)}) async-start(bf16[8,256,512]{2,1,0:T(8,128)(2,1)} %bitcast.612), calls=%async_computation.15 | async-start | bytes 4194304 | tf_op jit(solution)/shard_map/all_to_all | solution.py:72
  894.2 137.2 %reduce-scatter.21.cloned.1.call-start = ((), (), s32[]{:S(2)}) async-start(), calls=%async_computation.44 | async-start | bytes 6291456 | tf_op jit(solution)/shard_map/reduce_scatter | solution.py:160
  903.7 214.4 %reduce-scatter.23.cloned.1.call-start = ((), (), s32[]{:S(2)}) async-start(), calls=%async_computation.45 | async-start | bytes 6291456 | tf_op jit(solution)/shard_map/reduce_scatter | solution.py:160
  966.8 235.9 %reduce-scatter.25.cloned.1.call-start = ((), (), s32[]{:S(2)}) async-start(), calls=%async_computation.46 | async-start | bytes 6291456 | tf_op jit(solution)/shard_map/reduce_scatter | solution.py:160
  993.3 38.0 %all-to-all-start.14 = ((bf16[8,256,256]{2,1,0:T(8,128)(2,1)}), bf16[8,256,256]{2,1,0:T(8,128)(2,1)S(1)}, u32[]{:S(2)}, u32[]{:S(2)}) async-start(bf16[8,256,256]{2,1,0:T(8,128)(2,1)} %bitcast.647), calls=%async_computation.19 | async-start | bytes 2097152 | tf_op jit(solution)/shard_map/all_to_all | solution.py:72
  1032.3 83.0 %all-to-all-start.15 = ((bf16[8,256,512]{2,1,0:T(8,128)(2,1)}), bf16[8,256,512]{2,1,0:T(8,128)(2,1)}, u32[]{:S(2)}, u32[]{:S(2)}) async-start(bf16[8,256,512]{2,1,0:T(8,128)(2,1)} %bitcast.615), calls=%async_computation.21 | async-start | bytes 4194304 | tf_op jit(solution)/shard_map/all_to_all | solution.py:72
  1070.7 42.4 %collective-permute-start.93 = (bf16[2,2,1,48,2048]{4,3,2,1,0:T(8,128)(2,1)}, bf16[2,2,1,48,2048]{4,3,2,1,0:T(8,128)(2,1)}, u32[]{:S(2)}, u32[]{:S(2)}) collective-permute-start(bf16[2,2,1,48,2048]{4,3,2,1,0:T(8,128)(2,1)} %maximum_select_fusion.5), channel_id=1, source_target_pairs={{0,1},{1,0},{2,3},{3,2},{4,5},{5,4},{6,7},{7,6},{8,9},{9,8},{10,11... | collective-permute-start | bytes 2359304 | tf_op jit(solution)/shard_map/ppermute | solution.py:20
  1118.1 76.4 %all-to-all-start.16 = ((bf16[8,256,512]{2,1,0:T(8,128)(2,1)}), bf16[8,256,512]{2,1,0:T(8,128)(2,1)}, u32[]{:S(2)}, u32[]{:S(2)}) async-start(bf16[8,256,512]{2,1,0:T(8,128)(2,1)} %bitcast.611), calls=%async_computation.23 | async-start | bytes 4194304 | tf_op jit(solution)/shard_map/all_to_all | solution.py:72
  1124.4 169.9 %reduce-scatter.29.cloned.1.call-start = ((), (), s32[]{:S(2)}) async-start(), calls=%async_computation.48 | async-start | bytes 3145728 | tf_op jit(solution)/shard_map/reduce_scatter | solution.py:174
  1128.3 51.1 %collective-permute-start.98 = (bf16[1,192,128]{2,1,0:T(8,128)(2,1)S(1)}, bf16[1,192,128]{2,1,0:T(8,128)(2,1)}, u32[]{:S(2)}, u32[]{:S(2)}) collective-permute-start(bf16[1,192,128]{2,1,0:T(8,128)(2,1)S(1)} %get-tuple-element.211), channel_id=1, source_target_pairs={{0,16},{4,20},{8,24},{12,28},{16,0},{20,4},{24,8},{28,12},{1,17},{... | collective-permute-start | bytes 147464 | tf_op jit(solution)/shard_map/ppermute | solution.py:270
  1131.2 49.9 %collective-permute-start.99 = (bf16[1,192,128]{2,1,0:T(8,128)(2,1)S(1)}, bf16[1,192,128]{2,1,0:T(8,128)(2,1)}, u32[]{:S(2)}, u32[]{:S(2)}) collective-permute-start(bf16[1,192,128]{2,1,0:T(8,128)(2,1)S(1)} %get-tuple-element.210), channel_id=1, source_target_pairs={{0,20},{4,16},{8,28},{12,24},{16,4},{20,0},{24,12},{28,8},{1,21},{... | collective-permute-start | bytes 147464 | tf_op jit(solution)/shard_map/ppermute | solution.py:270
  1202.7 81.1 %all-to-all-start.17 = ((bf16[8,256,512]{2,1,0:T(8,128)(2,1)}), bf16[8,256,512]{2,1,0:T(8,128)(2,1)}, u32[]{:S(2)}, u32[]{:S(2)}) async-start(bf16[8,256,512]{2,1,0:T(8,128)(2,1)} %bitcast.610), calls=%async_computation.25 | async-start | bytes 4194304 | tf_op jit(solution)/shard_map/all_to_all | solution.py:72
  1207.0 116.9 %reduce-scatter.27.cloned.1.call-start = ((), (), s32[]{:S(2)}) async-start(), calls=%async_computation.47 | async-start | bytes 3145728 | tf_op jit(solution)/shard_map/reduce_scatter | solution.py:174
  (268 other events, 4461.6 us)
Sparse Core Ops, SparseCore 0:
  49.7 45.2 all-gather.9
  101.3 58.0 all-gather.11
  200.5 55.5 all-gather.13
  264.1 57.7 all-gather.15
  342.5 34.3 all-gather.17
  378.3 33.3 all-gather.19
  413.2 56.4 all-gather.21
  471.3 56.7 all-gather.23
  588.9 57.1 all-gather.25
  661.9 54.4 reduce-scatter.10
  718.8 54.3 reduce-scatter.12
  775.2 54.2 reduce-scatter.14
  832.5 31.8 reduce-scatter.16
  889.8 29.9 reduce-scatter.18
  922.0 54.3 reduce-scatter.20
  978.5 54.2 reduce-scatter.22
  1035.1 74.6 reduce-scatter.24
  1135.4 42.2 reduce-scatter.28
  1272.4 33.8 reduce-scatter.26

commit v4 on v3

--- a/solution.py
+++ b/solution.py
@@ -168,10 +168,14 @@
             return in_order(self.y, a, swap(a, "y"), 1).reshape(-1, w.shape[1])
         return lax.all_gather(a, "y", axis=1, tiled=True).reshape(-1, w.shape[1])
 
-    def scatter_rows(self, left, right):
+    def scatter_rows(self, left, right, swapped=False):
         part = dot_tn(left, right).astype(BF)
         t = part.reshape(-1, 2 * self.rows, right.shape[1])
-        t = lax.psum_scatter(t, "y", scatter_dimension=1, tiled=True)
+        if swapped:
+            got = swap(half(t, 1 - self.y, 1), "y")
+            t = half(t, self.y, 1).astype(F32) + got.astype(F32)
+        else:
+            t = lax.psum_scatter(t, "y", scatter_dimension=1, tiled=True)
         t = self.ordered(total_ze(t).astype(BF), ("zh", "zl")).astype(F32)
         return part, (t[0] + t[1]) + (t[2] + t[3])
 
@@ -432,14 +436,14 @@
     dn3 = after(at.collect(dn3), (part_o, far, zline[10]))
     memory_grad = at.memory_out(dm[0], dm[1], mb)
     back, gain3 = rms_back(x2, gains[2], dn3)
-    dx2 = dx3 + back
+    dx2 = held(dx3 + back, zline[11])
 
     part_i, memory_in_grad = at.close_grad(n3, dz[0], got)
     ya = after(at.spread(dx2.astype(BF)), (part_i, zline[11]))
     dn2, down_first_grad, open_g, open_u = ffn_back(ya, kept1, g1, u1, d1, (zline[12],))
     dn2 = after(dn2, (zline[13], zline[14]))
     back, gain2 = rms_back(x1, gains[1], dn2)
-    dx1 = dx2 + back
+    dx1 = held(dx2 + back, zline[15])
 
     part_g, gate_first_grad = at.close_grad(*open_g)
     yo = after(at.spread_tp(dx1.astype(BF), mb), (part_g, zline[15])).reshape(mb * tok, width)
@@ -447,18 +451,19 @@
     do = to_pairs(dot(yo, wo).astype(BF).reshape(1, mb, tok, -1))[0]
     do = after(do, part_u)
     part_w, output_grad = at.scatter_rows(yo, attn)
+    do = held(do, zline[16])
     delta = jnp.sum(do.astype(F32) * o, axis=1, keepdims=True)
     p = jnp.exp(s - lse)
     ds = (p * (dot_nt(do, values) - delta)).astype(BF)
     dq = after((dot(ds, keys) * scaling).astype(BF)[None], (part_w, zline[16]))
-    dq = from_pairs(held(dq, zline[16]), mb, tok)
+    dq = from_pairs(dq, mb, tok)
     dk = total_ze(dot_tn(ds, q) * scaling).astype(BF)
     dv = total_ze(dot_tn(p.astype(BF), do)).astype(BF)
     dkv = from_pairs(held(jnp.stack([dk, dv]), dq), mb, tok).astype(F32)
     keys_grad, values_grad = dkv[0], dkv[1]
     dq = dq.reshape(mb * tok, -1)
     dn1 = at.collect_tp(held(dot_nt(dq, wq), zline[17]), mb)
-    _, query_grad = at.scatter_rows(n1, dq)
+    _, query_grad = at.scatter_rows(n1, dq, True)
     back, gain1 = rms_back(r0, gains[0], dn1)
     stream_grad = at.spread_tp((dx1 + back).astype(BF), mb).astype(F32)
 

time: 1380 us -> 1350 us (0.978)
  starting transfers between devices: 289 us -> 268 us
    all_to_all x20, waiting for transfers between devices: 114 us -> 143 us  [trade(): return lax.all_to_all(value, axes, split_axis=0, concat_axis=0, tiled=True)]
    ppermute x21, waiting for transfers between devices: 67.5 us -> 39 us  [exchange(): lax.ppermute(block, GROUP, [(i, i ^ k) for i in range(8)])]
    ppermute x88 -> x89, waiting for transfers between devices: 298 us -> 285 us  [swap(): return lax.ppermute(value, axis, [(0, 1), (1, 0)])]
    ppermute x88 -> x89, starting transfers between devices: 93.8 us -> 87.6 us  [swap(): return lax.ppermute(value, axis, [(0, 1), (1, 0)])]
    unnamed x358 -> x376, local copies, waits for them, and re-layouts: 51.8 us -> 54.1 us
  transfers between devices with their start and end apart: 169 -> 169, of which waited for: 73 -> 69; matrix products, arithmetic and copies ran while one was open for 28% -> 29% of each run, Pallas kernels for 5% -> 6%
where the time goes in v4:
time: 1350 us; the launch traced here: 1340 us
  waiting for transfers between devices  563 us (42%)
  starting transfers between devices  268 us (20%)
  matrix products  235 us (17%)
  local copies, waits for them, and re-layouts  98.6 us (7%)
  other arithmetic  85.1 us (6%)
  Pallas kernels  73.9 us (5%)
  between operations  17.7 us (1%)
    ppermute x89, waiting for transfers between devices, swap(): return lax.ppermute(value, axis, [(0, 1), (1, 0)])  285 us
    all_to_all x20, waiting for transfers between devices, trade(): return lax.all_to_all(value, axes, split_axis=0, concat_axis=0, tiled=True)  143 us
    all_to_all x20, starting transfers between devices, trade(): return lax.all_to_all(value, axes, split_axis=0, concat_axis=0, tiled=True)  90.5 us
    ppermute x89, starting transfers between devices, swap(): return lax.ppermute(value, axis, [(0, 1), (1, 0)])  87.6 us
    dot_general x20, matrix products, dot_tn(): lax.dot_general(a, b, (((0,), (0,)), ((), ())), preferred_element_type=F32)  85.4 us
    dot_general x20, matrix products, dot(): return jnp.dot(a, b, preferred_element_type=F32)  83.4 us
    dot_general x20, matrix products, dot_nt(): lax.dot_general(a, b, (((1,), (1,)), ((), ())), preferred_element_type=F32)  66.1 us
    ppermute x21, waiting for transfers between devices, from_pairs(): got.append(lax.ppermute(v[:, k], GROUP, [(i, i ^ k) for i in range(8)]))  60.1 us
  transfers between devices with their start and end apart: 169, of which 69 were waited for; matrix products, arithmetic and copies ran while one was open for 29% of the time, Pallas kernels for 6%

profile of v4, /device:TPU:0, one launch (start us, length us, event | category | flops | bytes accessed | tf_op | source)
XLA Modules:
  0.0 1341.1 jit_solution(8252573384857167539)
XLA Ops:
  9.3 6.3 all-to-all-start
  21.3 20.1 %all-to-all-done = bf16[4,256,512]{2,1,0:T(8,128)(2,1)S(1)} async-done(((bf16[4,256,512]{2,1,0:T(8,128)(2,1)}), bf16[4,256,512]{2,1,0:T(8,128)(2,1)S(1)}, u32[]{:S(2)}, u32[]{:S(2)}) %all-to-all-start) | async-done | bytes 1048608 | tf_op jit(solution)/shard_map/all_to_all | solution.py:72
  47.4 5.7 shard_map.297
  53.1 41.4 %all-to-all-done.1 = bf16[8,256,512]{2,1,0:T(8,128)(2,1)} async-done(((bf16[8,256,512]{2,1,0:T(8,128)(2,1)}), bf16[8,256,512]{2,1,0:T(8,128)(2,1)}, u32[]{:S(2)}, u32[]{:S(2)}) %all-to-all-start.1) | async-done | bytes 2097184 | tf_op jit(solution)/shard_map/all_to_all | solution.py:72
  111.1 5.7 shard_map.299
  128.5 8.2 collective-permute-done.8
  143.9 15.1 %collective-permute-done.10 = bf16[2,192,128]{2,1,0:T(8,128)(2,1)} collective-permute-done((bf16[2,192,128]{2,1,0:T(8,128)(2,1)}, bf16[2,192,128]{2,1,0:T(8,128)(2,1)}, u32[]{:S(2)}, u32[]{:S(2)}) %collective-permute-start.10) | collective-permute-done | bytes 98336 | tf_op jit(solution)/shard_map/ppermute | solution.py:274
  190.9 7.4 collective-permute-done.3
  234.7 6.3 collective-permute-done.15
  245.8 13.0 collective-permute-done.17
  272.7 20.3 %collective-permute-done.21 = bf16[4,256,512]{2,1,0:T(8,128)(2,1)} collective-permute-done((bf16[4,256,512]{2,1,0:T(8,128)(2,1)}, bf16[4,256,512]{2,1,0:T(8,128)(2,1)}, u32[]{:S(2)}, u32[]{:S(2)}) %collective-permute-start.21) | collective-permute-done | bytes 1048608 | tf_op jit(solution)/shard_map/ppermute | solution.py:20
  319.6 7.6 collective-permute-done.23
  345.0 24.2 %collective-permute-done.24 = bf16[96,2048]{1,0:T(8,128)(2,1)S(1)} collective-permute-done((bf16[96,2048]{1,0:T(8,128)(2,1)S(1)}, bf16[96,2048]{1,0:T(8,128)(2,1)S(1)}, u32[]{:S(2)}, u32[]{:S(2)}) %collective-permute-start.24) | collective-permute-done | bytes 393248 | tf_op jit(solution)/shard_map/ppermute | solution.py:20
  372.7 12.2 collective-permute-done.25
  386.5 5.7 shard_map.301
  430.4 15.3 %all-to-all-done.8 = bf16[8,256,512]{2,1,0:T(8,128)(2,1)} async-done(((bf16[8,256,512]{2,1,0:T(8,128)(2,1)}), bf16[8,256,512]{2,1,0:T(8,128)(2,1)}, u32[]{:S(2)}, u32[]{:S(2)}) %all-to-all-start.8) | async-done | bytes 2097184 | tf_op jit(solution)/shard_map/all_to_all | solution.py:72
  454.7 5.8 multiply_convert_fusion.10
  460.6 8.8 all-gather.26.cloned.1.call-start
  515.6 9.6 collective-permute-done.39
  548.3 8.5 collective-permute-done.45
  567.8 8.7 collective-permute-done.49
  596.3 6.4 multiply_convert_fusion.8
  602.7 5.7 convolution_convert_fusion.5
  613.6 32.4 %all-gather.26.cloned.1.call-done = bf16[2048,1024]{1,0:T(8,128)(2,1)} async-done(((bf16[2048,512]{1,0:T(8,128)(2,1)}), bf16[2048,1024]{1,0:T(8,128)(2,1)}) %all-gather.26.cloned.1.call-update) | async-done | bytes 4194320 | tf_op jit(solution)/shard_map/all_gather | solution.py:151
  654.7 6.9 add_convert_fusion.5
  661.7 6.7 multiply_convert_fusion.4
  672.2 6.8 collective-permute-done.75
  750.2 17.7 %collective-permute-done.71 = bf16[96,2048]{1,0:T(8,128)(2,1)S(1)} collective-permute-done((bf16[96,2048]{1,0:T(8,128)(2,1)S(1)}, bf16[96,2048]{1,0:T(8,128)(2,1)S(1)}, u32[]{:S(2)}, u32[]{:S(2)}) %collective-permute-start.71) | collective-permute-done | bytes 393248 | tf_op jit(solution)/shard_map/ppermute | solution.py:20
  768.4 16.0 %collective-permute-done.72 = bf16[96,2048]{1,0:T(8,128)(2,1)S(1)} collective-permute-done((bf16[96,2048]{1,0:T(8,128)(2,1)S(1)}, bf16[96,2048]{1,0:T(8,128)(2,1)S(1)}, u32[]{:S(2)}, u32[]{:S(2)}) %collective-permute-start.72) | collective-permute-done | bytes 393248 | tf_op jit(solution)/shard_map/ppermute | solution.py:20
  795.7 6.4 all-to-all-start.11
  824.4 21.1 %collective-permute-done.77 = bf16[2,96,1024]{2,1,0:T(8,128)(2,1)S(1)} collective-permute-done((bf16[2,96,1024]{2,1,0:T(8,128)(2,1)S(1)}, bf16[2,96,1024]{2,1,0:T(8,128)(2,1)S(1)}, u32[]{:S(2)}, u32[]{:S(2)}) %collective-permute-start.77) | collective-permute-done | bytes 393248 | tf_op jit(solution)/shard_map/ppermute | solution.py:20
  860.9 7.3 collective-permute-done.82
  889.4 6.6 add_convert_fusion.2
  897.4 6.2 multiply_convert_fusion.1
  903.6 5.7 multiply_convert_fusion
  909.3 26.4 %all-to-all-done.12.a_ref.b_ref = bf16[8,256,512]{2,1,0:T(8,128)(2,1)} async-done(((bf16[8,256,512]{2,1,0:T(8,128)(2,1)}), bf16[8,256,512]{2,1,0:T(8,128)(2,1)}, u32[]{:S(2)}, u32[]{:S(2)}) %all-to-all-start.12) | async-done | bytes 2097184 | tf_op jit(solution)/shard_map/all_to_all | solution.py:72
  939.4 7.1 collective-permute-done.94
  960.3 26.4 %all-to-all-done.13.a_ref.b_ref = bf16[8,256,256]{2,1,0:T(8,128)(2,1)S(1)} async-done(((bf16[8,256,256]{2,1,0:T(8,128)(2,1)}), bf16[8,256,256]{2,1,0:T(8,128)(2,1)S(1)}, u32[]{:S(2)}, u32[]{:S(2)}) %all-to-all-start.13) | async-done | bytes 1048608 | tf_op jit(solution)/shard_map/all_to_all | solution.py:72
  990.8 7.6 add_convert_fusion
  1002.4 5.9 fusion.152
  1008.3 8.1 all-to-all-done.14.a_ref.b_ref
  1041.7 22.3 %collective-permute-done.88 = bf16[2,96,1024]{2,1,0:T(8,128)(2,1)S(1)} collective-permute-done((bf16[2,96,1024]{2,1,0:T(8,128)(2,1)S(1)}, bf16[2,96,1024]{2,1,0:T(8,128)(2,1)S(1)}, u32[]{:S(2)}, u32[]{:S(2)}) %collective-permute-start.88) | collective-permute-done | bytes 393248 | tf_op jit(solution)/shard_map/ppermute | solution.py:20
  1083.6 6.2 collective-permute-done.60
  1091.1 6.4 collective-permute-done.92
  1103.5 9.9 collective-permute-done.124
  1199.3 19.0 %collective-permute-done.105 = bf16[1,192,128]{2,1,0:T(8,128)(2,1)S(1)} collective-permute-done((bf16[1,192,128]{2,1,0:T(8,128)(2,1)S(1)}, bf16[1,192,128]{2,1,0:T(8,128)(2,1)S(1)}, u32[]{:S(2)}, u32[]{:S(2)}) %collective-permute-start.105) | collective-permute-done | bytes 49184 | tf_op jit(solution)/shard_map/ppermute | solution.py:290
  1218.3 17.9 %collective-permute-done.106 = bf16[1,192,128]{2,1,0:T(8,128)(2,1)S(1)} collective-permute-done((bf16[1,192,128]{2,1,0:T(8,128)(2,1)S(1)}, bf16[1,192,128]{2,1,0:T(8,128)(2,1)S(1)}, u32[]{:S(2)}, u32[]{:S(2)}) %collective-permute-start.106) | collective-permute-done | bytes 49184 | tf_op jit(solution)/shard_map/ppermute | solution.py:290
  1287.3 8.1 collective-permute-done.112
  (965 shorter events, 744.8 us)
Async XLA Ops:
  42.3 52.1 %all-to-all-start.1 = ((bf16[8,256,512]{2,1,0:T(8,128)(2,1)}), bf16[8,256,512]{2,1,0:T(8,128)(2,1)}, u32[]{:S(2)}, u32[]{:S(2)}) async-start(bf16[8,256,512]{2,1,0:T(8,128)(2,1)} %shard_map.298), calls=%async_computation.1 | async-start | bytes 4194304 | tf_op jit(solution)/shard_map/all_to_all | solution.py:72
  46.7 124.6 %all-gather.10.cloned.1.call-start = ((), (), s32[]{:S(2)}) async-start(), calls=%async_computation.29 | async-start | bytes 3145728 | tf_op jit(solution)/shard_map/all_gather | solution.py:169
  94.5 68.3 %all-to-all-start.2 = ((bf16[8,256,512]{2,1,0:T(8,128)(2,1)}), bf16[8,256,512]{2,1,0:T(8,128)(2,1)}, u32[]{:S(2)}, u32[]{:S(2)}) async-start(bf16[8,256,512]{2,1,0:T(8,128)(2,1)} %shard_map.297), calls=%async_computation.2 | async-start | bytes 4194304 | tf_op jit(solution)/shard_map/all_to_all | solution.py:72
  98.8 246.2 %all-gather.12.cloned.1.call-start = ((), (), s32[]{:S(2)}) async-start(), calls=%async_computation.30 | async-start | bytes 6291456 | tf_op jit(solution)/shard_map/all_gather | solution.py:151
  106.8 52.2 %collective-permute-start.10 = (bf16[2,192,128]{2,1,0:T(8,128)(2,1)}, bf16[2,192,128]{2,1,0:T(8,128)(2,1)}, u32[]{:S(2)}, u32[]{:S(2)}) collective-permute-start(bf16[2,192,128]{2,1,0:T(8,128)(2,1)} %get-tuple-element.191), channel_id=1, source_target_pairs={{0,16},{4,20},{8,24},{12,28},{16,0},{20,4},{24,8},{28,12},{1,17},{... | collective-permute-start | bytes 294920 | tf_op jit(solution)/shard_map/ppermute | solution.py:274
  109.6 51.6 %collective-permute-start.11 = (bf16[2,192,128]{2,1,0:T(8,128)(2,1)}, bf16[2,192,128]{2,1,0:T(8,128)(2,1)}, u32[]{:S(2)}, u32[]{:S(2)}) collective-permute-start(bf16[2,192,128]{2,1,0:T(8,128)(2,1)} %get-tuple-element.190), channel_id=1, source_target_pairs={{0,20},{4,16},{8,28},{12,24},{16,4},{20,0},{24,12},{28,8},{1,21},{... | collective-permute-start | bytes 294920 | tf_op jit(solution)/shard_map/ppermute | solution.py:274
  123.6 44.6 %collective-permute-start.12 = (bf16[2,192,128]{2,1,0:T(8,128)(2,1)}, bf16[2,192,128]{2,1,0:T(8,128)(2,1)}, u32[]{:S(2)}, u32[]{:S(2)}) collective-permute-start(bf16[2,192,128]{2,1,0:T(8,128)(2,1)} %get-tuple-element.189), channel_id=1, source_target_pairs={{0,24},{4,28},{8,16},{12,20},{16,8},{20,12},{24,0},{28,4},{1,25},{... | collective-permute-start | bytes 294920 | tf_op jit(solution)/shard_map/ppermute | solution.py:274
  168.1 230.5 %all-gather.14.cloned.1.call-start = ((), (), s32[]{:S(2)}) async-start(), calls=%async_computation.31 | async-start | bytes 6291456 | tf_op jit(solution)/shard_map/all_gather | solution.py:151
  201.0 63.0 %all-to-all-start.4 = ((bf16[8,256,512]{2,1,0:T(8,128)(2,1)}), bf16[8,256,512]{2,1,0:T(8,128)(2,1)}, u32[]{:S(2)}, u32[]{:S(2)}) async-start(bf16[8,256,512]{2,1,0:T(8,128)(2,1)} %shard_map.299), calls=%async_computation.4 | async-start | bytes 4194304 | tf_op jit(solution)/shard_map/all_to_all | solution.py:72
  205.5 194.8 %all-gather.16.cloned.1.call-start = ((), (), s32[]{:S(2)}) async-start(), calls=%async_computation.32 | async-start | bytes 6291456 | tf_op jit(solution)/shard_map/all_gather | solution.py:151
  264.7 40.4 %all-to-all-start.5 = ((bf16[8,256,256]{2,1,0:T(8,128)(2,1)}), bf16[8,256,256]{2,1,0:T(8,128)(2,1)}, u32[]{:S(2)}, u32[]{:S(2)}) async-start(bf16[8,256,256]{2,1,0:T(8,128)(2,1)} %shard_map.304), calls=%async_computation.5 | async-start | bytes 2097152 | tf_op jit(solution)/shard_map/all_to_all | solution.py:72
  336.1 57.4 %all-to-all-start.7 = ((bf16[8,256,512]{2,1,0:T(8,128)(2,1)}), bf16[8,256,512]{2,1,0:T(8,128)(2,1)}, u32[]{:S(2)}, u32[]{:S(2)}) async-start(bf16[8,256,512]{2,1,0:T(8,128)(2,1)} %shard_map.302), calls=%async_computation.7 | async-start | bytes 4194304 | tf_op jit(solution)/shard_map/all_to_all | solution.py:72
  340.4 167.5 %all-gather.18.cloned.1.call-start = ((), (), s32[]{:S(2)}) async-start(), calls=%async_computation.33 | async-start | bytes 3145728 | tf_op jit(solution)/shard_map/all_gather | solution.py:151
  341.0 173.5 %all-gather.20.cloned.1.call-start = ((), (), s32[]{:S(2)}) async-start(), calls=%async_computation.34 | async-start | bytes 3145728 | tf_op jit(solution)/shard_map/all_gather | solution.py:151
  343.5 41.4 %collective-permute-start.25 = (bf16[96,2048]{1,0:T(8,128)(2,1)S(1)}, bf16[96,2048]{1,0:T(8,128)(2,1)S(1)}, u32[]{:S(2)}, u32[]{:S(2)}) collective-permute-start(bf16[96,2048]{1,0:T(8,128)(2,1)S(1)} %get-tuple-element.117), channel_id=1, source_target_pairs={{0,8},{8,0},{1,9},{9,1},{2,10},{10,2},{3,11},{11,3},{4,12},{12,4},... | collective-permute-start | bytes 1179656 | tf_op jit(solution)/shard_map/ppermute | solution.py:20
  345.0 105.1 %collective-permute-start.28 = (bf16[2048,1024]{1,0:T(8,128)(2,1)}, bf16[2048,1024]{1,0:T(8,128)(2,1)}, u32[]{:S(2)}, u32[]{:S(2)}) collective-permute-start(bf16[2048,1024]{1,0:T(8,128)(2,1)} %all-gather.12.cloned.1.call-done), channel_id=1, source_target_pairs={{0,1},{1,0},{2,3},{3,2},{4,5},{5,4},{6,7},{7,6},{8,9},{9,8},{10,11... | collective-permute-start | bytes 12582920 | tf_op jit(solution)/shard_map/ppermute | solution.py:20
  393.4 52.3 %all-to-all-start.8 = ((bf16[8,256,512]{2,1,0:T(8,128)(2,1)}), bf16[8,256,512]{2,1,0:T(8,128)(2,1)}, u32[]{:S(2)}, u32[]{:S(2)}) async-start(bf16[8,256,512]{2,1,0:T(8,128)(2,1)} %shard_map.301), calls=%async_computation.8 | async-start | bytes 4194304 | tf_op jit(solution)/shard_map/all_to_all | solution.py:72
  398.5 130.8 %all-gather.22.cloned.1.call-start = ((), (), s32[]{:S(2)}) async-start(), calls=%async_computation.35 | async-start | bytes 6291456 | tf_op jit(solution)/shard_map/all_gather | solution.py:151
  398.6 56.1 %collective-permute-start.29 = (bf16[2048,1024]{1,0:T(8,128)(2,1)}, bf16[2048,1024]{1,0:T(8,128)(2,1)}, u32[]{:S(2)}, u32[]{:S(2)}) collective-permute-start(bf16[2048,1024]{1,0:T(8,128)(2,1)} %all-gather.14.cloned.1.call-done), channel_id=1, source_target_pairs={{0,1},{1,0},{2,3},{3,2},{4,5},{5,4},{6,7},{7,6},{8,9},{9,8},{10,11... | collective-permute-start | bytes 12582920 | tf_op jit(solution)/shard_map/ppermute | solution.py:20
  400.3 73.4 %collective-permute-start.30 = (bf16[2048,1024]{1,0:T(8,128)(2,1)}, bf16[2048,1024]{1,0:T(8,128)(2,1)}, u32[]{:S(2)}, u32[]{:S(2)}) collective-permute-start(bf16[2048,1024]{1,0:T(8,128)(2,1)} %all-gather.16.cloned.1.call-done), channel_id=1, source_target_pairs={{0,1},{1,0},{2,3},{3,2},{4,5},{5,4},{6,7},{7,6},{8,9},{9,8},{10,11... | collective-permute-start | bytes 12582920 | tf_op jit(solution)/shard_map/ppermute | solution.py:20
  445.7 64.8 %all-to-all-start.9 = ((bf16[8,256,512]{2,1,0:T(8,128)(2,1)}), bf16[8,256,512]{2,1,0:T(8,128)(2,1)}, u32[]{:S(2)}, u32[]{:S(2)}) async-start(bf16[8,256,512]{2,1,0:T(8,128)(2,1)} %shard_map.300), calls=%async_computation.9 | async-start | bytes 4194304 | tf_op jit(solution)/shard_map/all_to_all | solution.py:72
  450.1 79.3 %all-gather.24.cloned.1.call-start = ((), (), s32[]{:S(2)}) async-start(), calls=%async_computation.36 | async-start | bytes 6291456 | tf_op jit(solution)/shard_map/all_gather | solution.py:151
  460.6 185.4 %all-gather.26.cloned.1.call-start = ((), (), s32[]{:S(2)}) async-start(), calls=%async_computation.37 | async-start | bytes 6291456 | tf_op jit(solution)/shard_map/all_gather | solution.py:151
  529.3 62.4 %collective-permute-start.53 = (bf16[2048,1024]{1,0:T(8,128)(2,1)}, bf16[2048,1024]{1,0:T(8,128)(2,1)}, u32[]{:S(2)}, u32[]{:S(2)}) collective-permute-start(bf16[2048,1024]{1,0:T(8,128)(2,1)} %all-gather.22.cloned.1.call-done), channel_id=1, source_target_pairs={{0,1},{1,0},{2,3},{3,2},{4,5},{5,4},{6,7},{7,6},{8,9},{9,8},{10,11... | collective-permute-start | bytes 12582920 | tf_op jit(solution)/shard_map/ppermute | solution.py:20
  532.9 63.4 %collective-permute-start.54 = (bf16[2048,1024]{1,0:T(8,128)(2,1)}, bf16[2048,1024]{1,0:T(8,128)(2,1)}, u32[]{:S(2)}, u32[]{:S(2)}) collective-permute-start(bf16[2048,1024]{1,0:T(8,128)(2,1)} %all-gather.24.cloned.1.call-done), channel_id=1, source_target_pairs={{0,1},{1,0},{2,3},{3,2},{4,5},{5,4},{6,7},{7,6},{8,9},{9,8},{10,11... | collective-permute-start | bytes 12582920 | tf_op jit(solution)/shard_map/ppermute | solution.py:20
  588.6 148.1 %reduce-scatter.10.cloned.1.call-start = ((), (), s32[]{:S(2)}) async-start(), calls=%async_computation.38 | async-start | bytes 6291456 | tf_op jit(solution)/shard_map/reduce_scatter | solution.py:160
  608.4 45.4 %collective-permute-start.66 = (bf16[2048,1024]{1,0:T(8,128)(2,1)}, bf16[2048,1024]{1,0:T(8,128)(2,1)}, u32[]{:S(2)}, u32[]{:S(2)}) collective-permute-start(bf16[2048,1024]{1,0:T(8,128)(2,1)} %convolution_convert_fusion.5), channel_id=1, source_target_pairs={{0,1},{1,0},{2,3},{3,2},{4,5},{5,4},{6,7},{7,6},{8,9},{9,8},{10,11... | collective-permute-start | bytes 12582920 | tf_op jit(solution)/shard_map/ppermute | solution.py:20
  661.7 134.1 %reduce-scatter.12.cloned.1.call-start = ((), (), s32[]{:S(2)}) async-start(), calls=%async_computation.39 | async-start | bytes 6291456 | tf_op jit(solution)/shard_map/reduce_scatter | solution.py:160
  683.6 198.4 %reduce-scatter.14.cloned.1.call-start = ((), (), s32[]{:S(2)}) async-start(), calls=%async_computation.40 | async-start | bytes 6291456 | tf_op jit(solution)/shard_map/reduce_scatter | solution.py:160
  736.8 59.0 %all-to-all-start.10 = ((bf16[8,256,512]{2,1,0:T(8,128)(2,1)}), bf16[8,256,512]{2,1,0:T(8,128)(2,1)}, u32[]{:S(2)}, u32[]{:S(2)}) async-start(bf16[8,256,512]{2,1,0:T(8,128)(2,1)} %bitcast.615), calls=%async_computation.11 | async-start | bytes 4194304 | tf_op jit(solution)/shard_map/all_to_all | solution.py:72
  795.7 61.3 %all-to-all-start.11 = ((bf16[8,256,512]{2,1,0:T(8,128)(2,1)}), bf16[8,256,512]{2,1,0:T(8,128)(2,1)}, u32[]{:S(2)}, u32[]{:S(2)}) async-start(bf16[8,256,512]{2,1,0:T(8,128)(2,1)} %bitcast.613), calls=%async_computation.13 | async-start | bytes 4194304 | tf_op jit(solution)/shard_map/all_to_all | solution.py:72
  802.1 154.5 %reduce-scatter.16.cloned.1.call-start = ((), (), s32[]{:S(2)}) async-start(), calls=%async_computation.41 | async-start | bytes 3145728 | tf_op jit(solution)/shard_map/reduce_scatter | solution.py:160
  819.4 140.9 %reduce-scatter.18.cloned.1.call-start = ((), (), s32[]{:S(2)}) async-start(), calls=%async_computation.42 | async-start | bytes 3145728 | tf_op jit(solution)/shard_map/reduce_scatter | solution.py:160
  824.4 46.2 %collective-permute-start.86 = (bf16[2048,512]{1,0:T(8,128)(2,1)}, bf16[2048,512]{1,0:T(8,128)(2,1)}, u32[]{:S(2)}, u32[]{:S(2)}) collective-permute-start(bf16[2048,512]{1,0:T(8,128)(2,1)} %convolution_convert_fusion.8), channel_id=1, source_target_pairs={{0,1},{1,0},{2,3},{3,2},{4,5},{5,4},{6,7},{7,6},{8,9},{9,8},{10,11... | collective-permute-start | bytes 6291464 | tf_op jit(solution)/shard_map/ppermute | solution.py:20
  882.0 53.7 %all-to-all-start.12 = ((bf16[8,256,512]{2,1,0:T(8,128)(2,1)}), bf16[8,256,512]{2,1,0:T(8,128)(2,1)}, u32[]{:S(2)}, u32[]{:S(2)}) async-start(bf16[8,256,512]{2,1,0:T(8,128)(2,1)} %bitcast.612), calls=%async_computation.15 | async-start | bytes 4194304 | tf_op jit(solution)/shard_map/all_to_all | solution.py:72
  886.5 129.9 %reduce-scatter.20.cloned.1.call-start = ((), (), s32[]{:S(2)}) async-start(), calls=%async_computation.43 | async-start | bytes 6291456 | tf_op jit(solution)/shard_map/reduce_scatter | solution.py:160
  896.0 179.1 %reduce-scatter.22.cloned.1.call-start = ((), (), s32[]{:S(2)}) async-start(), calls=%async_computation.44 | async-start | bytes 6291456 | tf_op jit(solution)/shard_map/reduce_scatter | solution.py:160
  990.3 189.0 %reduce-scatter.24.cloned.1.call-start = ((), (), s32[]{:S(2)}) async-start(), calls=%async_computation.45 | async-start | bytes 6291456 | tf_op jit(solution)/shard_map/reduce_scatter | solution.py:160
  1000.6 39.2 %collective-permute-start.121 = (bf16[2,2,1,2,96,256]{5,4,3,2,1,0:T(8,128)(2,1)}, bf16[2,2,1,2,96,256]{5,4,3,2,1,0:T(8,128)(2,1)}, u32[]{:S(2)}, u32[]{:S(2)}) collective-permute-start(bf16[2,2,1,2,96,256]{5,4,3,2,1,0:T(8,128)(2,1)} %get-tuple-element.169), channel_id=1, source_target_pairs={{0,8},{8,0},{1,9},{9,1},{2,10},{10,2},{3,11},{11,3},{4,12},{12,4},... | collective-permute-start | bytes 1179656 | tf_op jit(solution)/shard_map/ppermute | solution.py:20
  1017.4 57.8 %all-to-all-start.15 = ((bf16[8,256,512]{2,1,0:T(8,128)(2,1)}), bf16[8,256,512]{2,1,0:T(8,128)(2,1)}, u32[]{:S(2)}, u32[]{:S(2)}) async-start(bf16[8,256,512]{2,1,0:T(8,128)(2,1)} %bitcast.616), calls=%async_computation.21 | async-start | bytes 4194304 | tf_op jit(solution)/shard_map/all_to_all | solution.py:72
  1075.2 88.2 %all-to-all-start.16 = ((bf16[8,256,512]{2,1,0:T(8,128)(2,1)}), bf16[8,256,512]{2,1,0:T(8,128)(2,1)}, u32[]{:S(2)}, u32[]{:S(2)}) async-start(bf16[8,256,512]{2,1,0:T(8,128)(2,1)} %bitcast.611), calls=%async_computation.23 | async-start | bytes 4194304 | tf_op jit(solution)/shard_map/all_to_all | solution.py:72
  1079.7 193.6 %reduce-scatter.26.cloned.1.call-start = ((), (), s32[]{:S(2)}) async-start(), calls=%async_computation.46 | async-start | bytes 3145728 | tf_op jit(solution)/shard_map/reduce_scatter | solution.py:178
  1099.7 39.4 %collective-permute-start.93 = (bf16[2,2,1,48,2048]{4,3,2,1,0:T(8,128)(2,1)}, bf16[2,2,1,48,2048]{4,3,2,1,0:T(8,128)(2,1)}, u32[]{:S(2)}, u32[]{:S(2)}) collective-permute-start(bf16[2,2,1,48,2048]{4,3,2,1,0:T(8,128)(2,1)} %maximum_select_fusion.5), channel_id=1, source_target_pairs={{0,1},{1,0},{2,3},{3,2},{4,5},{5,4},{6,7},{7,6},{8,9},{9,8},{10,11... | collective-permute-start | bytes 2359304 | tf_op jit(solution)/shard_map/ppermute | solution.py:20
  1179.3 79.2 %all-to-all-start.17 = ((bf16[8,256,512]{2,1,0:T(8,128)(2,1)}), bf16[8,256,512]{2,1,0:T(8,128)(2,1)}, u32[]{:S(2)}, u32[]{:S(2)}) async-start(bf16[8,256,512]{2,1,0:T(8,128)(2,1)} %bitcast.610), calls=%async_computation.25 | async-start | bytes 4194304 | tf_op jit(solution)/shard_map/all_to_all | solution.py:72
  1187.7 48.4 %collective-permute-start.106 = (bf16[1,192,128]{2,1,0:T(8,128)(2,1)S(1)}, bf16[1,192,128]{2,1,0:T(8,128)(2,1)S(1)}, u32[]{:S(2)}, u32[]{:S(2)}) collective-permute-start(bf16[1,192,128]{2,1,0:T(8,128)(2,1)S(1)} %get-tuple-element.198), channel_id=1, source_target_pairs={{0,16},{4,20},{8,24},{12,28},{16,0},{20,4},{24,8},{28,12},{1,17},{... | collective-permute-start | bytes 147464 | tf_op jit(solution)/shard_map/ppermute | solution.py:290
  1190.1 47.3 %collective-permute-start.107 = (bf16[1,192,128]{2,1,0:T(8,128)(2,1)S(1)}, bf16[1,192,128]{2,1,0:T(8,128)(2,1)S(1)}, u32[]{:S(2)}, u32[]{:S(2)}) collective-permute-start(bf16[1,192,128]{2,1,0:T(8,128)(2,1)S(1)} %get-tuple-element.197), channel_id=1, source_target_pairs={{0,20},{4,16},{8,28},{12,24},{16,4},{20,0},{24,12},{28,8},{1,21},{... | collective-permute-start | bytes 147464 | tf_op jit(solution)/shard_map/ppermute | solution.py:290
  1194.4 43.0 %collective-permute-start.108 = (bf16[1,192,128]{2,1,0:T(8,128)(2,1)S(1)}, bf16[1,192,128]{2,1,0:T(8,128)(2,1)S(1)}, u32[]{:S(2)}, u32[]{:S(2)}) collective-permute-start(bf16[1,192,128]{2,1,0:T(8,128)(2,1)S(1)} %get-tuple-element.196), channel_id=1, source_target_pairs={{0,24},{4,28},{8,16},{12,20},{16,8},{20,12},{24,0},{28,4},{1,25},{... | collective-permute-start | bytes 147464 | tf_op jit(solution)/shard_map/ppermute | solution.py:290
  1196.8 40.6 %collective-permute-start.109 = (bf16[1,192,128]{2,1,0:T(8,128)(2,1)S(1)}, bf16[1,192,128]{2,1,0:T(8,128)(2,1)S(1)}, u32[]{:S(2)}, u32[]{:S(2)}) collective-permute-start(bf16[1,192,128]{2,1,0:T(8,128)(2,1)S(1)} %get-tuple-element.195), channel_id=1, source_target_pairs={{0,28},{4,24},{8,20},{12,16},{16,12},{20,8},{24,4},{28,0},{1,29},{... | collective-permute-start | bytes 147464 | tf_op jit(solution)/shard_map/ppermute | solution.py:290
  (277 other events, 4351.3 us)
Sparse Core Ops, SparseCore 0:
  49.7 45.2 all-gather.9
  101.2 58.0 all-gather.11
  200.5 55.5 all-gather.13
  264.2 57.8 all-gather.15
  342.5 34.3 all-gather.17
  378.3 33.3 all-gather.19
  413.2 56.4 all-gather.21
  471.3 56.7 all-gather.23
  588.8 57.1 all-gather.25
  661.8 54.4 reduce-scatter.9
  718.7 54.3 reduce-scatter.11
  775.1 54.2 reduce-scatter.13
  832.4 31.8 reduce-scatter.15
  882.1 30.2 reduce-scatter.17
  914.6 54.2 reduce-scatter.19
  971.0 54.3 reduce-scatter.21
  1027.6 64.3 reduce-scatter.23
  1153.0 33.1 reduce-scatter.25

commit v5 on v4

--- a/solution.py
+++ b/solution.py
@@ -369,7 +369,7 @@
     g2 = at.gather(gate_second)
 
     def ffn(x, gain, wg, wu, wd, pins):
-        n = after(at.spread(rms(x, gain).astype(BF)), pins)
+        n = held(at.spread(rms(x, gain).astype(BF)), pins)
         gate = [dot(n, w) for w in wg]
         up = [dot(n, w) for w in wu]
         hidden = [(jax.nn.silu(g) * u).astype(BF) for g, u in zip(gate, up)]
@@ -388,7 +388,7 @@
     gm = [(m.astype(F32) * jax.nn.silu(z)).astype(BF) for m, z in zip(mem, za)]
     x3 = x2 + at.collect(dot_nt(gm[0], mo[0]) + dot_nt(gm[1], mo[1]))
 
-    x4, kept2 = ffn(x3, gains[3], g2, u2, d2, ())
+    x4, kept2 = ffn(x3, gains[3], g2, u2, d2, d2[0])
     stream_out = at.spread_tp(x4.astype(BF), mb)
 
     cot = at.own_rows(cotangent)

time: 1350 us -> 1340 us (level)
  waiting for transfers between devices: 563 us -> 545 us
    all_to_all x20, waiting for transfers between devices: 143 us -> 199 us  [trade(): return lax.all_to_all(value, axes, split_axis=0, concat_axis=0, tiled=True)]
    all_gather x8, waiting for transfers between devices: 32.5 us -> 0.08 us  [gather(): own = lax.all_gather(w, 'x', axis=1, tiled=True)]
    ppermute x21, waiting for transfers between devices: 39 us -> 16.3 us  [exchange(): lax.ppermute(block, GROUP, [(i, i ^ k) for i in range(8)])]
    ppermute x89, waiting for transfers between devices: 285 us -> 269 us  [swap(): return lax.ppermute(value, axis, [(0, 1), (1, 0)])]
    unnamed x376 -> x358, local copies, waits for them, and re-layouts: 54.1 us -> 57.2 us
  transfers between devices with their start and end apart: 169 -> 169, of which waited for: 69 -> 60; matrix products, arithmetic and copies ran while one was open for 29% -> 29% of each run, Pallas kernels for 6% -> 6%
where the time goes in v5:
time: 1340 us; the launch traced here: 1330 us
  waiting for transfers between devices  545 us (41%)
  starting transfers between devices  268 us (20%)
  matrix products  236 us (18%)
  local copies, waits for them, and re-layouts  104 us (8%)
  other arithmetic  82.7 us (6%)
  Pallas kernels  73.9 us (6%)
  between operations  17.8 us (1%)
    ppermute x89, waiting for transfers between devices, swap(): return lax.ppermute(value, axis, [(0, 1), (1, 0)])  269 us
    all_to_all x20, waiting for transfers between devices, trade(): return lax.all_to_all(value, axes, split_axis=0, concat_axis=0, tiled=True)  199 us
    all_to_all x20, starting transfers between devices, trade(): return lax.all_to_all(value, axes, split_axis=0, concat_axis=0, tiled=True)  94 us
    ppermute x89, starting transfers between devices, swap(): return lax.ppermute(value, axis, [(0, 1), (1, 0)])  90.5 us
    dot_general x20, matrix products, dot_tn(): lax.dot_general(a, b, (((0,), (0,)), ((), ())), preferred_element_type=F32)  85.1 us
    dot_general x20, matrix products, dot(): return jnp.dot(a, b, preferred_element_type=F32)  83.3 us
    dot_general x20, matrix products, dot_nt(): lax.dot_general(a, b, (((1,), (1,)), ((), ())), preferred_element_type=F32)  68 us
    ppermute x21, waiting for transfers between devices, from_pairs(): got.append(lax.ppermute(v[:, k], GROUP, [(i, i ^ k) for i in range(8)]))  57.5 us
  transfers between devices with their start and end apart: 169, of which 60 were waited for; matrix products, arithmetic and copies ran while one was open for 29% of the time, Pallas kernels for 6%

profile of v5, /device:TPU:0, one launch (start us, length us, event | category | flops | bytes accessed | tf_op | source)
XLA Modules:
  0.0 1327.5 jit_solution(7125693557521966406)
XLA Ops:
  9.3 6.3 all-to-all-start
  15.6 5.6 shard_map.298
  21.3 20.1 %all-to-all-done = bf16[4,256,512]{2,1,0:T(8,128)(2,1)S(1)} async-done(((bf16[4,256,512]{2,1,0:T(8,128)(2,1)}), bf16[4,256,512]{2,1,0:T(8,128)(2,1)S(1)}, u32[]{:S(2)}, u32[]{:S(2)}) %all-to-all-start) | async-done | bytes 1048608 | tf_op jit(solution)/shard_map/all_to_all | solution.py:72
  47.4 5.7 shard_map.297
  53.1 41.4 %all-to-all-done.1 = bf16[8,256,512]{2,1,0:T(8,128)(2,1)} async-done(((bf16[8,256,512]{2,1,0:T(8,128)(2,1)}), bf16[8,256,512]{2,1,0:T(8,128)(2,1)}, u32[]{:S(2)}, u32[]{:S(2)}) %all-to-all-start.1) | async-done | bytes 2097184 | tf_op jit(solution)/shard_map/all_to_all | solution.py:72
  111.5 5.7 shard_map.299
  128.9 26.0 %all-to-all-done.2 = bf16[8,256,512]{2,1,0:T(8,128)(2,1)} async-done(((bf16[8,256,512]{2,1,0:T(8,128)(2,1)}), bf16[8,256,512]{2,1,0:T(8,128)(2,1)}, u32[]{:S(2)}, u32[]{:S(2)}) %all-to-all-start.2) | async-done | bytes 2097184 | tf_op jit(solution)/shard_map/all_to_all | solution.py:72
  171.8 10.0 collective-permute-done.13
  189.3 7.3 collective-permute-start.1
  252.1 13.0 collective-permute-done.17
  279.8 19.5 %collective-permute-done.21 = bf16[4,256,512]{2,1,0:T(8,128)(2,1)} collective-permute-done((bf16[4,256,512]{2,1,0:T(8,128)(2,1)}, bf16[4,256,512]{2,1,0:T(8,128)(2,1)}, u32[]{:S(2)}, u32[]{:S(2)}) %collective-permute-start.21) | collective-permute-done | bytes 1048608 | tf_op jit(solution)/shard_map/ppermute | solution.py:20
  320.4 5.6 shard_map.302
  335.6 6.8 all-to-all-done.6
  347.9 5.6 shard_map.301
  353.6 41.6 %all-to-all-done.7 = bf16[8,256,512]{2,1,0:T(8,128)(2,1)} async-done(((bf16[8,256,512]{2,1,0:T(8,128)(2,1)}), bf16[8,256,512]{2,1,0:T(8,128)(2,1)}, u32[]{:S(2)}, u32[]{:S(2)}) %all-to-all-start.7) | async-done | bytes 2097184 | tf_op jit(solution)/shard_map/all_to_all | solution.py:72
  406.7 21.7 %collective-permute-done.24 = bf16[96,2048]{1,0:T(8,128)(2,1)S(1)} collective-permute-done((bf16[96,2048]{1,0:T(8,128)(2,1)S(1)}, bf16[96,2048]{1,0:T(8,128)(2,1)S(1)}, u32[]{:S(2)}, u32[]{:S(2)}) %collective-permute-start.24) | collective-permute-done | bytes 393248 | tf_op jit(solution)/shard_map/ppermute | solution.py:20
  430.7 11.2 collective-permute-done.25
  448.0 5.6 shard_map.300
  469.6 9.6 all-to-all-start.9
  479.2 6.1 multiply_convert_fusion.10
  501.9 17.0 %collective-permute-done.31 = bf16[2,96,1024]{2,1,0:T(8,128)(2,1)S(1)} collective-permute-done((bf16[2,96,1024]{2,1,0:T(8,128)(2,1)S(1)}, bf16[2,96,1024]{2,1,0:T(8,128)(2,1)S(1)}, u32[]{:S(2)}, u32[]{:S(2)}) %collective-permute-start.31) | collective-permute-done | bytes 393248 | tf_op jit(solution)/shard_map/ppermute | solution.py:20
  539.4 6.4 collective-permute-done.39
  568.6 8.0 collective-permute-done.45
  587.8 8.2 collective-permute-done.49
  615.7 5.8 multiply_convert_fusion.8
  632.0 5.7 multiply_convert_fusion.5
  638.6 5.5 add_convert_fusion.5
  644.2 6.7 multiply_convert_fusion.4
  654.7 6.8 collective-permute-done.75
  734.9 17.8 %collective-permute-done.71 = bf16[96,2048]{1,0:T(8,128)(2,1)S(1)} collective-permute-done((bf16[96,2048]{1,0:T(8,128)(2,1)S(1)}, bf16[96,2048]{1,0:T(8,128)(2,1)S(1)}, u32[]{:S(2)}, u32[]{:S(2)}) %collective-permute-start.71) | collective-permute-done | bytes 393248 | tf_op jit(solution)/shard_map/ppermute | solution.py:20
  753.3 16.1 %collective-permute-done.72 = bf16[96,2048]{1,0:T(8,128)(2,1)S(1)} collective-permute-done((bf16[96,2048]{1,0:T(8,128)(2,1)S(1)}, bf16[96,2048]{1,0:T(8,128)(2,1)S(1)}, u32[]{:S(2)}, u32[]{:S(2)}) %collective-permute-start.72) | collective-permute-done | bytes 393248 | tf_op jit(solution)/shard_map/ppermute | solution.py:20
  808.5 21.4 %collective-permute-done.77 = bf16[2,96,1024]{2,1,0:T(8,128)(2,1)S(1)} collective-permute-done((bf16[2,96,1024]{2,1,0:T(8,128)(2,1)S(1)}, bf16[2,96,1024]{2,1,0:T(8,128)(2,1)S(1)}, u32[]{:S(2)}, u32[]{:S(2)}) %collective-permute-start.77) | collective-permute-done | bytes 393248 | tf_op jit(solution)/shard_map/ppermute | solution.py:20
  845.3 7.9 collective-permute-done.82
  859.9 5.5 convolution_convert_fusion.2
  872.9 6.6 add_convert_fusion.2
  880.9 6.1 multiply_convert_fusion.1
  892.4 26.7 %all-to-all-done.12.a_ref.b_ref = bf16[8,256,512]{2,1,0:T(8,128)(2,1)} async-done(((bf16[8,256,512]{2,1,0:T(8,128)(2,1)}), bf16[8,256,512]{2,1,0:T(8,128)(2,1)}, u32[]{:S(2)}, u32[]{:S(2)}) %all-to-all-start.12) | async-done | bytes 2097184 | tf_op jit(solution)/shard_map/all_to_all | solution.py:72
  923.3 7.1 collective-permute-done.94
  945.2 26.4 %all-to-all-done.13.a_ref.b_ref = bf16[8,256,256]{2,1,0:T(8,128)(2,1)S(1)} async-done(((bf16[8,256,256]{2,1,0:T(8,128)(2,1)}), bf16[8,256,256]{2,1,0:T(8,128)(2,1)S(1)}, u32[]{:S(2)}, u32[]{:S(2)}) %all-to-all-start.13) | async-done | bytes 1048608 | tf_op jit(solution)/shard_map/all_to_all | solution.py:72
  975.5 7.5 add_convert_fusion
  987.2 5.9 fusion.154
  993.1 8.2 all-to-all-done.14.a_ref.b_ref
  1026.7 22.2 %collective-permute-done.88 = bf16[2,96,1024]{2,1,0:T(8,128)(2,1)S(1)} collective-permute-done((bf16[2,96,1024]{2,1,0:T(8,128)(2,1)S(1)}, bf16[2,96,1024]{2,1,0:T(8,128)(2,1)S(1)}, u32[]{:S(2)}, u32[]{:S(2)}) %collective-permute-start.88) | collective-permute-done | bytes 393248 | tf_op jit(solution)/shard_map/ppermute | solution.py:20
  1076.1 6.6 collective-permute-done.92
  1088.6 9.8 collective-permute-done.124
  1185.4 19.0 %collective-permute-done.105 = bf16[1,192,128]{2,1,0:T(8,128)(2,1)S(1)} collective-permute-done((bf16[1,192,128]{2,1,0:T(8,128)(2,1)S(1)}, bf16[1,192,128]{2,1,0:T(8,128)(2,1)S(1)}, u32[]{:S(2)}, u32[]{:S(2)}) %collective-permute-start.105) | collective-permute-done | bytes 49184 | tf_op jit(solution)/shard_map/ppermute | solution.py:290
  1204.3 17.9 %collective-permute-done.106 = bf16[1,192,128]{2,1,0:T(8,128)(2,1)S(1)} collective-permute-done((bf16[1,192,128]{2,1,0:T(8,128)(2,1)S(1)}, bf16[1,192,128]{2,1,0:T(8,128)(2,1)S(1)}, u32[]{:S(2)}, u32[]{:S(2)}) %collective-permute-start.106) | collective-permute-done | bytes 49184 | tf_op jit(solution)/shard_map/ppermute | solution.py:290
  1273.4 8.1 collective-permute-done.112
  (947 shorter events, 718.3 us)
Async XLA Ops:
  42.3 52.2 %all-to-all-start.1 = ((bf16[8,256,512]{2,1,0:T(8,128)(2,1)}), bf16[8,256,512]{2,1,0:T(8,128)(2,1)}, u32[]{:S(2)}, u32[]{:S(2)}) async-start(bf16[8,256,512]{2,1,0:T(8,128)(2,1)} %shard_map.298), calls=%async_computation.1 | async-start | bytes 4194304 | tf_op jit(solution)/shard_map/all_to_all | solution.py:72
  46.7 135.8 %all-gather.10.cloned.1.call-start = ((), (), s32[]{:S(2)}) async-start(), calls=%async_computation.29 | async-start | bytes 3145728 | tf_op jit(solution)/shard_map/all_gather | solution.py:169
  94.5 60.4 %all-to-all-start.2 = ((bf16[8,256,512]{2,1,0:T(8,128)(2,1)}), bf16[8,256,512]{2,1,0:T(8,128)(2,1)}, u32[]{:S(2)}, u32[]{:S(2)}) async-start(bf16[8,256,512]{2,1,0:T(8,128)(2,1)} %shard_map.297), calls=%async_computation.2 | async-start | bytes 4194304 | tf_op jit(solution)/shard_map/all_to_all | solution.py:72
  98.9 248.5 %all-gather.12.cloned.1.call-start = ((), (), s32[]{:S(2)}) async-start(), calls=%async_computation.30 | async-start | bytes 6291456 | tf_op jit(solution)/shard_map/all_gather | solution.py:151
  105.7 54.6 %collective-permute-start.8 = (bf16[2,192,128]{2,1,0:T(8,128)(2,1)}, bf16[2,192,128]{2,1,0:T(8,128)(2,1)}, u32[]{:S(2)}, u32[]{:S(2)}) collective-permute-start(bf16[2,192,128]{2,1,0:T(8,128)(2,1)} %get-tuple-element.193), channel_id=1, source_target_pairs={{0,8},{4,12},{8,0},{12,4},{16,24},{20,28},{24,16},{28,20},{1,9},{5... | collective-permute-start | bytes 294920 | tf_op jit(solution)/shard_map/ppermute | solution.py:274
  107.1 58.5 %collective-permute-start.9 = (bf16[2,192,128]{2,1,0:T(8,128)(2,1)}, bf16[2,192,128]{2,1,0:T(8,128)(2,1)}, u32[]{:S(2)}, u32[]{:S(2)}) collective-permute-start(bf16[2,192,128]{2,1,0:T(8,128)(2,1)} %get-tuple-element.192), channel_id=1, source_target_pairs={{0,12},{4,8},{8,4},{12,0},{16,28},{20,24},{24,20},{28,16},{1,13},{... | collective-permute-start | bytes 294920 | tf_op jit(solution)/shard_map/ppermute | solution.py:274
  107.3 59.9 %collective-permute-start.10 = (bf16[2,192,128]{2,1,0:T(8,128)(2,1)}, bf16[2,192,128]{2,1,0:T(8,128)(2,1)}, u32[]{:S(2)}, u32[]{:S(2)}) collective-permute-start(bf16[2,192,128]{2,1,0:T(8,128)(2,1)} %get-tuple-element.191), channel_id=1, source_target_pairs={{0,16},{4,20},{8,24},{12,28},{16,0},{20,4},{24,8},{28,12},{1,17},{... | collective-permute-start | bytes 294920 | tf_op jit(solution)/shard_map/ppermute | solution.py:274
  110.1 58.6 %collective-permute-start.11 = (bf16[2,192,128]{2,1,0:T(8,128)(2,1)}, bf16[2,192,128]{2,1,0:T(8,128)(2,1)}, u32[]{:S(2)}, u32[]{:S(2)}) collective-permute-start(bf16[2,192,128]{2,1,0:T(8,128)(2,1)} %get-tuple-element.190), channel_id=1, source_target_pairs={{0,20},{4,16},{8,28},{12,24},{16,4},{20,0},{24,12},{28,8},{1,21},{... | collective-permute-start | bytes 294920 | tf_op jit(solution)/shard_map/ppermute | solution.py:274
  124.0 46.3 %collective-permute-start.12 = (bf16[2,192,128]{2,1,0:T(8,128)(2,1)}, bf16[2,192,128]{2,1,0:T(8,128)(2,1)}, u32[]{:S(2)}, u32[]{:S(2)}) collective-permute-start(bf16[2,192,128]{2,1,0:T(8,128)(2,1)} %get-tuple-element.189), channel_id=1, source_target_pairs={{0,24},{4,28},{8,16},{12,20},{16,8},{20,12},{24,0},{28,4},{1,25},{... | collective-permute-start | bytes 294920 | tf_op jit(solution)/shard_map/ppermute | solution.py:274
  155.9 52.1 %all-to-all-start.3 = ((bf16[4,256,512]{2,1,0:T(8,128)(2,1)}), bf16[4,256,512]{2,1,0:T(8,128)(2,1)}, u32[]{:S(2)}, u32[]{:S(2)}) async-start(bf16[4,256,512]{2,1,0:T(8,128)(2,1)} %broadcast_in_dim.26), calls=%async_computation.3 | async-start | bytes 2097152 | tf_op jit(solution)/shard_map/all_to_all | solution.py:72
  160.2 187.3 %all-gather.14.cloned.1.call-start = ((), (), s32[]{:S(2)}) async-start(), calls=%async_computation.31 | async-start | bytes 6291456 | tf_op jit(solution)/shard_map/all_gather | solution.py:151
  208.0 59.3 %all-to-all-start.4 = ((bf16[8,256,512]{2,1,0:T(8,128)(2,1)}), bf16[8,256,512]{2,1,0:T(8,128)(2,1)}, u32[]{:S(2)}, u32[]{:S(2)}) async-start(bf16[8,256,512]{2,1,0:T(8,128)(2,1)} %shard_map.299), calls=%async_computation.4 | async-start | bytes 4194304 | tf_op jit(solution)/shard_map/all_to_all | solution.py:72
  212.5 191.4 %all-gather.16.cloned.1.call-start = ((), (), s32[]{:S(2)}) async-start(), calls=%async_computation.32 | async-start | bytes 6291456 | tf_op jit(solution)/shard_map/all_gather | solution.py:151
  271.8 39.6 %all-to-all-start.5 = ((bf16[8,256,256]{2,1,0:T(8,128)(2,1)}), bf16[8,256,256]{2,1,0:T(8,128)(2,1)}, u32[]{:S(2)}, u32[]{:S(2)}) async-start(bf16[8,256,256]{2,1,0:T(8,128)(2,1)} %shard_map.304), calls=%async_computation.5 | async-start | bytes 2097152 | tf_op jit(solution)/shard_map/all_to_all | solution.py:72
  315.7 212.9 %all-gather.18.cloned.1.call-start = ((), (), s32[]{:S(2)}) async-start(), calls=%async_computation.33 | async-start | bytes 3145728 | tf_op jit(solution)/shard_map/all_gather | solution.py:151
  342.4 52.8 %all-to-all-start.7 = ((bf16[8,256,512]{2,1,0:T(8,128)(2,1)}), bf16[8,256,512]{2,1,0:T(8,128)(2,1)}, u32[]{:S(2)}, u32[]{:S(2)}) async-start(bf16[8,256,512]{2,1,0:T(8,128)(2,1)} %shard_map.302), calls=%async_computation.7 | async-start | bytes 4194304 | tf_op jit(solution)/shard_map/all_to_all | solution.py:72
  346.8 191.5 %all-gather.20.cloned.1.call-start = ((), (), s32[]{:S(2)}) async-start(), calls=%async_computation.34 | async-start | bytes 3145728 | tf_op jit(solution)/shard_map/all_gather | solution.py:151
  347.4 116.9 %collective-permute-start.28 = (bf16[2048,1024]{1,0:T(8,128)(2,1)}, bf16[2048,1024]{1,0:T(8,128)(2,1)}, u32[]{:S(2)}, u32[]{:S(2)}) collective-permute-start(bf16[2048,1024]{1,0:T(8,128)(2,1)} %all-gather.12.cloned.1.call-done), channel_id=1, source_target_pairs={{0,1},{1,0},{2,3},{3,2},{4,5},{5,4},{6,7},{7,6},{8,9},{9,8},{10,11... | collective-permute-start | bytes 12582920 | tf_op jit(solution)/shard_map/ppermute | solution.py:20
  347.5 131.7 %collective-permute-start.29 = (bf16[2048,1024]{1,0:T(8,128)(2,1)}, bf16[2048,1024]{1,0:T(8,128)(2,1)}, u32[]{:S(2)}, u32[]{:S(2)}) collective-permute-start(bf16[2048,1024]{1,0:T(8,128)(2,1)} %all-gather.14.cloned.1.call-done), channel_id=1, source_target_pairs={{0,1},{1,0},{2,3},{3,2},{4,5},{5,4},{6,7},{7,6},{8,9},{9,8},{10,11... | collective-permute-start | bytes 12582920 | tf_op jit(solution)/shard_map/ppermute | solution.py:20
  395.2 74.4 %all-to-all-start.8 = ((bf16[8,256,512]{2,1,0:T(8,128)(2,1)}), bf16[8,256,512]{2,1,0:T(8,128)(2,1)}, u32[]{:S(2)}, u32[]{:S(2)}) async-start(bf16[8,256,512]{2,1,0:T(8,128)(2,1)} %shard_map.301), calls=%async_computation.8 | async-start | bytes 4194304 | tf_op jit(solution)/shard_map/all_to_all | solution.py:72
  399.5 150.4 %all-gather.24.cloned.1.call-start = ((), (), s32[]{:S(2)}) async-start(), calls=%async_computation.36 | async-start | bytes 6291456 | tf_op jit(solution)/shard_map/all_gather | solution.py:151
  403.8 86.4 %collective-permute-start.30 = (bf16[2048,1024]{1,0:T(8,128)(2,1)}, bf16[2048,1024]{1,0:T(8,128)(2,1)}, u32[]{:S(2)}, u32[]{:S(2)}) collective-permute-start(bf16[2048,1024]{1,0:T(8,128)(2,1)} %all-gather.16.cloned.1.call-done), channel_id=1, source_target_pairs={{0,1},{1,0},{2,3},{3,2},{4,5},{5,4},{6,7},{7,6},{8,9},{9,8},{10,11... | collective-permute-start | bytes 12582920 | tf_op jit(solution)/shard_map/ppermute | solution.py:20
  469.6 63.2 %all-to-all-start.9 = ((bf16[8,256,512]{2,1,0:T(8,128)(2,1)}), bf16[8,256,512]{2,1,0:T(8,128)(2,1)}, u32[]{:S(2)}, u32[]{:S(2)}) async-start(bf16[8,256,512]{2,1,0:T(8,128)(2,1)} %shard_map.300), calls=%async_computation.9 | async-start | bytes 4194304 | tf_op jit(solution)/shard_map/all_to_all | solution.py:72
  479.2 71.1 %all-gather.26.cloned.1.call-start = ((), (), s32[]{:S(2)}) async-start(), calls=%async_computation.37 | async-start | bytes 6291456 | tf_op jit(solution)/shard_map/all_gather | solution.py:151
  485.4 125.6 %all-gather.22.cloned.1.call-start = ((), (), s32[]{:S(2)}) async-start(), calls=%async_computation.35 | async-start | bytes 6291456 | tf_op jit(solution)/shard_map/all_gather | solution.py:151
  549.9 61.2 %collective-permute-start.53 = (bf16[2048,1024]{1,0:T(8,128)(2,1)}, bf16[2048,1024]{1,0:T(8,128)(2,1)}, u32[]{:S(2)}, u32[]{:S(2)}) collective-permute-start(bf16[2048,1024]{1,0:T(8,128)(2,1)} %all-gather.24.cloned.1.call-done), channel_id=1, source_target_pairs={{0,1},{1,0},{2,3},{3,2},{4,5},{5,4},{6,7},{7,6},{8,9},{9,8},{10,11... | collective-permute-start | bytes 12582920 | tf_op jit(solution)/shard_map/ppermute | solution.py:20
  550.0 171.7 %reduce-scatter.10.cloned.1.call-start = ((), (), s32[]{:S(2)}) async-start(), calls=%async_computation.38 | async-start | bytes 6291456 | tf_op jit(solution)/shard_map/reduce_scatter | solution.py:160
  552.5 63.2 %collective-permute-start.54 = (bf16[2048,1024]{1,0:T(8,128)(2,1)}, bf16[2048,1024]{1,0:T(8,128)(2,1)}, u32[]{:S(2)}, u32[]{:S(2)}) collective-permute-start(bf16[2048,1024]{1,0:T(8,128)(2,1)} %all-gather.26.cloned.1.call-done), channel_id=1, source_target_pairs={{0,1},{1,0},{2,3},{3,2},{4,5},{5,4},{6,7},{7,6},{8,9},{9,8},{10,11... | collective-permute-start | bytes 12582920 | tf_op jit(solution)/shard_map/ppermute | solution.py:20
  644.1 136.6 %reduce-scatter.12.cloned.1.call-start = ((), (), s32[]{:S(2)}) async-start(), calls=%async_computation.39 | async-start | bytes 6291456 | tf_op jit(solution)/shard_map/reduce_scatter | solution.py:160
  666.0 199.4 %reduce-scatter.14.cloned.1.call-start = ((), (), s32[]{:S(2)}) async-start(), calls=%async_computation.40 | async-start | bytes 6291456 | tf_op jit(solution)/shard_map/reduce_scatter | solution.py:160
  721.7 59.1 %all-to-all-start.10 = ((bf16[8,256,512]{2,1,0:T(8,128)(2,1)}), bf16[8,256,512]{2,1,0:T(8,128)(2,1)}, u32[]{:S(2)}, u32[]{:S(2)}) async-start(bf16[8,256,512]{2,1,0:T(8,128)(2,1)} %bitcast.607), calls=%async_computation.11 | async-start | bytes 4194304 | tf_op jit(solution)/shard_map/all_to_all | solution.py:72
  780.8 61.0 %all-to-all-start.11 = ((bf16[8,256,512]{2,1,0:T(8,128)(2,1)}), bf16[8,256,512]{2,1,0:T(8,128)(2,1)}, u32[]{:S(2)}, u32[]{:S(2)}) async-start(bf16[8,256,512]{2,1,0:T(8,128)(2,1)} %bitcast.605), calls=%async_computation.13 | async-start | bytes 4194304 | tf_op jit(solution)/shard_map/all_to_all | solution.py:72
  786.2 155.3 %reduce-scatter.16.cloned.1.call-start = ((), (), s32[]{:S(2)}) async-start(), calls=%async_computation.41 | async-start | bytes 3145728 | tf_op jit(solution)/shard_map/reduce_scatter | solution.py:160
  803.5 141.8 %reduce-scatter.18.cloned.1.call-start = ((), (), s32[]{:S(2)}) async-start(), calls=%async_computation.42 | async-start | bytes 3145728 | tf_op jit(solution)/shard_map/reduce_scatter | solution.py:160
  808.5 46.9 %collective-permute-start.86 = (bf16[2048,512]{1,0:T(8,128)(2,1)}, bf16[2048,512]{1,0:T(8,128)(2,1)}, u32[]{:S(2)}, u32[]{:S(2)}) collective-permute-start(bf16[2048,512]{1,0:T(8,128)(2,1)} %convolution_convert_fusion.8), channel_id=1, source_target_pairs={{0,1},{1,0},{2,3},{3,2},{4,5},{5,4},{6,7},{7,6},{8,9},{9,8},{10,11... | collective-permute-start | bytes 6291464 | tf_op jit(solution)/shard_map/ppermute | solution.py:20
  865.5 53.7 %all-to-all-start.12 = ((bf16[8,256,512]{2,1,0:T(8,128)(2,1)}), bf16[8,256,512]{2,1,0:T(8,128)(2,1)}, u32[]{:S(2)}, u32[]{:S(2)}) async-start(bf16[8,256,512]{2,1,0:T(8,128)(2,1)} %bitcast.604), calls=%async_computation.15 | async-start | bytes 4194304 | tf_op jit(solution)/shard_map/all_to_all | solution.py:72
  870.0 131.3 %reduce-scatter.20.cloned.1.call-start = ((), (), s32[]{:S(2)}) async-start(), calls=%async_computation.43 | async-start | bytes 6291456 | tf_op jit(solution)/shard_map/reduce_scatter | solution.py:160
  879.5 180.6 %reduce-scatter.22.cloned.1.call-start = ((), (), s32[]{:S(2)}) async-start(), calls=%async_computation.44 | async-start | bytes 6291456 | tf_op jit(solution)/shard_map/reduce_scatter | solution.py:160
  975.3 190.1 %reduce-scatter.24.cloned.1.call-start = ((), (), s32[]{:S(2)}) async-start(), calls=%async_computation.45 | async-start | bytes 6291456 | tf_op jit(solution)/shard_map/reduce_scatter | solution.py:160
  985.2 39.5 %collective-permute-start.121 = (bf16[2,2,1,2,96,256]{5,4,3,2,1,0:T(8,128)(2,1)}, bf16[2,2,1,2,96,256]{5,4,3,2,1,0:T(8,128)(2,1)}, u32[]{:S(2)}, u32[]{:S(2)}) collective-permute-start(bf16[2,2,1,2,96,256]{5,4,3,2,1,0:T(8,128)(2,1)} %get-tuple-element.169), channel_id=1, source_target_pairs={{0,8},{8,0},{1,9},{9,1},{2,10},{10,2},{3,11},{11,3},{4,12},{12,4},... | collective-permute-start | bytes 1179656 | tf_op jit(solution)/shard_map/ppermute | solution.py:20
  1002.3 57.8 %all-to-all-start.15 = ((bf16[8,256,512]{2,1,0:T(8,128)(2,1)}), bf16[8,256,512]{2,1,0:T(8,128)(2,1)}, u32[]{:S(2)}, u32[]{:S(2)}) async-start(bf16[8,256,512]{2,1,0:T(8,128)(2,1)} %bitcast.608), calls=%async_computation.21 | async-start | bytes 4194304 | tf_op jit(solution)/shard_map/all_to_all | solution.py:72
  1060.1 88.3 %all-to-all-start.16 = ((bf16[8,256,512]{2,1,0:T(8,128)(2,1)}), bf16[8,256,512]{2,1,0:T(8,128)(2,1)}, u32[]{:S(2)}, u32[]{:S(2)}) async-start(bf16[8,256,512]{2,1,0:T(8,128)(2,1)} %bitcast.603), calls=%async_computation.23 | async-start | bytes 4194304 | tf_op jit(solution)/shard_map/all_to_all | solution.py:72
  1064.6 194.8 %reduce-scatter.26.cloned.1.call-start = ((), (), s32[]{:S(2)}) async-start(), calls=%async_computation.46 | async-start | bytes 3145728 | tf_op jit(solution)/shard_map/reduce_scatter | solution.py:178
  1165.4 79.3 %all-to-all-start.17 = ((bf16[8,256,512]{2,1,0:T(8,128)(2,1)}), bf16[8,256,512]{2,1,0:T(8,128)(2,1)}, u32[]{:S(2)}, u32[]{:S(2)}) async-start(bf16[8,256,512]{2,1,0:T(8,128)(2,1)} %bitcast.602), calls=%async_computation.25 | async-start | bytes 4194304 | tf_op jit(solution)/shard_map/all_to_all | solution.py:72
  1173.8 48.4 %collective-permute-start.106 = (bf16[1,192,128]{2,1,0:T(8,128)(2,1)S(1)}, bf16[1,192,128]{2,1,0:T(8,128)(2,1)S(1)}, u32[]{:S(2)}, u32[]{:S(2)}) collective-permute-start(bf16[1,192,128]{2,1,0:T(8,128)(2,1)S(1)} %get-tuple-element.198), channel_id=1, source_target_pairs={{0,16},{4,20},{8,24},{12,28},{16,0},{20,4},{24,8},{28,12},{1,17},{... | collective-permute-start | bytes 147464 | tf_op jit(solution)/shard_map/ppermute | solution.py:290
  1176.2 47.3 %collective-permute-start.107 = (bf16[1,192,128]{2,1,0:T(8,128)(2,1)S(1)}, bf16[1,192,128]{2,1,0:T(8,128)(2,1)S(1)}, u32[]{:S(2)}, u32[]{:S(2)}) collective-permute-start(bf16[1,192,128]{2,1,0:T(8,128)(2,1)S(1)} %get-tuple-element.197), channel_id=1, source_target_pairs={{0,20},{4,16},{8,28},{12,24},{16,4},{20,0},{24,12},{28,8},{1,21},{... | collective-permute-start | bytes 147464 | tf_op jit(solution)/shard_map/ppermute | solution.py:290
  1180.5 43.0 %collective-permute-start.108 = (bf16[1,192,128]{2,1,0:T(8,128)(2,1)S(1)}, bf16[1,192,128]{2,1,0:T(8,128)(2,1)S(1)}, u32[]{:S(2)}, u32[]{:S(2)}) collective-permute-start(bf16[1,192,128]{2,1,0:T(8,128)(2,1)S(1)} %get-tuple-element.196), channel_id=1, source_target_pairs={{0,24},{4,28},{8,16},{12,20},{16,8},{20,12},{24,0},{28,4},{1,25},{... | collective-permute-start | bytes 147464 | tf_op jit(solution)/shard_map/ppermute | solution.py:290
  1182.9 40.6 %collective-permute-start.109 = (bf16[1,192,128]{2,1,0:T(8,128)(2,1)S(1)}, bf16[1,192,128]{2,1,0:T(8,128)(2,1)S(1)}, u32[]{:S(2)}, u32[]{:S(2)}) collective-permute-start(bf16[1,192,128]{2,1,0:T(8,128)(2,1)S(1)} %get-tuple-element.195), channel_id=1, source_target_pairs={{0,28},{4,24},{8,20},{12,16},{16,12},{20,8},{24,4},{28,0},{1,29},{... | collective-permute-start | bytes 147464 | tf_op jit(solution)/shard_map/ppermute | solution.py:290
  (268 other events, 4322.3 us)
Sparse Core Ops, SparseCore 0:
  49.7 45.2 all-gather.9
  101.3 58.0 all-gather.11
  188.8 61.7 all-gather.13
  267.4 54.7 all-gather.15
  333.5 34.0 all-gather.17
  369.0 33.0 all-gather.19
  403.7 65.1 all-gather.23
  485.5 58.1 all-gather.25
  550.1 57.6 all-gather.21
  644.3 54.5 reduce-scatter.9
  701.3 54.3 reduce-scatter.11
  757.8 54.2 reduce-scatter.13
  815.0 31.8 reduce-scatter.15
  865.6 31.8 reduce-scatter.17
  899.7 54.3 reduce-scatter.19
  956.2 54.2 reduce-scatter.21
  1012.8 64.5 reduce-scatter.23
  1138.1 32.4 reduce-scatter.25
